TPU v7x, 512 devices: a whole 4x8x8 slice. The times are simulated.
512 devices in a mesh: row: 16 (over y, core), col: 32 (over z, x).
Axes of the slice: x: 4, y: 8, z: 8, core: 2. Of those that a mesh axis runs over, the one named last changes fastest.
Arguments:
- covariance: float32 [2, 8192, 1, 16384], P(None, 'row', None, 'col'), may hold values from 0 to 11, as said below
Outputs:
- factored: float32 [2, 8192, 1, 16384], P(None, 'row', None, 'col')
Inputs may be any that keep to these rules, and one draw needn't show every extreme that they name: covariance read as a matrix of order 16384 is exactly symmetric and positive definite, with positive entries.
All inputs are finite; a program needn't handle non-finite values.
Results may differ from a plain program's by a relative error of at most 0.000065.
Values sent between devices are 32-bit elements; how exact they have to be, the bound alone decides.
No kernel may reach another device: no remote copies, remote signals or barrier semaphores. Data moves between devices by JAX's collectives and lax.ppermute only.
A program may use at most 64 MiB of HBM per device.

v0:
```python
import jax
import jax.numpy as jnp
from jax import lax
from jax.sharding import PartitionSpec as P


def spread(value, axis, source):
    kept = jnp.where(lax.axis_index(axis) == source, value, 0).astype(value.dtype)
    return lax.psum(kept, axis)


def solve_panel(factor, raw_tiles):
    tile_count = raw_tiles.shape[0]
    width = raw_tiles.shape[1]
    right_side = jnp.transpose(raw_tiles, (2, 0, 1)).reshape(width, tile_count * width)
    solved = jax.scipy.linalg.solve_triangular(factor, right_side, lower=True)
    return jnp.transpose(solved.reshape(width, tile_count, width), (1, 2, 0))


def owner_columns(panel_rows, row_count, col_pos):
    target = 0 + col_pos
    picked = lax.dynamic_index_in_dim(panel_rows, target // row_count, 0, keepdims=False)
    received = [spread(picked, "row", target % row_count)]
    return jnp.stack(received)


def on_device(covariance):
    row_pos = lax.axis_index("row")
    col_pos = lax.axis_index("col")
    row_count = lax.axis_size("row")
    col_count = lax.axis_size("col")
    tile_rows = covariance.shape[0]
    width = covariance.shape[1]
    tile_cols = covariance.shape[2]
    global_rows = jnp.arange(tile_rows, dtype=jnp.int32) * row_count + row_pos
    global_cols = jnp.arange(tile_cols, dtype=jnp.int32) * col_count + col_pos
    is_root = jnp.logical_and(row_pos == 0, col_pos == 0)
    identity = jnp.eye(width, dtype=jnp.float32)
    raw_tiles = covariance[:, :, 0, :]
    first_row = (global_rows == 0)[:, None, None]
    factor = jnp.linalg.cholesky(jnp.where(is_root, covariance[0, :, 0, :], identity))
    factor = spread(factor, "row", 0)
    panel_rows = jnp.where(first_row, factor[None], solve_panel(factor, raw_tiles))
    panel_rows = spread(panel_rows, "col", 0)
    panel_cols = owner_columns(panel_rows, row_count, col_pos)
    product = jnp.einsum(
        "arx,csx->arcs",
        panel_rows,
        panel_cols,
        precision=lax.Precision.HIGHEST,
        preferred_element_type=jnp.float32,
    )
    updated = covariance - product
    lower = global_rows[:, None, None, None] >= global_cols[None, None, :, None]
    first_col = (global_cols == 0)[None, None, :, None]
    inner = jnp.where(lower, updated, covariance)
    return jnp.where(first_col, panel_rows[:, :, None, :], inner)


def solution(mesh):
    return jax.shard_map(
        on_device,
        mesh=mesh,
        in_specs=(P(None, "row", None, "col"),),
        out_specs=P(None, "row", None, "col"),
        check_vma=False,
    )
```

profile of v0, /device:TPU:1, one launch (start us, length us, event | category | flops | bytes accessed | tf_op | source)
XLA Modules:
  0.0 587.4 jit_solution(8940039226502144366)
XLA Ops:
  6.5 1.2 slice-done
  7.8 1.3 copy.10
  9.1 0.1 bitcast_select_fusion
  9.2 0.3 copy.3
  9.6 0.2 fusion.14
  9.8 0.0 copy-start.2
  9.8 11.7 %cholesky.105 = f32[128,128]{1,0:T(8,128)S(1)} custom-call(f32[128,128]{1,0:T(8,128)S(1)} %cholesky.269), custom_call_target="Cholesky" | custom-call | tf_op jit(solution)/shard_map/jit(cholesky)/cholesky | solution.py:41
  21.6 0.1 cholesky.226
  21.7 9.8 %custom-call.31 = f32[1,128,128]{1,2,0:T(8,128)S(1)} custom-call(f32[1,128,128]{2,1,0:T(8,128)S(1)} %get-tuple-element.36), custom_call_target="InvertDiagBlocksLowerTriangular" | custom-call | tf_op jit(solution)/shard_map/jit(cholesky)/cholesky | solution.py:41
  31.5 0.3 constant_dynamic-update-slice_fusion.3
  31.8 0.3 convolution_subtract_fusion.2
  32.2 11.7 %cholesky.219 = f32[128,128]{1,0:T(8,128)S(1)} custom-call(f32[128,128]{1,0:T(8,128)S(1)} %cholesky.273), custom_call_target="Cholesky" | custom-call | tf_op jit(solution)/shard_map/jit(cholesky)/cholesky | solution.py:41
  43.9 10.0 %custom-call.32 = f32[1,128,128]{1,2,0:T(8,128)S(1)} custom-call(f32[1,128,128]{2,1,0:T(8,128)S(1)} %get-tuple-element.33), custom_call_target="InvertDiagBlocksLowerTriangular" | custom-call | tf_op jit(solution)/shard_map/jit(cholesky)/cholesky | solution.py:41
  53.9 0.3 convolution_dynamic-update-slice_fusion
  54.2 0.4 convolution_subtract_fusion.3
  54.6 0.0 copy-start
  54.6 11.7 %cholesky.240 = f32[128,128]{1,0:T(8,128)S(1)} custom-call(f32[128,128]{1,0:T(8,128)S(1)} %cholesky.278), custom_call_target="Cholesky" | custom-call | tf_op jit(solution)/shard_map/jit(cholesky)/cholesky | solution.py:41
  66.3 9.8 %custom-call.33 = f32[1,128,128]{1,2,0:T(8,128)S(1)} custom-call(f32[1,128,128]{2,1,0:T(8,128)S(1)} %get-tuple-element.30), custom_call_target="InvertDiagBlocksLowerTriangular" | custom-call | tf_op jit(solution)/shard_map/jit(cholesky)/cholesky | solution.py:41
  76.2 0.2 convolution_dynamic-update-slice_fusion.1
  76.4 1.2 convolution_subtract_fusion.4
  77.6 11.7 %cholesky.257 = f32[128,128]{1,0:T(8,128)S(1)} custom-call(f32[128,128]{1,0:T(8,128)S(1)} %convolution_subtract_fusion.4), custom_call_target="Cholesky" | custom-call | tf_op jit(solution)/shard_map/jit(cholesky)/cholesky | solution.py:41
  89.3 0.7 compare_reduce_fusion.1
  90.1 0.6 compare_reduce_fusion
  90.7 0.7 compare_reduce_fusion.2
  94.1 1.1 select_select_fusion.1
  95.2 0.0 all-reduce.5.cloned.1.call-update
  95.2 0.0 all-reduce.7.cloned.1.call-start
  95.3 1.5 copy.13
  96.8 2.9 fusion.39
  99.7 117.8 %all-reduce.5.cloned.1.call-done = f32[512,512]{1,0:T(8,128)} async-done(((f32[512,512]{1,0:T(8,128)}), f32[512,512]{1,0:T(8,128)}) %all-reduce.5.cloned.1.call-update) | async-done | bytes 1048592 | tf_op jit(solution)/shard_map/psum | solution.py:9
  217.5 1.3 fusion.15
  218.8 10.9 %while.1 = (s32[]{:T(128)}, f32[512,512]{1,0:T(8,128)S(1)}, s32[4,2]{0,1:T(2,128)S(1)}, f32[4,128,128]{2,1,0:T(8,128)}, s32[]{:T(128)}) while((s32[]{:T(128)}, f32[512,512]{1,0:T(8,128)S(1)}, s32[4,2]{0,1:T(2,128)S(1)}, f32[4,128,128]{2,1,0:T(8,128)}, s32[]{:T(128)}) %tuple.30), condition=%wide.while_cond, body=%wide.while_body.sunk | while | flops 2 | bytes 132205 | solution.py:16
  218.8 0.1 constant_dynamic-slice_fusion.2
  218.9 0.6 fusion.48
  219.5 2.1 bitcast_dynamic-update-slice_fusion.2
  221.6 0.1 constant_dynamic-slice_fusion.2
  221.6 0.6 fusion.48
  222.2 2.0 bitcast_dynamic-update-slice_fusion.2
  224.3 0.1 constant_dynamic-slice_fusion.2
  224.4 0.6 fusion.48
  224.9 2.0 bitcast_dynamic-update-slice_fusion.2
  227.0 0.1 constant_dynamic-slice_fusion.2
  227.1 0.6 fusion.48
  227.7 2.0 bitcast_dynamic-update-slice_fusion.2
  229.7 40.1 %custom-call.34 = f32[4,128,128]{1,2,0:T(8,128)S(1)} custom-call(f32[4,128,128]{2,1,0:T(8,128)} %get-tuple-element.12), custom_call_target="InvertDiagBlocksLowerTriangular" | custom-call | tf_op jit(solution)/shard_map/jit(_solve_triangular)/triangular_solve | solution.py:16
  269.9 1.7 fusion.28
  271.6 2.0 convolution_subtract_fusion.1
  273.7 0.6 fusion.27
  274.3 0.0 copy-done.3
  274.3 1.8 convolution_subtract_fusion
  276.2 0.6 fusion.25
  276.8 2.8 fusion.7
  279.6 0.6 fusion.24
  280.2 1.6 pad_maximum_fusion
  281.8 3.0 copy.8
  284.9 3.3 select_select_fusion
  288.2 0.0 all-reduce.7.cloned.1.call-update
  288.2 0.3 all-reduce.9.cloned.1.call-start
  288.6 162.3 %all-reduce.7.cloned.1.call-done = f32[2,512,512]{2,1,0:T(8,128)} async-done(((f32[2,512,512]{2,1,0:T(8,128)}), f32[2,512,512]{2,1,0:T(8,128)}) %all-reduce.7.cloned.1.call-update) | async-done | bytes 2097168 | tf_op jit(solution)/shard_map/psum | solution.py:9
  450.8 2.3 select_bitcast_fusion
  453.1 0.0 all-reduce.9.cloned.1.call-update
  453.2 117.6 %all-reduce.9.cloned.1.call-done = f32[512,512]{1,0:T(8,128)} async-done(((f32[512,512]{1,0:T(8,128)}), f32[512,512]{1,0:T(8,128)}) %all-reduce.9.cloned.1.call-update) | async-done | bytes 1048592 | tf_op jit(solution)/shard_map/psum | solution.py:9
  570.8 6.1 %fusion = f32[2,512,1,512]{3,1,0,2:T(8,128)S(1)} fusion(f32[2,512,512]{2,1,0:T(8,128)} %all-reduce.7.cloned.1.call-done, f32[2,512,1,512]{3,2,1,0:T(1,128)S(1)} %copy-done, f32[512,512]{1,0:T(8,128)} %all-reduce.9.cloned.1.call-done, pred[2]{0:T(512)(128)(4,1)S(1)} %fusion.34, pred[]{:T(512)S(6)} %eq.25), kind=kOutput, calls=%fused_computation.3 | convolution fusion | flops 3222798336 | bytes 7340035 | tf_op jit(solution)/shard_map/arx,csx->arcs/dot_general | solution.py:46
  576.9 3.5 copy.7
  (21 shorter events, 0.2 us)
Async XLA Ops:
  6.5 1.2 slice-start
  6.5 210.9 %all-reduce.5.cloned.1.call-start = ((), (), s32[]{:S(2)}) async-start(), calls=%async_computation | async-start | bytes 2097152 | tf_op jit(solution)/shard_map/psum | solution.py:9
  9.8 44.4 %copy-start.2 = (f32[512,512]{1,0:T(8,128)}, f32[512,512]{1,0:T(8,128)S(1)}, u32[]{:S(2)}) copy-start(f32[512,512]{1,0:T(8,128)S(1)} %fusion.14) | copy-start | bytes 3145732
  54.6 40.7 %copy-start = (f32[2,512,1,512]{3,2,1,0:T(1,128)S(1)}, f32[2,512,1,512]{3,2,1,0:T(1,128)}, u32[]{:S(2)}) copy-start(f32[2,512,1,512]{3,2,1,0:T(1,128)} %param.1) | copy-start | bytes 6291460
  95.2 355.6 %all-reduce.7.cloned.1.call-start = ((), (), s32[]{:S(2)}) async-start(), calls=%async_computation.1 | async-start | bytes 4194304 | tf_op jit(solution)/shard_map/psum | solution.py:9
  269.8 4.5 copy-start.3
  273.6 3.2 copy-start.4
  281.8 3.0 copy-start.1
  288.2 282.6 %all-reduce.9.cloned.1.call-start = ((), (), s32[]{:S(2)}) async-start(), calls=%async_computation.2 | async-start | bytes 2097152 | tf_op jit(solution)/shard_map/psum | solution.py:9
Sparse Core Ops, SparseCore 0:
  95.3 122.0 all-reduce.4
  288.3 162.4 all-reduce.6
  453.3 117.4 all-reduce.8
where the time goes:
time: 597 us; the launch traced here: 587 us
  waiting for transfers between devices  398 us (67%)
  other arithmetic  129 us (22%)
  local copies, waits for them, and re-layouts  24.8 us (4%)
  matrix products  19.1 us (3%)
  between operations  16.6 us (3%)
    psum x3, waiting for transfers between devices, spread(): return lax.psum(kept, axis)  398 us
    another operation x14, other arithmetic, on_device(): jnp.linalg.cholesky(jnp.where(is_root, covariance[0, :, 0, :], identity))  78.6 us
    another operation x4, other arithmetic, solve_panel(): solved = jax.scipy.linalg.solve_triangular(factor, right_side, lower=True)  43 us
  transfers between devices with their start and end apart: 3, of which 3 were waited for; matrix products, arithmetic and copies ran while one was open for 1% of the time, Pallas kernels for 0%

commit v1 on v0

v1 whole, which is shorter than its diff:
```python
import functools

import jax
import jax.numpy as jnp
from jax import lax
from jax.experimental import pallas as pl
from jax.experimental.pallas import tpu as pltpu
from jax.sharding import PartitionSpec as P

AXES = ("row", "col")
ROWS, COLS = 16, 32
NY, NZ, NX = 8, 8, 4
TB = 512
SB = 128
HB = 256
SLOTS = 12
HIGHEST = lax.Precision.HIGHEST
M0, M1, X10, L20, L21, L30, L31, M2, M3, X32 = range(10)


def nn(a, b):
    return lax.dot_general(a, b, (((1,), (0,)), ((), ())), precision=HIGHEST, preferred_element_type=jnp.float32)


def nt(a, b):
    return lax.dot_general(a, b, (((1,), (1,)), ((), ())), precision=HIGHEST, preferred_element_type=jnp.float32)


def factor_block(block):
    tiles = SB // 8
    lane = lax.broadcasted_iota(jnp.int32, (8, SB), 1)
    sub = lax.broadcasted_iota(jnp.int32, (8, SB), 0)
    s = [block[8 * t : 8 * t + 8, :] for t in range(tiles)]
    e = [jnp.where(lane == sub + 8 * t, 1.0, 0.0).astype(jnp.float32) for t in range(tiles)]
    upper, inverse = [], []
    for b in range(tiles):
        cols = [
            [jnp.broadcast_to(s[t][:, 8 * b + m : 8 * b + m + 1], (8, SB)) for t in range(b, tiles)]
            for m in range(8)
        ]
        top, top_e = s[b], e[b]
        out_u, out_e = jnp.zeros_like(top), jnp.zeros_like(top)
        done = []
        for m in range(8):
            d = jnp.broadcast_to(cols[m][0][m : m + 1, :], (8, SB))
            r = lax.rsqrt(d)
            r = r * (1.5 - (0.5 * d) * (r * r))
            lc = [c * r for c in cols[m]]
            ur = jnp.broadcast_to(top[m : m + 1, :], (8, SB)) * r
            er = jnp.broadcast_to(top_e[m : m + 1, :], (8, SB)) * r
            out_u = jnp.where(sub == m, ur, out_u)
            out_e = jnp.where(sub == m, er, out_e)
            for k in range(m + 1, 8):
                f = jnp.broadcast_to(lc[0][k : k + 1, :], (8, SB))
                cols[k] = [c - l * f for c, l in zip(cols[k], lc)]
            below = jnp.where(sub > m, lc[0], 0.0)
            top = top - below * ur
            top_e = top_e - below * er
            done.append((lc, ur, er))
        for t in range(b + 1, tiles):
            for lc, ur, er in done:
                s[t] = s[t] - lc[t - b] * ur
                e[t] = e[t] - lc[t - b] * er
        upper.append(jnp.where(lane >= sub + 8 * b, out_u, 0.0))
        inverse.append(out_e)
    return jnp.concatenate(upper, axis=0), jnp.concatenate(inverse, axis=0)


def factor_kernel(k, flag_ref, w_in, f_in, w_ref, f_ref):
    @pl.when(flag_ref[0] == 1)
    def _():
        lo, hi = k * SB, (k + 1) * SB
        w_ref[...] = w_in[...]
        f_ref[...] = f_in[...]

        def slot(i):
            return pl.ds(i * SB, SB)

        u, inv = factor_block(w_in[lo:hi, lo:hi])
        f_ref[slot((M0, M1, M2, M3)[k]), :] = inv
        w_ref[lo:hi, lo:hi] = u.T
        if k % 2 == 1:
            prev = f_in[slot((M0, M2)[k // 2]), :]
            f_ref[slot((X10, X32)[k // 2]), :] = -nn(inv, nn(w_in[lo:hi, lo - SB : lo], prev))
        if hi < TB:
            below = nt(w_in[hi:, lo:hi], inv)
            w_ref[hi:, lo:hi] = below
            w_ref[lo:hi, hi:] = jnp.zeros((SB, TB - hi), jnp.float32)
            w_ref[hi:, hi:] = w_in[hi:, hi:] - nt(below, below)
            if k < 2:
                f_ref[slot((L20, L21)[k]), :] = below[2 * SB - hi : 3 * SB - hi]
                f_ref[slot((L30, L31)[k]), :] = below[3 * SB - hi : 4 * SB - hi]


def factor_step(k, flag, w, f):
    vmem = pl.BlockSpec(memory_space=pltpu.VMEM)
    return pl.pallas_call(
        functools.partial(factor_kernel, k),
        out_shape=(
            jax.ShapeDtypeStruct((TB, TB), jnp.float32),
            jax.ShapeDtypeStruct((SLOTS * SB, SB), jnp.float32),
        ),
        in_specs=[pl.BlockSpec(memory_space=pltpu.SMEM), vmem, vmem],
        out_specs=(vmem, vmem),
        cost_estimate=pl.CostEstimate(flops=8_000_000_000, bytes_accessed=3_000_000, transcendentals=0),
        compiler_params=pltpu.CompilerParams(vmem_limit_bytes=24 * 1024 * 1024),
        name=f"factor_{k}",
    )(flag, w, f)


def update_kernel(pos_ref, own_ref, left_ref, right_ref, opp_a_ref, opp_b_ref, b_ref, f_ref, w_ref, cov_ref, out_ref, y_ref):
    row, col, x = pos_ref[0], pos_ref[1], pos_ref[2]

    def block(i):
        place = lax.rem(i // 3 - x + 4, 4)
        return f_ref[pl.ds(pl.multiple_of(place * (3 * SB) + (i % 3) * SB, SB), SB), :]

    zero = jnp.zeros((SB, SB), jnp.float32)

    def square(a, b, c, d):
        return jnp.concatenate(
            [jnp.concatenate([a, b], axis=1), jnp.concatenate([c, d], axis=1)], axis=0
        )

    d0 = square(block(M0), zero, block(X10), block(M1))
    d1 = square(block(M2), zero, block(X32), block(M3))
    g = square(block(L20), block(L21), block(L30), block(L31))
    y0 = nn(d0, b_ref[0:HB, :])
    y_ref[0:HB, :] = y0
    y_ref[HB:TB, :] = nn(d1, b_ref[HB:TB, :] - nn(g, y0))

    opp = jnp.concatenate([opp_a_ref[...], opp_b_ref[...]], axis=0)
    pieces = ((0, own_ref[...]), (3, left_ref[...]), (1, right_ref[...]), (2, opp))
    for shift, raw in pieces:
        q = lax.rem(x + shift, 4)
        rows = pl.ds(pl.multiple_of(q * HB, HB), HB)
        x0 = nt(raw[:, 0:HB], d0)
        x1 = nt(raw[:, HB:TB] - nt(x0, g), d1)
        cov = cov_ref[rows, :]
        new = cov - (nn(x0, y_ref[0:HB, :]) + nn(x1, y_ref[HB:TB, :]))
        tile_row = row + ROWS * (q // 2)
        out = jnp.where(tile_row >= col, new, cov)
        out = jnp.where(col == 0, jnp.concatenate([x0, x1], axis=1), out)
        half = pl.ds(pl.multiple_of(lax.rem(q, 2) * HB, HB), HB)
        out_ref[rows, :] = jnp.where(jnp.logical_and(col == 0, tile_row == 0), w_ref[half, :], out)


def update(pos, own, left, right, opp_a, opp_b, b, f, w, cov):
    vmem = pl.BlockSpec(memory_space=pltpu.VMEM)
    return pl.pallas_call(
        update_kernel,
        out_shape=jax.ShapeDtypeStruct((2 * TB, TB), jnp.float32),
        in_specs=[pl.BlockSpec(memory_space=pltpu.SMEM)] + [vmem] * 9,
        out_specs=vmem,
        scratch_shapes=[pltpu.VMEM((TB, TB), jnp.float32)],
        cost_estimate=pl.CostEstimate(flops=8_000_000_000, bytes_accessed=9_000_000, transcendentals=0),
        compiler_params=pltpu.CompilerParams(vmem_limit_bytes=40 * 1024 * 1024),
        name="update",
    )(pos, own, left, right, opp_a, opp_b, b, f, w, cov)


def device(y, core, z, x):
    return (y * 2 + core) * COLS + z * NX + x


def send(value, pairs):
    return lax.ppermute(value, AXES, pairs)


def one_of(pos, places):
    found = pos == places[0]
    for place in places[1:]:
        found = jnp.logical_or(found, pos == place)
    return found


ROUNDS = (
    (((0, 3),), ((0, 5),)),
    (((0, 1), (3, 4), (5, 6)), ((0, 7), (3, 2))),
)


def ring_sends(value, moves, lift):
    return [send(value, [p for a, b in pairs for p in lift(a, b)]) for pairs in moves]


def ring_pick(value, moves, pos, got):
    for pairs, received in zip(moves, got):
        value = jnp.where(one_of(pos, [b for _, b in pairs]), received, value)
    return value


def ring_round(value, moves, pos, lift):
    return ring_pick(value, moves, pos, ring_sends(value, moves, lift))


def on_device(covariance):
    row = lax.axis_index("row")
    col = lax.axis_index("col")
    y, core = row // 2, row % 2
    z, x = col // NX, col % NX
    cov = lax.optimization_barrier(covariance.reshape(2 * TB, TB))
    is_root = jnp.logical_and(row == 0, col == 0)
    flag = is_root.astype(jnp.int32).reshape(1)
    everywhere = [(a, c) for a in range(NY) for c in range(2)]

    quarter = [cov[HB * q : HB * (q + 1)] for q in range(4)]
    got = [
        send(quarter[q], [(device(a, c, 0, 0), device(a, c, 0, q)) for a, c in everywhere])
        for q in (1, 3, 2)
    ]

    def along_z(a, b):
        xs = range(NX) if a < 4 and b < 4 else (2, 3)
        return [(device(i, c, a, j), device(i, c, b, j)) for i, c in everywhere for j in xs]

    def along_y(a, b):
        return [(device(a, 0, k, j), device(b, 0, k, j)) for k in range(NZ) for j in range(NX)]

    w, f = cov[0:TB], jnp.zeros((SLOTS * SB, SB), jnp.float32)
    b_tile = cov[0:TB]

    w, f = factor_step(0, flag, w, f)
    w, f = factor_step(1, flag, w, f)
    moved = ring_sends(b_tile, ROUNDS[0], along_y)
    w, f, got, moved = lax.optimization_barrier((w, f, got, moved))
    own = jnp.where(x == 0, quarter[0], jnp.where(x == 1, got[0], jnp.where(x == 2, got[2], got[1])))
    b_tile = ring_pick(b_tile, ROUNDS[0], y, moved)

    w, f = factor_step(2, flag, w, f)
    w, f = factor_step(3, flag, w, f)
    got = ring_sends(own, ROUNDS[0], along_z)
    moved = ring_sends(b_tile, ROUNDS[1], along_y)
    w, f, got, moved = lax.optimization_barrier((w, f, got, moved))
    own = ring_pick(own, ROUNDS[0], z, got)
    b_tile = ring_pick(b_tile, ROUNDS[1], y, moved)

    part = [f[3 * SB * q : 3 * SB * (q + 1)] for q in range(4)]
    got = [send(part[q], [(device(0, 0, 0, 0), device(0, 0, 0, q))]) for q in (1, 3, 2)]
    mine = jnp.where(x == 0, part[0], jnp.where(x == 1, got[0], jnp.where(x == 2, got[2], got[1])))

    def factor_y(a, b):
        return [(device(a, 0, 0, j), device(b, 0, 0, j)) for j in range(NX)]

    def factor_z(a, b):
        return [(device(i, 0, a, j), device(i, 0, b, j)) for i in range(NY) for j in range(NX)]

    def shift_x(by, cores):
        return [
            (device(i, c, k, j), device(i, c, k, (j + by) % NX))
            for i in range(NY)
            for c in cores
            for k in range(NZ)
            for j in range(NX)
        ]

    across = [(device(i, 0, k, j), device(i, 1, k, j)) for i in range(NY) for k in range(NZ) for j in range(NX)]

    got = ring_sends(own, ROUNDS[1], along_z)
    mine = ring_round(mine, ROUNDS[0], y, factor_y)
    b_other = send(b_tile, across)
    mine, got, b_other = lax.optimization_barrier((mine, got, b_other))
    own = ring_pick(own, ROUNDS[1], z, got)
    b_tile = jnp.where(core == 1, b_other, b_tile)

    left = send(own, shift_x(1, (0, 1)))
    right = send(own, shift_x(-1, (0, 1)))
    mine = ring_round(mine, ROUNDS[1], y, factor_y)
    mine = ring_round(mine, ROUNDS[0], z, factor_z)
    mine, left, right = lax.optimization_barrier((mine, left, right))

    opp_a = send(left[: HB // 2], shift_x(1, (0, 1)))
    opp_b = send(right[HB // 2 :], shift_x(-1, (0, 1)))
    mine = ring_round(mine, ROUNDS[1], z, factor_z)
    turned = jnp.concatenate([mine] + [send(mine, shift_x(-by, (0,))) for by in (1, 2, 3)], axis=0)
    turned = jnp.where(core == 1, send(turned, across), turned)

    pos = jnp.stack([row, col, x, 0]).astype(jnp.int32)
    out = update(pos, own, left, right, opp_a, opp_b, b_tile, turned, w, cov)
    return out.reshape(covariance.shape)


def solution(mesh):
    return jax.shard_map(
        on_device,
        mesh=mesh,
        in_specs=(P(None, "row", None, "col"),),
        out_specs=P(None, "row", None, "col"),
        check_vma=False,
    )
```

time: 597 us -> 153 us (0.26)
  the two profiles are of different devices: /device:TPU:1 before, /device:TPU:40 now
where the time goes in v1:
time: 153 us; the launch traced here: 152 us
  waiting for transfers between devices  60.6 us (40%)
  starting transfers between devices  58.8 us (38%)
  local copies, waits for them, and re-layouts  11.7 us (8%)
  Pallas kernels  11.6 us (8%)
  other arithmetic  9.1 us (6%)
    ppermute x31, waiting for transfers between devices, send(): return lax.ppermute(value, AXES, pairs)  60.6 us
    ppermute x31, starting transfers between devices, send(): return lax.ppermute(value, AXES, pairs)  58.8 us
    pallas_call x1, Pallas kernels, update(): pl.pallas_call(update_kernel, out_shape=jax.ShapeDtypeStruct((2 * TB, TB)...  11.4 us
    unnamed x27, local copies, waits for them, and re-layouts  6.79 us
    select_n x8, other arithmetic, ring_pick(): value = jnp.where(one_of(pos, [b for _, b in pairs]), received, value)  5.14 us
    reshape x1, local copies, waits for them, and re-layouts, on_device(): return out.reshape(covariance.shape)  3.48 us
  transfers between devices with their start and end apart: 31, of which 16 were waited for; matrix products, arithmetic and copies ran while one was open for 5% of the time, Pallas kernels for 0%

profile of v1, /device:TPU:40, one launch (start us, length us, event | category | flops | bytes accessed | tf_op | source)
XLA Modules:
  0.0 152.4 jit_solution(17966412681430085122)
XLA Ops:
  0.0 1.8 %copy.3 = f32[2,512,1,512]{3,1,2,0:T(8,128)S(1)} copy(f32[2,512,1,512]{3,2,1,0:T(1,128)} %param.1) | data formatting | bytes 4194304
  1.8 1.3 collective-permute-start.4
  3.1 1.7 %collective-permute-start.3 = (f32[512,512]{1,0:T(8,128)S(1)}, f32[512,512]{1,0:T(8,128)}, u32[]{:S(2)}, u32[]{:S(2)}) collective-permute-start(f32[512,512]{1,0:T(8,128)S(1)} %slice.45.w_in), channel_id=1, source_target_pairs={{0,192},{1,193},{2,194},{3,195},{4,196},{5,197},{6,198},{7,199},{8... | collective-permute-start | bytes 3145736 | tf_op jit(solution)/shard_map/ppermute | solution.py:167
  4.8 1.2 fusion
  6.0 5.7 %collective-permute-start.2 = (f32[256,512]{1,0:T(8,128)}, f32[256,512]{1,0:T(8,128)}, u32[]{:S(2)}, u32[]{:S(2)}) collective-permute-start(f32[256,512]{1,0:T(8,128)} %get-tuple-element.61), channel_id=1, source_target_pairs={{0,2},{32,34},{64,66},{96,98},{128,130},{160,162},{192,194},{224,2... | collective-permute-start | bytes 1572872 | tf_op jit(solution)/shard_map/ppermute | solution.py:167
  11.7 2.1 %collective-permute-start.1 = (f32[256,512]{1,0:T(8,128)}, f32[256,512]{1,0:T(8,128)}, u32[]{:S(2)}, u32[]{:S(2)}) collective-permute-start(f32[256,512]{1,0:T(8,128)} %get-tuple-element.62), channel_id=1, source_target_pairs={{0,3},{32,35},{64,67},{96,99},{128,131},{160,163},{192,195},{224,2... | collective-permute-start | bytes 1572872 | tf_op jit(solution)/shard_map/ppermute | solution.py:167
  13.8 2.1 %collective-permute-start = (f32[256,512]{1,0:T(8,128)}, f32[256,512]{1,0:T(8,128)}, u32[]{:S(2)}, u32[]{:S(2)}) collective-permute-start(f32[256,512]{1,0:T(8,128)} %get-tuple-element.63), channel_id=1, source_target_pairs={{0,1},{32,33},{64,65},{96,97},{128,129},{160,161},{192,193},{224,2... | collective-permute-start | bytes 1572872 | tf_op jit(solution)/shard_map/ppermute | solution.py:167
  16.0 1.0 copy-done.4
  17.0 0.9 copy-done.6
  17.8 1.2 copy-done.5
  19.1 1.1 copy-done.7
  20.2 3.3 %collective-permute-done.2 = f32[256,512]{1,0:T(8,128)} collective-permute-done((f32[256,512]{1,0:T(8,128)}, f32[256,512]{1,0:T(8,128)}, u32[]{:S(2)}, u32[]{:S(2)}) %collective-permute-start.2) | collective-permute-done | bytes 524320 | tf_op jit(solution)/shard_map/ppermute | solution.py:167
  23.5 1.3 collective-permute-done.1
  24.9 9.1 %collective-permute-done = f32[256,512]{1,0:T(8,128)} collective-permute-done((f32[256,512]{1,0:T(8,128)}, f32[256,512]{1,0:T(8,128)}, u32[]{:S(2)}, u32[]{:S(2)}) %collective-permute-start) | collective-permute-done | bytes 524320 | tf_op jit(solution)/shard_map/ppermute | solution.py:167
  34.0 1.3 slice_select_fusion
  35.3 0.7 collective-permute-start.6
  36.0 1.3 collective-permute-start.5
  37.3 1.6 %select_select_fusion.1 = f32[512,512]{1,0:T(8,128)S(1)} fusion(f32[512,512]{1,0:T(8,128)} %collective-permute-done.4, f32[512,512]{1,0:T(8,128)} %collective-permute-done.3, pred[]{:T(512)S(6)} %eq.89, pred[]{:T(512)S(6)} %eq.83, f32[1024,512]{1,0:T(8,128)S(1)} %bitcast.9), kind=kLoop, calls=%fused_computation.1 | loop fusion | flops 524288 | bytes 4194306 | tf_op jit(solution)/shard_map/jit(_where)/select_n | solution.py:189
  38.9 0.7 collective-permute-start.8
  39.6 1.4 collective-permute-start.7
  41.3 6.9 %collective-permute-done.5 = f32[256,512]{1,0:T(8,128)S(1)} collective-permute-done((f32[256,512]{1,0:T(8,128)S(1)}, f32[256,512]{1,0:T(8,128)S(1)}, u32[]{:S(2)}, u32[]{:S(2)}) %collective-permute-start.5) | collective-permute-done | bytes 524320 | tf_op jit(solution)/shard_map/ppermute | solution.py:167
  48.3 5.1 %collective-permute-done.7 = f32[512,512]{1,0:T(8,128)S(1)} collective-permute-done((f32[512,512]{1,0:T(8,128)S(1)}, f32[512,512]{1,0:T(8,128)S(1)}, u32[]{:S(2)}, u32[]{:S(2)}) %collective-permute-start.7) | collective-permute-done | bytes 1048608 | tf_op jit(solution)/shard_map/ppermute | solution.py:167
  53.3 0.3 select_select_fusion
  53.7 2.3 %collective-permute-start.16 = (f32[512,512]{1,0:T(8,128)S(1)}, f32[512,512]{1,0:T(8,128)}, u32[]{:S(2)}, u32[]{:S(2)}) collective-permute-start(f32[512,512]{1,0:T(8,128)S(1)} %select_select_fusion), channel_id=1, source_target_pairs={{0,32},{1,33},{2,34},{3,35},{4,36},{5,37},{6,38},{7,39},{8,40},{9,... | collective-permute-start | bytes 3145736 | tf_op jit(solution)/shard_map/ppermute | solution.py:167
  56.0 0.7 collective-permute-start.11
  56.7 0.7 collective-permute-start.10
  57.4 0.7 collective-permute-start.9
  58.1 1.0 select_select_fusion.3
  59.0 1.4 collective-permute-start.15
  60.5 2.1 %collective-permute-start.14 = (f32[256,512]{1,0:T(8,128)}, f32[256,512]{1,0:T(8,128)}, u32[]{:S(2)}, u32[]{:S(2)}) collective-permute-start(f32[256,512]{1,0:T(8,128)} %select_select_fusion.3), channel_id=1, source_target_pairs={{0,4},{1,5},{2,6},{3,7},{32,36},{33,37},{34,38},{35,39},{64,68},{6... | collective-permute-start | bytes 1572872 | tf_op jit(solution)/shard_map/ppermute | solution.py:167
  62.7 0.7 collective-permute-start.13
  63.3 1.3 collective-permute-start.12
  64.7 11.6 %collective-permute-done.12 = f32[384,128]{1,0:T(8,128)} collective-permute-done((f32[384,128]{1,0:T(8,128)S(1)}, f32[384,128]{1,0:T(8,128)}, u32[]{:S(2)}, u32[]{:S(2)}) %collective-permute-start.12) | collective-permute-done | bytes 196640 | tf_op jit(solution)/shard_map/ppermute | solution.py:167
  76.3 1.0 select_select_fusion.7
  77.3 1.3 collective-permute-start.18
  78.6 0.7 collective-permute-start.17
  79.3 1.2 select_select_fusion.2.own_ref
  80.5 3.7 %collective-permute-start.22 = (f32[256,512]{1,0:T(8,128)S(1)}, f32[256,512]{1,0:T(8,128)S(1)}, u32[]{:S(2)}, u32[]{:S(2)}) collective-permute-start(f32[256,512]{1,0:T(8,128)S(1)} %select_select_fusion.2.own_ref), channel_id=1, source_target_pairs={{0,3},{1,0},{2,1},{3,2},{4,7},{5,4},{6,5},{7,6},{8,11},{9,8},{10,9... | collective-permute-start | bytes 1572872 | tf_op jit(solution)/shard_map/ppermute | solution.py:167
  84.2 2.2 %collective-permute-start.21 = (f32[256,512]{1,0:T(8,128)S(1)}, f32[256,512]{1,0:T(8,128)S(1)}, u32[]{:S(2)}, u32[]{:S(2)}) collective-permute-start(f32[256,512]{1,0:T(8,128)S(1)} %select_select_fusion.2.own_ref), channel_id=1, source_target_pairs={{0,1},{1,2},{2,3},{3,0},{4,5},{5,6},{6,7},{7,4},{8,9},{9,10},{10,1... | collective-permute-start | bytes 1572872 | tf_op jit(solution)/shard_map/ppermute | solution.py:167
  86.4 1.3 collective-permute-start.20
  87.7 1.3 collective-permute-start.19
  89.0 1.8 %collective-permute-done.20 = f32[384,128]{1,0:T(8,128)S(1)} collective-permute-done((f32[384,128]{1,0:T(8,128)S(1)}, f32[384,128]{1,0:T(8,128)S(1)}, u32[]{:S(2)}, u32[]{:S(2)}) %collective-permute-start.20) | collective-permute-done | bytes 196640 | tf_op jit(solution)/shard_map/ppermute | solution.py:167
  90.9 1.3 collective-permute-done.19
  92.2 0.8 collective-permute-done.22.right_ref
  93.0 5.0 %collective-permute-done.21.left_ref = f32[256,512]{1,0:T(8,128)S(1)} collective-permute-done((f32[256,512]{1,0:T(8,128)S(1)}, f32[256,512]{1,0:T(8,128)S(1)}, u32[]{:S(2)}, u32[]{:S(2)}) %collective-permute-start.21) | collective-permute-done | bytes 524320 | tf_op jit(solution)/shard_map/ppermute | solution.py:167
  98.0 0.8 copy-done
  98.7 1.3 collective-permute-start.26
  100.0 1.3 collective-permute-start.25
  101.4 1.8 %collective-permute-done.26 = f32[384,128]{1,0:T(8,128)S(1)} collective-permute-done((f32[384,128]{1,0:T(8,128)S(1)}, f32[384,128]{1,0:T(8,128)S(1)}, u32[]{:S(2)}, u32[]{:S(2)}) %collective-permute-start.26) | collective-permute-done | bytes 196640 | tf_op jit(solution)/shard_map/ppermute | solution.py:167
  103.2 1.3 collective-permute-done.25
  104.5 1.9 %collective-permute-start.29 = (f32[384,128]{1,0:T(8,128)S(1)}, f32[384,128]{1,0:T(8,128)S(1)}, u32[]{:S(2)}, u32[]{:S(2)}) collective-permute-start(f32[384,128]{1,0:T(8,128)S(1)} %select_select_fusion.4), channel_id=1, source_target_pairs={{0,1},{1,2},{2,3},{3,0},{4,5},{5,6},{6,7},{7,4},{8,9},{9,10},{10,1... | collective-permute-start | bytes 589832 | tf_op jit(solution)/shard_map/ppermute | solution.py:167
  106.5 3.2 %collective-permute-start.28 = (f32[384,128]{1,0:T(8,128)S(1)}, f32[384,128]{1,0:T(8,128)S(1)}, u32[]{:S(2)}, u32[]{:S(2)}) collective-permute-start(f32[384,128]{1,0:T(8,128)S(1)} %select_select_fusion.4), channel_id=1, source_target_pairs={{0,2},{1,3},{2,0},{3,1},{4,6},{5,7},{6,4},{7,5},{8,10},{9,11},{10,... | collective-permute-start | bytes 589832 | tf_op jit(solution)/shard_map/ppermute | solution.py:167
  109.7 4.5 %collective-permute-start.27 = (f32[384,128]{1,0:T(8,128)S(1)}, f32[384,128]{1,0:T(8,128)S(1)}, u32[]{:S(2)}, u32[]{:S(2)}) collective-permute-start(f32[384,128]{1,0:T(8,128)S(1)} %select_select_fusion.4), channel_id=1, source_target_pairs={{0,3},{1,0},{2,1},{3,2},{4,7},{5,4},{6,5},{7,6},{8,11},{9,8},{10,9... | collective-permute-start | bytes 589832 | tf_op jit(solution)/shard_map/ppermute | solution.py:167
  114.3 1.3 collective-permute-done.28
  115.5 2.7 %collective-permute-done.27 = f32[384,128]{1,0:T(8,128)S(1)} collective-permute-done((f32[384,128]{1,0:T(8,128)S(1)}, f32[384,128]{1,0:T(8,128)S(1)}, u32[]{:S(2)}, u32[]{:S(2)}) %collective-permute-start.27) | collective-permute-done | bytes 196640 | tf_op jit(solution)/shard_map/ppermute | solution.py:167
  118.2 0.9 pad_maximum_fusion
  119.2 2.2 %collective-permute-start.30 = (f32[1536,128]{1,0:T(8,128)}, f32[1536,128]{1,0:T(8,128)}, u32[]{:S(2)}, u32[]{:S(2)}) collective-permute-start(f32[1536,128]{1,0:T(8,128)} %pad_maximum_fusion), channel_id=1, source_target_pairs={{0,32},{1,33},{2,34},{3,35},{4,36},{5,37},{6,38},{7,39},{8,40},{9,... | collective-permute-start | bytes 2359304 | tf_op jit(solution)/shard_map/ppermute | solution.py:167
  121.4 1.5 broadcast_select_fusion.b_ref
  123.0 5.0 %collective-permute-start.24 = (f32[128,512]{1,0:T(8,128)S(1)}, f32[128,512]{1,0:T(8,128)S(1)}, u32[]{:S(2)}, u32[]{:S(2)}) collective-permute-start(f32[128,512]{1,0:T(8,128)S(1)} %slice.44), channel_id=1, source_target_pairs={{0,3},{1,0},{2,1},{3,2},{4,7},{5,4},{6,5},{7,6},{8,11},{9,8},{10,9... | collective-permute-start | bytes 786440 | tf_op jit(solution)/shard_map/ppermute | solution.py:167
  127.9 2.1 %collective-permute-start.23 = (f32[128,512]{1,0:T(8,128)S(1)}, f32[128,512]{1,0:T(8,128)S(1)}, u32[]{:S(2)}, u32[]{:S(2)}) collective-permute-start(f32[128,512]{1,0:T(8,128)S(1)} %slice.43), channel_id=1, source_target_pairs={{0,1},{1,2},{2,3},{3,0},{4,5},{5,6},{6,7},{7,4},{8,9},{9,10},{10,1... | collective-permute-start | bytes 786440 | tf_op jit(solution)/shard_map/ppermute | solution.py:167
  130.2 1.6 %collective-permute-done.24.opp_b_ref = f32[128,512]{1,0:T(8,128)S(1)} collective-permute-done((f32[128,512]{1,0:T(8,128)S(1)}, f32[128,512]{1,0:T(8,128)S(1)}, u32[]{:S(2)}, u32[]{:S(2)}) %collective-permute-start.24) | collective-permute-done | bytes 262176 | tf_op jit(solution)/shard_map/ppermute | solution.py:167
  131.8 5.6 %collective-permute-done.23.opp_a_ref = f32[128,512]{1,0:T(8,128)S(1)} collective-permute-done((f32[128,512]{1,0:T(8,128)S(1)}, f32[128,512]{1,0:T(8,128)S(1)}, u32[]{:S(2)}, u32[]{:S(2)}) %collective-permute-start.23) | collective-permute-done | bytes 262176 | tf_op jit(solution)/shard_map/ppermute | solution.py:167
  137.4 11.4 %update.1 = f32[1024,512]{1,0:T(8,128)S(1)} custom-call(s32[4]{0:T(128)S(1)} %pad_add_fusion.pos_ref, f32[256,512]{1,0:T(8,128)S(1)} %select_select_fusion.2.own_ref, f32[256,512]{1,0:T(8,128)S(1)} %copy-done.1, f32[256,512]{1,0:T(8,128)S(1)} %collective-permute-done.22.right_ref, f32[128,512]{1,0:T(8,128)S(1)} %collective-permute-done.23.opp_a_ref, ...), custom_call_target="tpu_custom_call" | custom-call | flops 8000000000 | bytes 9000000 | tf_op jit(solution)/shard_map/update/pallas_call | solution.py:150
  148.9 3.5 %copy.2 = f32[2,512,1,512]{3,2,1,0:T(1,128)} copy(f32[2,512,1,512]{3,1,0,2:T(8,128)S(1)} %bitcast.11) | data formatting | bytes 4194304 | tf_op jit(solution)/shard_map/reshape | solution.py:280
  (51 shorter events, 0.8 us)
Async XLA Ops:
  1.8 32.2 %collective-permute-start.4 = (f32[512,512]{1,0:T(8,128)S(1)}, f32[512,512]{1,0:T(8,128)}, u32[]{:S(2)}, u32[]{:S(2)}) collective-permute-start(f32[512,512]{1,0:T(8,128)S(1)} %slice.45.w_in), channel_id=1, source_target_pairs={{0,320},{1,321},{2,322},{3,323},{4,324},{5,325},{6,326},{7,327},{8... | collective-permute-start | bytes 3145736 | tf_op jit(solution)/shard_map/ppermute | solution.py:167
  3.1 30.9 %collective-permute-start.3 = (f32[512,512]{1,0:T(8,128)S(1)}, f32[512,512]{1,0:T(8,128)}, u32[]{:S(2)}, u32[]{:S(2)}) collective-permute-start(f32[512,512]{1,0:T(8,128)S(1)} %slice.45.w_in), channel_id=1, source_target_pairs={{0,192},{1,193},{2,194},{3,195},{4,196},{5,197},{6,198},{7,199},{8... | collective-permute-start | bytes 3145736 | tf_op jit(solution)/shard_map/ppermute | solution.py:167
  6.0 17.5 %collective-permute-start.2 = (f32[256,512]{1,0:T(8,128)}, f32[256,512]{1,0:T(8,128)}, u32[]{:S(2)}, u32[]{:S(2)}) collective-permute-start(f32[256,512]{1,0:T(8,128)} %get-tuple-element.61), channel_id=1, source_target_pairs={{0,2},{32,34},{64,66},{96,98},{128,130},{160,162},{192,194},{224,2... | collective-permute-start | bytes 1572872 | tf_op jit(solution)/shard_map/ppermute | solution.py:167
  11.7 13.1 %collective-permute-start.1 = (f32[256,512]{1,0:T(8,128)}, f32[256,512]{1,0:T(8,128)}, u32[]{:S(2)}, u32[]{:S(2)}) collective-permute-start(f32[256,512]{1,0:T(8,128)} %get-tuple-element.62), channel_id=1, source_target_pairs={{0,3},{32,35},{64,67},{96,99},{128,131},{160,163},{192,195},{224,2... | collective-permute-start | bytes 1572872 | tf_op jit(solution)/shard_map/ppermute | solution.py:167
  13.8 20.2 %collective-permute-start = (f32[256,512]{1,0:T(8,128)}, f32[256,512]{1,0:T(8,128)}, u32[]{:S(2)}, u32[]{:S(2)}) collective-permute-start(f32[256,512]{1,0:T(8,128)} %get-tuple-element.63), channel_id=1, source_target_pairs={{0,1},{32,33},{64,65},{96,97},{128,129},{160,161},{192,193},{224,2... | collective-permute-start | bytes 1572872 | tf_op jit(solution)/shard_map/ppermute | solution.py:167
  16.0 1.0 copy-start.4
  17.0 0.9 copy-start.6
  17.8 1.2 copy-start.5
  19.1 1.1 copy-start.7
  35.3 6.0 %collective-permute-start.6 = (f32[256,512]{1,0:T(8,128)S(1)}, f32[256,512]{1,0:T(8,128)S(1)}, u32[]{:S(2)}, u32[]{:S(2)}) collective-permute-start(f32[256,512]{1,0:T(8,128)S(1)} %slice_select_fusion), channel_id=1, source_target_pairs={{2,22},{3,23},{34,54},{35,55},{66,86},{67,87},{98,118},{99,119},{1... | collective-permute-start | bytes 1572872 | tf_op jit(solution)/shard_map/ppermute | solution.py:167
  36.0 12.3 %collective-permute-start.5 = (f32[256,512]{1,0:T(8,128)S(1)}, f32[256,512]{1,0:T(8,128)S(1)}, u32[]{:S(2)}, u32[]{:S(2)}) collective-permute-start(f32[256,512]{1,0:T(8,128)S(1)} %slice_select_fusion), channel_id=1, source_target_pairs={{0,12},{1,13},{2,14},{3,15},{32,44},{33,45},{34,46},{35,47},{64,76... | collective-permute-start | bytes 1572872 | tf_op jit(solution)/shard_map/ppermute | solution.py:167
  38.9 9.4 %collective-permute-start.8 = (f32[512,512]{1,0:T(8,128)S(1)}, f32[512,512]{1,0:T(8,128)S(1)}, u32[]{:S(2)}, u32[]{:S(2)}) collective-permute-start(f32[512,512]{1,0:T(8,128)S(1)} %select_select_fusion.1), channel_id=1, source_target_pairs={{0,448},{1,449},{2,450},{3,451},{4,452},{5,453},{6,454},{7,455},{8... | collective-permute-start | bytes 3145736 | tf_op jit(solution)/shard_map/ppermute | solution.py:167
  39.6 13.7 %collective-permute-start.7 = (f32[512,512]{1,0:T(8,128)S(1)}, f32[512,512]{1,0:T(8,128)S(1)}, u32[]{:S(2)}, u32[]{:S(2)}) collective-permute-start(f32[512,512]{1,0:T(8,128)S(1)} %select_select_fusion.1), channel_id=1, source_target_pairs={{0,64},{1,65},{2,66},{3,67},{4,68},{5,69},{6,70},{7,71},{8,72},{9,... | collective-permute-start | bytes 3145736 | tf_op jit(solution)/shard_map/ppermute | solution.py:167
  41.3 12.4 %copy-start.2 = (f32[512,512]{1,0:T(8,128)}, f32[512,512]{1,0:T(8,128)S(1)}, u32[]{:S(2)}) copy-start(f32[512,512]{1,0:T(8,128)S(1)} %get-tuple-element.60.w_ref) | copy-start | bytes 3145732
  53.7 9.0 %copy-start.8 = (f32[512,512]{1,0:T(8,128)}, f32[512,512]{1,0:T(8,128)S(1)}, u32[]{:S(2)}) copy-start(f32[512,512]{1,0:T(8,128)S(1)} %select_select_fusion) | copy-start | bytes 3145732
  53.7 23.6 %collective-permute-start.16 = (f32[512,512]{1,0:T(8,128)S(1)}, f32[512,512]{1,0:T(8,128)}, u32[]{:S(2)}, u32[]{:S(2)}) collective-permute-start(f32[512,512]{1,0:T(8,128)S(1)} %select_select_fusion), channel_id=1, source_target_pairs={{0,32},{1,33},{2,34},{3,35},{4,36},{5,37},{6,38},{7,39},{8,40},{9,... | collective-permute-start | bytes 3145736 | tf_op jit(solution)/shard_map/ppermute | solution.py:167
  56.0 4.5 %collective-permute-start.11 = (f32[384,128]{1,0:T(8,128)S(1)}, f32[384,128]{1,0:T(8,128)S(1)}, u32[]{:S(2)}, u32[]{:S(2)}) collective-permute-start(f32[384,128]{1,0:T(8,128)S(1)} %get-tuple-element.64), channel_id=1, source_target_pairs={{0,3}} | collective-permute-start | bytes 589832 | tf_op jit(solution)/shard_map/ppermute | solution.py:167
  56.7 5.9 %collective-permute-start.10 = (f32[384,128]{1,0:T(8,128)S(1)}, f32[384,128]{1,0:T(8,128)S(1)}, u32[]{:S(2)}, u32[]{:S(2)}) collective-permute-start(f32[384,128]{1,0:T(8,128)S(1)} %get-tuple-element.65), channel_id=1, source_target_pairs={{0,2}} | collective-permute-start | bytes 589832 | tf_op jit(solution)/shard_map/ppermute | solution.py:167
  57.4 5.2 %collective-permute-start.9 = (f32[384,128]{1,0:T(8,128)S(1)}, f32[384,128]{1,0:T(8,128)S(1)}, u32[]{:S(2)}, u32[]{:S(2)}) collective-permute-start(f32[384,128]{1,0:T(8,128)S(1)} %get-tuple-element.66), channel_id=1, source_target_pairs={{0,1}} | collective-permute-start | bytes 589832 | tf_op jit(solution)/shard_map/ppermute | solution.py:167
  59.0 18.2 %collective-permute-start.15 = (f32[256,512]{1,0:T(8,128)}, f32[256,512]{1,0:T(8,128)}, u32[]{:S(2)}, u32[]{:S(2)}) collective-permute-start(f32[256,512]{1,0:T(8,128)} %select_select_fusion.3), channel_id=1, source_target_pairs={{2,30},{3,31},{34,62},{35,63},{66,94},{67,95},{98,126},{99,127},{1... | collective-permute-start | bytes 1572872 | tf_op jit(solution)/shard_map/ppermute | solution.py:167
  60.5 16.8 %collective-permute-start.14 = (f32[256,512]{1,0:T(8,128)}, f32[256,512]{1,0:T(8,128)}, u32[]{:S(2)}, u32[]{:S(2)}) collective-permute-start(f32[256,512]{1,0:T(8,128)} %select_select_fusion.3), channel_id=1, source_target_pairs={{0,4},{1,5},{2,6},{3,7},{32,36},{33,37},{34,38},{35,39},{64,68},{6... | collective-permute-start | bytes 1572872 | tf_op jit(solution)/shard_map/ppermute | solution.py:167
  62.7 2.0 %collective-permute-start.13 = (f32[384,128]{1,0:T(8,128)S(1)}, f32[384,128]{1,0:T(8,128)S(1)}, u32[]{:S(2)}, u32[]{:S(2)}) collective-permute-start(f32[384,128]{1,0:T(8,128)S(1)} %select_select_fusion.8), channel_id=1, source_target_pairs={{0,192},{1,193},{2,194},{3,195}} | collective-permute-start | bytes 589832 | tf_op jit(solution)/shard_map/ppermute | solution.py:167
  63.3 12.9 %collective-permute-start.12 = (f32[384,128]{1,0:T(8,128)S(1)}, f32[384,128]{1,0:T(8,128)}, u32[]{:S(2)}, u32[]{:S(2)}) collective-permute-start(f32[384,128]{1,0:T(8,128)S(1)} %select_select_fusion.8), channel_id=1, source_target_pairs={{0,320},{1,321},{2,322},{3,323}} | collective-permute-start | bytes 589832 | tf_op jit(solution)/shard_map/ppermute | solution.py:167
  77.3 9.1 %collective-permute-start.18 = (f32[384,128]{1,0:T(8,128)S(1)}, f32[384,128]{1,0:T(8,128)S(1)}, u32[]{:S(2)}, u32[]{:S(2)}) collective-permute-start(f32[384,128]{1,0:T(8,128)S(1)} %select_select_fusion.7), channel_id=1, source_target_pairs={{0,64},{1,65},{2,66},{3,67},{192,256},{193,257},{194,258},{195,259... | collective-permute-start | bytes 589832 | tf_op jit(solution)/shard_map/ppermute | solution.py:167
  78.6 7.8 %collective-permute-start.17 = (f32[384,128]{1,0:T(8,128)S(1)}, f32[384,128]{1,0:T(8,128)S(1)}, u32[]{:S(2)}, u32[]{:S(2)}) collective-permute-start(f32[384,128]{1,0:T(8,128)S(1)} %select_select_fusion.7), channel_id=1, source_target_pairs={{0,448},{1,449},{2,450},{3,451},{192,128},{193,129},{194,130},{195... | collective-permute-start | bytes 589832 | tf_op jit(solution)/shard_map/ppermute | solution.py:167
  80.5 12.5 %collective-permute-start.22 = (f32[256,512]{1,0:T(8,128)S(1)}, f32[256,512]{1,0:T(8,128)S(1)}, u32[]{:S(2)}, u32[]{:S(2)}) collective-permute-start(f32[256,512]{1,0:T(8,128)S(1)} %select_select_fusion.2.own_ref), channel_id=1, source_target_pairs={{0,3},{1,0},{2,1},{3,2},{4,7},{5,4},{6,5},{7,6},{8,11},{9,8},{10,9... | collective-permute-start | bytes 1572872 | tf_op jit(solution)/shard_map/ppermute | solution.py:167
  84.2 13.8 %collective-permute-start.21 = (f32[256,512]{1,0:T(8,128)S(1)}, f32[256,512]{1,0:T(8,128)S(1)}, u32[]{:S(2)}, u32[]{:S(2)}) collective-permute-start(f32[256,512]{1,0:T(8,128)S(1)} %select_select_fusion.2.own_ref), channel_id=1, source_target_pairs={{0,1},{1,2},{2,3},{3,0},{4,5},{5,6},{6,7},{7,4},{8,9},{9,10},{10,1... | collective-permute-start | bytes 1572872 | tf_op jit(solution)/shard_map/ppermute | solution.py:167
  86.4 4.5 %collective-permute-start.20 = (f32[384,128]{1,0:T(8,128)S(1)}, f32[384,128]{1,0:T(8,128)S(1)}, u32[]{:S(2)}, u32[]{:S(2)}) collective-permute-start(f32[384,128]{1,0:T(8,128)S(1)} %select_select_fusion.6), channel_id=1, source_target_pairs={{0,12},{1,13},{2,14},{3,15},{64,76},{65,77},{66,78},{67,79},{128,1... | collective-permute-start | bytes 589832 | tf_op jit(solution)/shard_map/ppermute | solution.py:167
  87.7 4.5 %collective-permute-start.19 = (f32[384,128]{1,0:T(8,128)S(1)}, f32[384,128]{1,0:T(8,128)S(1)}, u32[]{:S(2)}, u32[]{:S(2)}) collective-permute-start(f32[384,128]{1,0:T(8,128)S(1)} %select_select_fusion.6), channel_id=1, source_target_pairs={{0,20},{1,21},{2,22},{3,23},{64,84},{65,85},{66,86},{67,87},{128,1... | collective-permute-start | bytes 589832 | tf_op jit(solution)/shard_map/ppermute | solution.py:167
  98.0 0.8 copy-start
  98.7 4.5 %collective-permute-start.26 = (f32[384,128]{1,0:T(8,128)S(1)}, f32[384,128]{1,0:T(8,128)S(1)}, u32[]{:S(2)}, u32[]{:S(2)}) collective-permute-start(f32[384,128]{1,0:T(8,128)S(1)} %select_select_fusion.5), channel_id=1, source_target_pairs={{0,4},{1,5},{2,6},{3,7},{64,68},{65,69},{66,70},{67,71},{128,132},... | collective-permute-start | bytes 589832 | tf_op jit(solution)/shard_map/ppermute | solution.py:167
  100.0 4.5 %collective-permute-start.25 = (f32[384,128]{1,0:T(8,128)S(1)}, f32[384,128]{1,0:T(8,128)S(1)}, u32[]{:S(2)}, u32[]{:S(2)}) collective-permute-start(f32[384,128]{1,0:T(8,128)S(1)} %select_select_fusion.5), channel_id=1, source_target_pairs={{0,28},{1,29},{2,30},{3,31},{64,92},{65,93},{66,94},{67,95},{128,1... | collective-permute-start | bytes 589832 | tf_op jit(solution)/shard_map/ppermute | solution.py:167
  104.5 9.7 %collective-permute-start.29 = (f32[384,128]{1,0:T(8,128)S(1)}, f32[384,128]{1,0:T(8,128)S(1)}, u32[]{:S(2)}, u32[]{:S(2)}) collective-permute-start(f32[384,128]{1,0:T(8,128)S(1)} %select_select_fusion.4), channel_id=1, source_target_pairs={{0,1},{1,2},{2,3},{3,0},{4,5},{5,6},{6,7},{7,4},{8,9},{9,10},{10,1... | collective-permute-start | bytes 589832 | tf_op jit(solution)/shard_map/ppermute | solution.py:167
  106.5 9.1 %collective-permute-start.28 = (f32[384,128]{1,0:T(8,128)S(1)}, f32[384,128]{1,0:T(8,128)S(1)}, u32[]{:S(2)}, u32[]{:S(2)}) collective-permute-start(f32[384,128]{1,0:T(8,128)S(1)} %select_select_fusion.4), channel_id=1, source_target_pairs={{0,2},{1,3},{2,0},{3,1},{4,6},{5,7},{6,4},{7,5},{8,10},{9,11},{10,... | collective-permute-start | bytes 589832 | tf_op jit(solution)/shard_map/ppermute | solution.py:167
  109.7 8.5 %collective-permute-start.27 = (f32[384,128]{1,0:T(8,128)S(1)}, f32[384,128]{1,0:T(8,128)S(1)}, u32[]{:S(2)}, u32[]{:S(2)}) collective-permute-start(f32[384,128]{1,0:T(8,128)S(1)} %select_select_fusion.4), channel_id=1, source_target_pairs={{0,3},{1,0},{2,1},{3,2},{4,7},{5,4},{6,5},{7,6},{8,11},{9,8},{10,9... | collective-permute-start | bytes 589832 | tf_op jit(solution)/shard_map/ppermute | solution.py:167
  115.5 2.7 %copy-start.9 = (f32[384,128]{1,0:T(8,128)}, f32[384,128]{1,0:T(8,128)S(1)}, u32[]{:S(2)}) copy-start(f32[384,128]{1,0:T(8,128)S(1)} %collective-permute-done.28) | copy-start | bytes 589828
  118.2 1.0 copy-start.11
  119.2 10.9 %collective-permute-start.30 = (f32[1536,128]{1,0:T(8,128)}, f32[1536,128]{1,0:T(8,128)}, u32[]{:S(2)}, u32[]{:S(2)}) collective-permute-start(f32[1536,128]{1,0:T(8,128)} %pad_maximum_fusion), channel_id=1, source_target_pairs={{0,32},{1,33},{2,34},{3,35},{4,36},{5,37},{6,38},{7,39},{8,40},{9,... | collective-permute-start | bytes 2359304 | tf_op jit(solution)/shard_map/ppermute | solution.py:167
  121.3 1.6 %copy-start.1 = (f32[256,512]{1,0:T(8,128)S(1)}, f32[256,512]{1,0:T(8,128)}, u32[]{:S(2)}) copy-start(f32[256,512]{1,0:T(8,128)} %copy-done) | copy-start | bytes 1572868
  121.4 8.7 %copy-start.10 = (f32[384,128]{1,0:T(8,128)S(1)}, f32[384,128]{1,0:T(8,128)}, u32[]{:S(2)}) copy-start(f32[384,128]{1,0:T(8,128)} %copy-done.9) | copy-start | bytes 589828
  121.4 8.7 %copy-start.12 = (f32[384,128]{1,0:T(8,128)S(1)}, f32[384,128]{1,0:T(8,128)}, u32[]{:S(2)}) copy-start(f32[384,128]{1,0:T(8,128)} %copy-done.11) | copy-start | bytes 589828
  122.9 14.5 %copy-start.3 = (f32[512,512]{1,0:T(8,128)S(1)}, f32[512,512]{1,0:T(8,128)}, u32[]{:S(2)}) copy-start(f32[512,512]{1,0:T(8,128)} %copy-done.2) | copy-start | bytes 3145732
  123.0 8.8 %collective-permute-start.24 = (f32[128,512]{1,0:T(8,128)S(1)}, f32[128,512]{1,0:T(8,128)S(1)}, u32[]{:S(2)}, u32[]{:S(2)}) collective-permute-start(f32[128,512]{1,0:T(8,128)S(1)} %slice.44), channel_id=1, source_target_pairs={{0,3},{1,0},{2,1},{3,2},{4,7},{5,4},{6,5},{7,6},{8,11},{9,8},{10,9... | collective-permute-start | bytes 786440 | tf_op jit(solution)/shard_map/ppermute | solution.py:167
  127.9 9.5 %collective-permute-start.23 = (f32[128,512]{1,0:T(8,128)S(1)}, f32[128,512]{1,0:T(8,128)S(1)}, u32[]{:S(2)}, u32[]{:S(2)}) collective-permute-start(f32[128,512]{1,0:T(8,128)S(1)} %slice.43), channel_id=1, source_target_pairs={{0,1},{1,2},{2,3},{3,0},{4,5},{5,6},{6,7},{7,4},{8,9},{9,10},{10,1... | collective-permute-start | bytes 786440 | tf_op jit(solution)/shard_map/ppermute | solution.py:167

commit v2 on v1

v2 whole, which is shorter than its diff:
```python
import jax
import jax.numpy as jnp
from jax import lax
from jax.experimental import pallas as pl
from jax.experimental.pallas import tpu as pltpu
from jax.sharding import PartitionSpec as P

AXES = ("row", "col")
ROWS, COLS = 16, 32
NZ, NX = 8, 4
TB = 512
SB = 128
HB = 256
SLOTS = 12
HIGHEST = lax.Precision.HIGHEST
M0, M1, X10, L20, L21, L30, L31, M2, M3, X32 = range(10)


def nn(a, b):
    return lax.dot_general(a, b, (((1,), (0,)), ((), ())), precision=HIGHEST, preferred_element_type=jnp.float32)


def nt(a, b):
    return lax.dot_general(a, b, (((1,), (1,)), ((), ())), precision=HIGHEST, preferred_element_type=jnp.float32)


def factor_block(block):
    tiles = SB // 8
    lane = lax.broadcasted_iota(jnp.int32, (8, SB), 1)
    sub = lax.broadcasted_iota(jnp.int32, (8, SB), 0)
    s = [block[8 * t : 8 * t + 8, :] for t in range(tiles)]
    e = [jnp.where(lane == sub + 8 * t, 1.0, 0.0).astype(jnp.float32) for t in range(tiles)]
    upper, inverse = [], []
    for b in range(tiles):
        cols = [
            [jnp.broadcast_to(s[t][:, 8 * b + m : 8 * b + m + 1], (8, SB)) for t in range(b, tiles)]
            for m in range(8)
        ]
        top, top_e = s[b], e[b]
        out_u, out_e = jnp.zeros_like(top), jnp.zeros_like(top)
        done = []
        for m in range(8):
            d = jnp.broadcast_to(cols[m][0][m : m + 1, :], (8, SB))
            r = lax.rsqrt(d)
            r = r * (1.5 - (0.5 * d) * (r * r))
            lc = [c * r for c in cols[m]]
            ur = jnp.broadcast_to(top[m : m + 1, :], (8, SB)) * r
            er = jnp.broadcast_to(top_e[m : m + 1, :], (8, SB)) * r
            out_u = jnp.where(sub == m, ur, out_u)
            out_e = jnp.where(sub == m, er, out_e)
            for k in range(m + 1, 8):
                f = jnp.broadcast_to(lc[0][k : k + 1, :], (8, SB))
                cols[k] = [c - l * f for c, l in zip(cols[k], lc)]
            below = jnp.where(sub > m, lc[0], 0.0)
            top = top - below * ur
            top_e = top_e - below * er
            done.append((lc, ur, er))
        for t in range(b + 1, tiles):
            for lc, ur, er in done:
                s[t] = s[t] - lc[t - b] * ur
                e[t] = e[t] - lc[t - b] * er
        upper.append(jnp.where(lane >= sub + 8 * b, out_u, 0.0))
        inverse.append(out_e)
    return jnp.concatenate(upper, axis=0), jnp.concatenate(inverse, axis=0)


def wide(ref, first, rows, lo=0, hi=4):
    return jnp.concatenate([ref[pl.ds(4 * first + i, rows, stride=4), :] for i in range(lo, hi)], axis=1)


def put_wide(ref, first, value):
    for i in range(value.shape[1] // SB):
        ref[pl.ds(4 * first + i, value.shape[0], stride=4), :] = value[:, i * SB : (i + 1) * SB]


def factor_kernel(flag_ref, a_ref, low_ref, f_ref, w_ref):
    @pl.when(flag_ref[0] == 1)
    def _():
        def slot(i):
            return pl.ds(i * SB, SB)

        w_ref[...] = wide(a_ref, 0, TB)
        for k in range(4):
            lo, hi = k * SB, (k + 1) * SB
            u, inv = factor_block(w_ref[lo:hi, lo:hi])
            f_ref[slot((M0, M1, M2, M3)[k]), :] = inv
            w_ref[lo:hi, lo:hi] = u.T
            if hi < TB:
                below = nt(w_ref[hi:, lo:hi], inv)
                w_ref[hi:, hi:] = w_ref[hi:, hi:] - nt(below, below)
                w_ref[hi:, lo:hi] = below
                w_ref[lo:hi, hi:] = jnp.zeros((SB, TB - hi), jnp.float32)
                if k < 2:
                    f_ref[slot((L20, L21)[k]), :] = below[2 * SB - hi : 3 * SB - hi]
                    f_ref[slot((L30, L31)[k]), :] = below[3 * SB - hi : 4 * SB - hi]
            if k % 2 == 1:
                prev = f_ref[slot((M0, M2)[k // 2]), :]
                f_ref[slot((X10, X32)[k // 2]), :] = -nn(inv, nn(w_ref[lo:hi, lo - SB : lo], prev))
        put_wide(low_ref, 0, w_ref[...])


def factor_tile(flag, a):
    vmem = pl.BlockSpec(memory_space=pltpu.VMEM)
    return pl.pallas_call(
        factor_kernel,
        out_shape=(
            jax.ShapeDtypeStruct((4 * TB, SB), jnp.float32),
            jax.ShapeDtypeStruct((SLOTS * SB, SB), jnp.float32),
        ),
        in_specs=[pl.BlockSpec(memory_space=pltpu.SMEM), vmem],
        out_specs=(vmem, vmem),
        scratch_shapes=[pltpu.VMEM((TB, TB), jnp.float32)],
        cost_estimate=pl.CostEstimate(flops=20_000_000_000, bytes_accessed=3_000_000, transcendentals=0),
        compiler_params=pltpu.CompilerParams(vmem_limit_bytes=24 * 1024 * 1024),
        name="factor",
    )(flag, a)


def update_kernel(pos_ref, own_ref, left_ref, right_ref, opp_a_ref, opp_b_ref, b_ref, f_ref, low_ref, cov_ref, out_ref, y_ref):
    row, col, x = pos_ref[0], pos_ref[1], pos_ref[2]

    def block(i):
        place = lax.rem(i // 3 - x + 4, 4)
        return f_ref[pl.ds(pl.multiple_of(place * (3 * SB) + (i % 3) * SB, SB), SB), :]

    zero = jnp.zeros((SB, SB), jnp.float32)

    def square(a, b, c, d):
        return jnp.concatenate(
            [jnp.concatenate([a, b], axis=1), jnp.concatenate([c, d], axis=1)], axis=0
        )

    d0 = square(block(M0), zero, block(X10), block(M1))
    d1 = square(block(M2), zero, block(X32), block(M3))
    g = square(block(L20), block(L21), block(L30), block(L31))
    y0 = nn(d0, wide(b_ref, 0, HB))
    y_ref[0:HB, :] = y0
    y_ref[HB:TB, :] = nn(d1, wide(b_ref, HB, HB) - nn(g, y0))

    def piece(q, raw0, raw1):
        x0 = nt(raw0, d0)
        x1 = nt(raw1 - nt(x0, g), d1)
        xs = jnp.concatenate([x0, x1], axis=1)
        tile_row = row + ROWS * (q // 2)

        @pl.when(col > 0)
        def _():
            cov = wide(cov_ref, q * HB, HB)
            new = cov - nn(xs, y_ref[...])
            put_wide(out_ref, q * HB, jnp.where(tile_row >= col, new, cov))

        @pl.when(col == 0)
        def _():
            low = wide(low_ref, lax.rem(q, 2) * HB, HB)
            put_wide(out_ref, q * HB, jnp.where(tile_row == 0, low, xs))

    for shift, ref in ((0, own_ref), (3, left_ref), (1, right_ref)):
        piece(lax.rem(x + shift, 4), wide(ref, 0, HB, 0, 2), wide(ref, 0, HB, 2, 4))
    half = HB // 2
    opp0 = jnp.concatenate([wide(opp_a_ref, 0, half, 0, 2), wide(opp_b_ref, 0, half, 0, 2)], axis=0)
    opp1 = jnp.concatenate([wide(opp_a_ref, 0, half, 2, 4), wide(opp_b_ref, 0, half, 2, 4)], axis=0)
    piece(lax.rem(x + 2, 4), opp0, opp1)


def update(pos, own, left, right, opp_a, opp_b, b, f, low, cov):
    vmem = pl.BlockSpec(memory_space=pltpu.VMEM)
    return pl.pallas_call(
        update_kernel,
        out_shape=jax.ShapeDtypeStruct((8 * TB, SB), jnp.float32),
        in_specs=[pl.BlockSpec(memory_space=pltpu.SMEM)] + [vmem] * 9,
        out_specs=vmem,
        scratch_shapes=[pltpu.VMEM((TB, TB), jnp.float32)],
        cost_estimate=pl.CostEstimate(flops=8_000_000_000, bytes_accessed=9_000_000, transcendentals=0),
        compiler_params=pltpu.CompilerParams(vmem_limit_bytes=40 * 1024 * 1024),
        name="update",
    )(pos, own, left, right, opp_a, opp_b, b, f, low, cov)


def send(value, pairs):
    return lax.ppermute(value, AXES, pairs)


def one_of(pos, places):
    found = pos == places[0]
    for place in places[1:]:
        found = jnp.logical_or(found, pos == place)
    return found


ROUNDS = (
    (((0, 3),), ((0, 5),)),
    (((0, 1), (3, 4), (5, 6)), ((0, 7), (3, 2))),
)


def ring_sends(value, moves, lift):
    return [send(value, [p for a, b in pairs for p in lift(a, b)]) for pairs in moves]


def ring_pick(value, moves, pos, got):
    for pairs, received in zip(moves, got):
        value = jnp.where(one_of(pos, [b for _, b in pairs]), received, value)
    return value


def ring_round(value, moves, pos, lift):
    return ring_pick(value, moves, pos, ring_sends(value, moves, lift))


def last_col(row, quarter):
    return row if quarter < 2 else row + ROWS


CHILDREN = {0: (3, 5, 1, 7), 3: (2, 4), 5: (6,), 1: (), 2: (), 4: (), 6: (), 7: ()}


def reaches(place, last):
    return NX * place <= last or any(reaches(c, last) for c in CHILDREN[place])


def on_device(covariance):
    row = lax.axis_index("row")
    col = lax.axis_index("col")
    y, core = row // 2, row % 2
    z, x = col // NX, col % NX
    cov = covariance.reshape(8 * TB, SB)
    is_root = jnp.logical_and(row == 0, col == 0)
    flag = is_root.astype(jnp.int32).reshape(1)
    rows = range(ROWS)
    quarter_rows = HB * 4

    def at(i, k, j):
        return i * COLS + k * NX + j

    def tied(*values):
        return lax.optimization_barrier(values)

    def scatter(q):
        return [(at(i, 0, 0), at(i, 0, q)) for i in rows if last_col(i, q) > 0]

    def along_z(a, b):
        return [(at(i, a, j), at(i, b, j)) for i in rows for j in range(NX) if last_col(i, j) > 0 and reaches(b, last_col(i, j))]

    def shift_x(by, cores):
        return [
            (at(i, k, j), at(i, k, (j + by) % NX))
            for i in rows
            if i % 2 in cores
            for k in range(NZ)
            for j in range(NX)
            if len(cores) == 1 or NX * k <= last_col(i, 2)
        ]

    def along_y(a, b):
        return [(at(2 * a, k, j), at(2 * b, k, j)) for k in range(NZ) for j in range(NX) if k + j > 0]

    across = [(at(i, k, j), at(i + 1, k, j)) for i in rows[::2] for k in range(NZ) for j in range(NX)]

    def factor_y(a, b):
        return [(at(2 * a, 0, j), at(2 * b, 0, j)) for j in range(NX)]

    def factor_z(a, b):
        return [(at(i, a, j), at(i, b, j)) for i in rows[::2] for j in range(NX)]

    def by_x(values):
        return jnp.where(x == 0, values[0], jnp.where(x == 1, values[1], jnp.where(x == 2, values[2], values[3])))

    quarter = [cov[quarter_rows * q : quarter_rows * (q + 1)] for q in range(4)]
    got = [send(quarter[q], scatter(q)) for q in (3, 2, 1)]
    low, f = factor_tile(flag, cov[0 : 4 * TB])

    got, f, b_tile = tied(got, f, cov[0 : 4 * TB])
    own = by_x([quarter[0], got[2], got[1], got[0]])
    moved = ring_sends(b_tile, ROUNDS[0], along_y)
    got = ring_sends(own, ROUNDS[0], along_z)

    f, got, moved = tied(f, got, moved)
    own = ring_pick(own, ROUNDS[0], z, got)
    b_tile = ring_pick(b_tile, ROUNDS[0], y, moved)
    got = ring_sends(own, ROUNDS[1], along_z)
    moved = ring_sends(b_tile, ROUNDS[1], along_y)

    part = [f[3 * SB * q : 3 * SB * (q + 1)] for q in range(4)]
    given = [send(part[q], [(0, q)]) for q in (1, 2, 3)]
    mine = by_x([part[0]] + given)

    mine, got, moved = tied(mine, got, moved)
    own = ring_pick(own, ROUNDS[1], z, got)
    b_tile = ring_pick(b_tile, ROUNDS[1], y, moved)
    left = send(own, shift_x(1, (0, 1)))
    right = send(own, shift_x(-1, (0, 1)))
    mine = ring_round(mine, ROUNDS[0], y, factor_y)
    mine, b_tile = tied(mine, b_tile)
    b_other = send(b_tile, across)
    mine = ring_round(mine, ROUNDS[1], y, factor_y)
    mine = ring_round(mine, ROUNDS[0], z, factor_z)

    mine, left, right, b_other = tied(mine, left, right, b_other)
    b_tile = jnp.where(core == 1, b_other, b_tile)
    opp_a = send(left[: quarter_rows // 2], shift_x(1, (0, 1)))
    opp_b = send(right[quarter_rows // 2 :], shift_x(-1, (0, 1)))
    mine = ring_round(mine, ROUNDS[1], z, factor_z)

    mine, opp_a, opp_b, b_tile = tied(mine, opp_a, opp_b, b_tile)
    turned = jnp.concatenate([mine] + [send(mine, shift_x(-by, (0,))) for by in (1, 2, 3)], axis=0)
    turned = jnp.where(core == 1, send(turned, across), turned)

    pos = jnp.stack([row, col, x, 0]).astype(jnp.int32)
    out = update(pos, own, left, right, opp_a, opp_b, b_tile, turned, low, cov)
    return out.reshape(covariance.shape)


def solution(mesh):
    return jax.shard_map(
        on_device,
        mesh=mesh,
        in_specs=(P(None, "row", None, "col"),),
        out_specs=P(None, "row", None, "col"),
        check_vma=False,
    )
```

time: 153 us -> 155 us (1.013)
  the two profiles are of different devices: /device:TPU:40 before, /device:TPU:29 now
where the time goes in v2:
time: 155 us; the launch traced here: 154 us
  waiting for transfers between devices  76.5 us (49%)
  starting transfers between devices  45.1 us (29%)
  Pallas kernels  13.5 us (9%)
  other arithmetic  10.6 us (7%)
  local copies, waits for them, and re-layouts  8.16 us (5%)
    ppermute x31, waiting for transfers between devices, send(): return lax.ppermute(value, AXES, pairs)  76.5 us
    ppermute x31, starting transfers between devices, send(): return lax.ppermute(value, AXES, pairs)  45.1 us
    pallas_call x1, Pallas kernels, update(): pl.pallas_call(update_kernel, out_shape=jax.ShapeDtypeStruct((8 * TB, SB)...  13.3 us
    select_n x8, other arithmetic, ring_pick(): value = jnp.where(one_of(pos, [b for _, b in pairs]), received, value)  6.04 us
  transfers between devices with their start and end apart: 31, of which 10 were waited for; matrix products, arithmetic and copies ran while one was open for 7% of the time, Pallas kernels for 0%

profile of v2, /device:TPU:29, one launch (start us, length us, event | category | flops | bytes accessed | tf_op | source)
XLA Modules:
  0.0 154.2 jit_solution(10849905908485875206)
XLA Ops:
  0.0 2.7 %fusion = (f32[1024,128]{1,0:T(8,128)}, f32[1024,128]{1,0:T(8,128)}, f32[1024,128]{1,0:T(8,128)}) fusion(f32[4096,128]{1,0:T(8,128)} %bitcast.7), kind=kLoop, calls=%fused_computation.17 | loop fusion | bytes 3145728 | tf_op jit(solution)/shard_map/slice | solution.py:268
  2.7 1.5 collective-permute-start
  4.1 1.3 collective-permute-start.1
  5.4 1.5 collective-permute-start.2
  6.9 0.7 slice.40
  7.6 0.2 factor.1
  7.9 0.9 copy-done.1
  8.8 1.0 copy-done.2
  9.7 0.0 collective-permute-done
  9.7 11.3 %collective-permute-done.1 = f32[1024,128]{1,0:T(8,128)} collective-permute-done((f32[1024,128]{1,0:T(8,128)}, f32[1024,128]{1,0:T(8,128)}, u32[]{:S(2)}, u32[]{:S(2)}) %collective-permute-start.1) | collective-permute-done | bytes 524320 | tf_op jit(solution)/shard_map/ppermute | solution.py:180
  21.0 0.0 collective-permute-done.2
  21.0 1.6 %collective-permute-start.5 = (f32[2048,128]{1,0:T(8,128)S(1)}, f32[2048,128]{1,0:T(8,128)}, u32[]{:S(2)}, u32[]{:S(2)}) collective-permute-start(f32[2048,128]{1,0:T(8,128)S(1)} %bitcast.11), channel_id=1, source_target_pairs={{1,193},{2,194},{3,195},{4,196},{5,197},{6,198},{7,199},{8,200},{9... | collective-permute-start | bytes 3145736 | tf_op jit(solution)/shard_map/ppermute | solution.py:180
  22.6 1.6 %collective-permute-start.6 = (f32[2048,128]{1,0:T(8,128)S(1)}, f32[2048,128]{1,0:T(8,128)}, u32[]{:S(2)}, u32[]{:S(2)}) collective-permute-start(f32[2048,128]{1,0:T(8,128)S(1)} %bitcast.12), channel_id=1, source_target_pairs={{1,321},{2,322},{3,323},{4,324},{5,325},{6,326},{7,327},{8,328},{9... | collective-permute-start | bytes 3145736 | tf_op jit(solution)/shard_map/ppermute | solution.py:180
  24.3 2.0 %slice_select_fusion = f32[1024,128]{1,0:T(8,128)} fusion(f32[4096,128]{1,0:T(8,128)S(1)} %bitcast.8, f32[1024,128]{1,0:T(8,128)} %collective-permute-done.2, f32[1024,128]{1,0:T(8,128)} %collective-permute-done.1, f32[1024,128]{1,0:T(8,128)} %collective-permute-done, pred[]{:T(512)S(6)} %eq.87, pred[]{:T(512)S(6)} %eq.86, pred[]{:T(512)S(6)} %eq.83), kind=kLoop, calls=%fused_computation.2 | loop fusion | flops 393216 | bytes 2621443 | tf_op jit(solution)/shard_map/jit(_where)/select_n | solution.py:266
  26.2 2.1 %collective-permute-start.3 = (f32[1024,128]{1,0:T(8,128)}, f32[1024,128]{1,0:T(8,128)}, u32[]{:S(2)}, u32[]{:S(2)}) collective-permute-start(f32[1024,128]{1,0:T(8,128)} %slice_select_fusion), channel_id=1, source_target_pairs={{2,14},{3,15},{34,46},{35,47},{66,78},{67,79},{98,110},{99,111},{1... | collective-permute-start | bytes 1572872 | tf_op jit(solution)/shard_map/ppermute | solution.py:180
  28.3 2.1 %collective-permute-start.4 = (f32[1024,128]{1,0:T(8,128)}, f32[1024,128]{1,0:T(8,128)}, u32[]{:S(2)}, u32[]{:S(2)}) collective-permute-start(f32[1024,128]{1,0:T(8,128)} %slice_select_fusion), channel_id=1, source_target_pairs={{130,150},{131,151},{162,182},{163,183},{194,214},{195,215},{226,2... | collective-permute-start | bytes 1572872 | tf_op jit(solution)/shard_map/ppermute | solution.py:180
  30.4 6.6 %collective-permute-done.3 = f32[1024,128]{1,0:T(8,128)} collective-permute-done((f32[1024,128]{1,0:T(8,128)}, f32[1024,128]{1,0:T(8,128)}, u32[]{:S(2)}, u32[]{:S(2)}) %collective-permute-start.3) | collective-permute-done | bytes 524320 | tf_op jit(solution)/shard_map/ppermute | solution.py:180
  37.0 2.1 %collective-permute-done.4 = f32[1024,128]{1,0:T(8,128)} collective-permute-done((f32[1024,128]{1,0:T(8,128)}, f32[1024,128]{1,0:T(8,128)}, u32[]{:S(2)}, u32[]{:S(2)}) %collective-permute-start.4) | collective-permute-done | bytes 524320 | tf_op jit(solution)/shard_map/ppermute | solution.py:180
  39.0 0.0 collective-permute-done.5
  39.0 0.0 collective-permute-done.6
  39.0 2.3 %select_select_fusion.1 = f32[2048,128]{1,0:T(8,128)} fusion(f32[2048,128]{1,0:T(8,128)} %collective-permute-done.6, f32[2048,128]{1,0:T(8,128)} %collective-permute-done.5, f32[2048,128]{1,0:T(8,128)S(1)} %bitcast.13, pred[]{:T(512)S(6)} %eq.91, pred[]{:T(512)S(6)} %eq.90), kind=kLoop, calls=%fused_computation.1 | loop fusion | flops 524288 | bytes 4194306 | tf_op jit(solution)/shard_map/jit(_where)/select_n | solution.py:202
  41.4 1.6 %collective-permute-start.12 = (f32[2048,128]{1,0:T(8,128)}, f32[2048,128]{1,0:T(8,128)}, u32[]{:S(2)}, u32[]{:S(2)}) collective-permute-start(f32[2048,128]{1,0:T(8,128)} %select_select_fusion.1), channel_id=1, source_target_pairs={{1,65},{2,66},{3,67},{4,68},{5,69},{6,70},{7,71},{8,72},{9,73},{10... | collective-permute-start | bytes 3145736 | tf_op jit(solution)/shard_map/ppermute | solution.py:180
  43.0 1.6 %collective-permute-start.13 = (f32[2048,128]{1,0:T(8,128)}, f32[2048,128]{1,0:T(8,128)}, u32[]{:S(2)}, u32[]{:S(2)}) collective-permute-start(f32[2048,128]{1,0:T(8,128)} %select_select_fusion.1), channel_id=1, source_target_pairs={{1,449},{2,450},{3,451},{4,452},{5,453},{6,454},{7,455},{8,456},{9... | collective-permute-start | bytes 3145736 | tf_op jit(solution)/shard_map/ppermute | solution.py:180
  44.7 1.2 fusion.1
  45.8 0.7 collective-permute-start.7
  46.5 0.7 collective-permute-start.8
  47.2 1.1 select_select_fusion.3
  48.3 1.3 collective-permute-start.10
  49.6 0.0 collective-permute-done.7
  49.6 1.5 collective-permute-start.11
  51.1 0.7 copy-done.5
  51.8 1.3 collective-permute-start.9
  53.1 1.1 select_select_fusion.8
  54.2 1.5 collective-permute-done.10
  55.7 0.7 collective-permute-start.14
  56.4 0.7 collective-permute-start.15
  57.1 2.4 %select_select_fusion = f32[2048,128]{1,0:T(8,128)} fusion(f32[2048,128]{1,0:T(8,128)} %collective-permute-done.13, f32[2048,128]{1,0:T(8,128)} %collective-permute-done.12, f32[2048,128]{1,0:T(8,128)} %select_select_fusion.1, pred[]{:T(512)S(6)} %or.29, pred[]{:T(512)S(6)} %or.27), kind=kLoop, calls=%fused_computation | loop fusion | flops 524288 | bytes 4194306 | tf_op jit(solution)/shard_map/jit(_where)/select_n | solution.py:202
  59.5 1.3 collective-permute-start.22
  60.8 0.7 collective-permute-start.16
  61.5 0.7 collective-permute-start.17
  62.2 0.1 select_select_fusion.2.own_ref
  62.3 1.9 %collective-permute-start.20 = (f32[1024,128]{1,0:T(8,128)S(1)}, f32[1024,128]{1,0:T(8,128)S(1)}, u32[]{:S(2)}, u32[]{:S(2)}) collective-permute-start(f32[1024,128]{1,0:T(8,128)S(1)} %select_select_fusion.2.own_ref), channel_id=1, source_target_pairs={{0,1},{1,2},{2,3},{3,0},{4,5},{5,6},{6,7},{7,4},{8,9},{9,10},{10,1... | collective-permute-start | bytes 1572872 | tf_op jit(solution)/shard_map/ppermute | solution.py:180
  64.2 3.7 %collective-permute-start.21 = (f32[1024,128]{1,0:T(8,128)S(1)}, f32[1024,128]{1,0:T(8,128)}, u32[]{:S(2)}, u32[]{:S(2)}) collective-permute-start(f32[1024,128]{1,0:T(8,128)S(1)} %select_select_fusion.2.own_ref), channel_id=1, source_target_pairs={{0,3},{1,0},{2,1},{3,2},{4,7},{5,4},{6,5},{7,6},{8,11},{9,8},{10,9... | collective-permute-start | bytes 1572872 | tf_op jit(solution)/shard_map/ppermute | solution.py:180
  68.0 0.7 collective-permute-start.18
  68.7 1.3 collective-permute-start.19
  70.0 2.5 %collective-permute-done.20.left_ref = f32[1024,128]{1,0:T(8,128)S(1)} collective-permute-done((f32[1024,128]{1,0:T(8,128)S(1)}, f32[1024,128]{1,0:T(8,128)S(1)}, u32[]{:S(2)}, u32[]{:S(2)}) %collective-permute-start.20) | collective-permute-done | bytes 524320 | tf_op jit(solution)/shard_map/ppermute | solution.py:180
  72.5 5.6 %collective-permute-done.21.right_ref = f32[1024,128]{1,0:T(8,128)} collective-permute-done((f32[1024,128]{1,0:T(8,128)S(1)}, f32[1024,128]{1,0:T(8,128)}, u32[]{:S(2)}, u32[]{:S(2)}) %collective-permute-start.21) | collective-permute-done | bytes 524320 | tf_op jit(solution)/shard_map/ppermute | solution.py:180
  78.1 6.6 %collective-permute-done.22 = f32[2048,128]{1,0:T(8,128)} collective-permute-done((f32[2048,128]{1,0:T(8,128)}, f32[2048,128]{1,0:T(8,128)}, u32[]{:S(2)}, u32[]{:S(2)}) %collective-permute-start.22) | collective-permute-done | bytes 1048608 | tf_op jit(solution)/shard_map/ppermute | solution.py:180
  84.7 0.7 collective-permute-start.23
  85.4 0.7 collective-permute-start.24
  86.1 6.0 %collective-permute-start.25 = (f32[512,128]{1,0:T(8,128)S(1)}, f32[512,128]{1,0:T(8,128)S(1)}, u32[]{:S(2)}, u32[]{:S(2)}) collective-permute-start(f32[512,128]{1,0:T(8,128)S(1)} %slice.47), channel_id=1, source_target_pairs={{0,1},{1,2},{2,3},{3,0},{4,5},{5,6},{6,7},{7,4},{8,9},{9,10},{10,1... | collective-permute-start | bytes 786440 | tf_op jit(solution)/shard_map/ppermute | solution.py:180
  92.1 1.0 slice.48
  93.1 2.4 %collective-permute-start.26 = (f32[512,128]{1,0:T(8,128)S(1)}, f32[512,128]{1,0:T(8,128)S(1)}, u32[]{:S(2)}, u32[]{:S(2)}) collective-permute-start(f32[512,128]{1,0:T(8,128)S(1)} %slice.48), channel_id=1, source_target_pairs={{0,3},{1,0},{2,1},{3,2},{4,7},{5,4},{6,5},{7,6},{8,11},{9,8},{10,9... | collective-permute-start | bytes 786440 | tf_op jit(solution)/shard_map/ppermute | solution.py:180
  95.5 1.3 broadcast_select_fusion.b_ref
  96.9 2.6 %collective-permute-done.25.opp_a_ref = f32[512,128]{1,0:T(8,128)S(1)} collective-permute-done((f32[512,128]{1,0:T(8,128)S(1)}, f32[512,128]{1,0:T(8,128)S(1)}, u32[]{:S(2)}, u32[]{:S(2)}) %collective-permute-start.25) | collective-permute-done | bytes 262176 | tf_op jit(solution)/shard_map/ppermute | solution.py:180
  99.5 3.8 %collective-permute-done.26.opp_b_ref = f32[512,128]{1,0:T(8,128)S(1)} collective-permute-done((f32[512,128]{1,0:T(8,128)S(1)}, f32[512,128]{1,0:T(8,128)S(1)}, u32[]{:S(2)}, u32[]{:S(2)}) %collective-permute-start.26) | collective-permute-done | bytes 262176 | tf_op jit(solution)/shard_map/ppermute | solution.py:180
  103.3 0.7 collective-permute-start.27
  104.0 0.7 collective-permute-start.28
  104.7 0.7 collective-permute-start.29
  105.5 1.3 collective-permute-start.30
  106.8 0.1 pad_add_fusion.pos_ref
  106.8 34.0 %collective-permute-done.30 = f32[1536,128]{1,0:T(8,128)S(1)} collective-permute-done((f32[1536,128]{1,0:T(8,128)S(1)}, f32[1536,128]{1,0:T(8,128)S(1)}, u32[]{:S(2)}, u32[]{:S(2)}) %collective-permute-start.30) | collective-permute-done | bytes 786464 | tf_op jit(solution)/shard_map/ppermute | solution.py:180
  140.9 0.1 broadcast_select_fusion.1.f_ref
  141.0 13.3 %update.1 = f32[4096,128]{1,0:T(8,128)} custom-call(s32[4]{0:T(128)S(1)} %pad_add_fusion.pos_ref, f32[1024,128]{1,0:T(8,128)S(1)} %select_select_fusion.2.own_ref, f32[1024,128]{1,0:T(8,128)S(1)} %collective-permute-done.20.left_ref, f32[1024,128]{1,0:T(8,128)} %collective-permute-done.21.right_ref, f32[512,128]{1,0:T(8,128)S(1)} %collective-permute-done.25.opp_a_ref, ...), custom_call_target="tpu_custom_call" | custom-call | flops 8000000000 | bytes 9000000 | tf_op jit(solution)/shard_map/update/pallas_call | solution.py:167
  (34 shorter events, 0.3 us)
Async XLA Ops:
  0.0 6.9 %copy-start = (f32[2,512,1,512]{3,2,1,0:T(1,128)S(1)}, f32[2,512,1,512]{3,2,1,0:T(1,128)}, u32[]{:S(2)}) copy-start(f32[2,512,1,512]{3,2,1,0:T(1,128)} %param.1) | copy-start | bytes 6291460
  2.7 7.1 %collective-permute-start = (f32[1024,128]{1,0:T(8,128)}, f32[1024,128]{1,0:T(8,128)}, u32[]{:S(2)}, u32[]{:S(2)}) collective-permute-start(f32[1024,128]{1,0:T(8,128)} %get-tuple-element.61), channel_id=1, source_target_pairs={{0,3},{32,35},{64,67},{96,99},{128,131},{160,163},{192,195},{224,2... | collective-permute-start | bytes 1572872 | tf_op jit(solution)/shard_map/ppermute | solution.py:180
  4.1 16.9 %collective-permute-start.1 = (f32[1024,128]{1,0:T(8,128)}, f32[1024,128]{1,0:T(8,128)}, u32[]{:S(2)}, u32[]{:S(2)}) collective-permute-start(f32[1024,128]{1,0:T(8,128)} %get-tuple-element.60), channel_id=1, source_target_pairs={{0,2},{32,34},{64,66},{96,98},{128,130},{160,162},{192,194},{224,2... | collective-permute-start | bytes 1572872 | tf_op jit(solution)/shard_map/ppermute | solution.py:180
  5.4 15.6 %collective-permute-start.2 = (f32[1024,128]{1,0:T(8,128)}, f32[1024,128]{1,0:T(8,128)}, u32[]{:S(2)}, u32[]{:S(2)}) collective-permute-start(f32[1024,128]{1,0:T(8,128)} %get-tuple-element.59), channel_id=1, source_target_pairs={{32,33},{64,65},{96,97},{128,129},{160,161},{192,193},{224,225},{2... | collective-permute-start | bytes 1572872 | tf_op jit(solution)/shard_map/ppermute | solution.py:180
  7.9 0.9 copy-start.1
  8.8 1.0 copy-start.2
  21.0 18.0 %collective-permute-start.5 = (f32[2048,128]{1,0:T(8,128)S(1)}, f32[2048,128]{1,0:T(8,128)}, u32[]{:S(2)}, u32[]{:S(2)}) collective-permute-start(f32[2048,128]{1,0:T(8,128)S(1)} %bitcast.11), channel_id=1, source_target_pairs={{1,193},{2,194},{3,195},{4,196},{5,197},{6,198},{7,199},{8,200},{9... | collective-permute-start | bytes 3145736 | tf_op jit(solution)/shard_map/ppermute | solution.py:180
  22.6 16.4 %collective-permute-start.6 = (f32[2048,128]{1,0:T(8,128)S(1)}, f32[2048,128]{1,0:T(8,128)}, u32[]{:S(2)}, u32[]{:S(2)}) collective-permute-start(f32[2048,128]{1,0:T(8,128)S(1)} %bitcast.12), channel_id=1, source_target_pairs={{1,321},{2,322},{3,323},{4,324},{5,325},{6,326},{7,327},{8,328},{9... | collective-permute-start | bytes 3145736 | tf_op jit(solution)/shard_map/ppermute | solution.py:180
  26.2 10.7 %collective-permute-start.3 = (f32[1024,128]{1,0:T(8,128)}, f32[1024,128]{1,0:T(8,128)}, u32[]{:S(2)}, u32[]{:S(2)}) collective-permute-start(f32[1024,128]{1,0:T(8,128)} %slice_select_fusion), channel_id=1, source_target_pairs={{2,14},{3,15},{34,46},{35,47},{66,78},{67,79},{98,110},{99,111},{1... | collective-permute-start | bytes 1572872 | tf_op jit(solution)/shard_map/ppermute | solution.py:180
  28.3 10.7 %collective-permute-start.4 = (f32[1024,128]{1,0:T(8,128)}, f32[1024,128]{1,0:T(8,128)}, u32[]{:S(2)}, u32[]{:S(2)}) collective-permute-start(f32[1024,128]{1,0:T(8,128)} %slice_select_fusion), channel_id=1, source_target_pairs={{130,150},{131,151},{162,182},{163,183},{194,214},{195,215},{226,2... | collective-permute-start | bytes 1572872 | tf_op jit(solution)/shard_map/ppermute | solution.py:180
  41.4 14.3 %collective-permute-start.12 = (f32[2048,128]{1,0:T(8,128)}, f32[2048,128]{1,0:T(8,128)}, u32[]{:S(2)}, u32[]{:S(2)}) collective-permute-start(f32[2048,128]{1,0:T(8,128)} %select_select_fusion.1), channel_id=1, source_target_pairs={{1,65},{2,66},{3,67},{4,68},{5,69},{6,70},{7,71},{8,72},{9,73},{10... | collective-permute-start | bytes 3145736 | tf_op jit(solution)/shard_map/ppermute | solution.py:180
  43.0 12.7 %collective-permute-start.13 = (f32[2048,128]{1,0:T(8,128)}, f32[2048,128]{1,0:T(8,128)}, u32[]{:S(2)}, u32[]{:S(2)}) collective-permute-start(f32[2048,128]{1,0:T(8,128)} %select_select_fusion.1), channel_id=1, source_target_pairs={{1,449},{2,450},{3,451},{4,452},{5,453},{6,454},{7,455},{8,456},{9... | collective-permute-start | bytes 3145736 | tf_op jit(solution)/shard_map/ppermute | solution.py:180
  45.8 3.8 %collective-permute-start.7 = (f32[384,128]{1,0:T(8,128)S(1)}, f32[384,128]{1,0:T(8,128)S(1)}, u32[]{:S(2)}, u32[]{:S(2)}) collective-permute-start(f32[384,128]{1,0:T(8,128)S(1)} %get-tuple-element.64), channel_id=1, source_target_pairs={{0,1}} | collective-permute-start | bytes 589832 | tf_op jit(solution)/shard_map/ppermute | solution.py:180
  46.5 4.6 %collective-permute-start.8 = (f32[384,128]{1,0:T(8,128)S(1)}, f32[384,128]{1,0:T(8,128)S(1)}, u32[]{:S(2)}, u32[]{:S(2)}) collective-permute-start(f32[384,128]{1,0:T(8,128)S(1)} %get-tuple-element.63), channel_id=1, source_target_pairs={{0,2}} | collective-permute-start | bytes 589832 | tf_op jit(solution)/shard_map/ppermute | solution.py:180
  48.3 7.4 %collective-permute-start.10 = (f32[1024,128]{1,0:T(8,128)S(1)}, f32[1024,128]{1,0:T(8,128)S(1)}, u32[]{:S(2)}, u32[]{:S(2)}) collective-permute-start(f32[1024,128]{1,0:T(8,128)S(1)} %select_select_fusion.3), channel_id=1, source_target_pairs={{2,6},{3,7},{34,38},{35,39},{66,70},{67,71},{98,102},{99,103},{128... | collective-permute-start | bytes 1572872 | tf_op jit(solution)/shard_map/ppermute | solution.py:180
  49.6 6.1 %collective-permute-start.11 = (f32[1024,128]{1,0:T(8,128)S(1)}, f32[1024,128]{1,0:T(8,128)}, u32[]{:S(2)}, u32[]{:S(2)}) collective-permute-start(f32[1024,128]{1,0:T(8,128)S(1)} %select_select_fusion.3), channel_id=1, source_target_pairs={{386,414},{387,415},{418,446},{419,447},{450,478},{451,479},{482,5... | collective-permute-start | bytes 1572872 | tf_op jit(solution)/shard_map/ppermute | solution.py:180
  51.1 0.7 copy-start.5
  51.8 1.3 collective-permute-start.9
  55.7 3.7 %copy-start.4 = (f32[1024,128]{1,0:T(8,128)}, f32[1024,128]{1,0:T(8,128)S(1)}, u32[]{:S(2)}) copy-start(f32[1024,128]{1,0:T(8,128)S(1)} %collective-permute-done.10) | copy-start | bytes 1572868
  55.7 3.7 %collective-permute-start.14 = (f32[384,128]{1,0:T(8,128)S(1)}, f32[384,128]{1,0:T(8,128)S(1)}, u32[]{:S(2)}, u32[]{:S(2)}) collective-permute-start(f32[384,128]{1,0:T(8,128)S(1)} %select_select_fusion.8), channel_id=1, source_target_pairs={{0,320},{1,321},{2,322},{3,323}} | collective-permute-start | bytes 589832 | tf_op jit(solution)/shard_map/ppermute | solution.py:180
  56.4 3.0 %collective-permute-start.15 = (f32[384,128]{1,0:T(8,128)S(1)}, f32[384,128]{1,0:T(8,128)S(1)}, u32[]{:S(2)}, u32[]{:S(2)}) collective-permute-start(f32[384,128]{1,0:T(8,128)S(1)} %select_select_fusion.8), channel_id=1, source_target_pairs={{0,192},{1,193},{2,194},{3,195}} | collective-permute-start | bytes 589832 | tf_op jit(solution)/shard_map/ppermute | solution.py:180
  59.5 25.2 %collective-permute-start.22 = (f32[2048,128]{1,0:T(8,128)}, f32[2048,128]{1,0:T(8,128)}, u32[]{:S(2)}, u32[]{:S(2)}) collective-permute-start(f32[2048,128]{1,0:T(8,128)} %select_select_fusion), channel_id=1, source_target_pairs={{0,32},{1,33},{2,34},{3,35},{4,36},{5,37},{6,38},{7,39},{8,40},{9,... | collective-permute-start | bytes 3145736 | tf_op jit(solution)/shard_map/ppermute | solution.py:180
  60.8 7.1 %collective-permute-start.16 = (f32[384,128]{1,0:T(8,128)S(1)}, f32[384,128]{1,0:T(8,128)S(1)}, u32[]{:S(2)}, u32[]{:S(2)}) collective-permute-start(f32[384,128]{1,0:T(8,128)S(1)} %select_select_fusion.7), channel_id=1, source_target_pairs={{0,448},{1,449},{2,450},{3,451},{192,128},{193,129},{194,130},{195... | collective-permute-start | bytes 589832 | tf_op jit(solution)/shard_map/ppermute | solution.py:180
  61.5 6.4 %collective-permute-start.17 = (f32[384,128]{1,0:T(8,128)S(1)}, f32[384,128]{1,0:T(8,128)S(1)}, u32[]{:S(2)}, u32[]{:S(2)}) collective-permute-start(f32[384,128]{1,0:T(8,128)S(1)} %select_select_fusion.7), channel_id=1, source_target_pairs={{0,64},{1,65},{2,66},{3,67},{192,256},{193,257},{194,258},{195,259... | collective-permute-start | bytes 589832 | tf_op jit(solution)/shard_map/ppermute | solution.py:180
  62.3 10.3 %collective-permute-start.20 = (f32[1024,128]{1,0:T(8,128)S(1)}, f32[1024,128]{1,0:T(8,128)S(1)}, u32[]{:S(2)}, u32[]{:S(2)}) collective-permute-start(f32[1024,128]{1,0:T(8,128)S(1)} %select_select_fusion.2.own_ref), channel_id=1, source_target_pairs={{0,1},{1,2},{2,3},{3,0},{4,5},{5,6},{6,7},{7,4},{8,9},{9,10},{10,1... | collective-permute-start | bytes 1572872 | tf_op jit(solution)/shard_map/ppermute | solution.py:180
  64.2 13.9 %collective-permute-start.21 = (f32[1024,128]{1,0:T(8,128)S(1)}, f32[1024,128]{1,0:T(8,128)}, u32[]{:S(2)}, u32[]{:S(2)}) collective-permute-start(f32[1024,128]{1,0:T(8,128)S(1)} %select_select_fusion.2.own_ref), channel_id=1, source_target_pairs={{0,3},{1,0},{2,1},{3,2},{4,7},{5,4},{6,5},{7,6},{8,11},{9,8},{10,9... | collective-permute-start | bytes 1572872 | tf_op jit(solution)/shard_map/ppermute | solution.py:180
  68.0 2.0 %collective-permute-start.18 = (f32[384,128]{1,0:T(8,128)S(1)}, f32[384,128]{1,0:T(8,128)S(1)}, u32[]{:S(2)}, u32[]{:S(2)}) collective-permute-start(f32[384,128]{1,0:T(8,128)S(1)} %select_select_fusion.6), channel_id=1, source_target_pairs={{0,20},{1,21},{2,22},{3,23},{64,84},{65,85},{66,86},{67,87},{128,1... | collective-permute-start | bytes 589832 | tf_op jit(solution)/shard_map/ppermute | solution.py:180
  68.7 1.3 collective-permute-start.19
  84.7 12.2 %collective-permute-start.23 = (f32[384,128]{1,0:T(8,128)S(1)}, f32[384,128]{1,0:T(8,128)S(1)}, u32[]{:S(2)}, u32[]{:S(2)}) collective-permute-start(f32[384,128]{1,0:T(8,128)S(1)} %select_select_fusion.5), channel_id=1, source_target_pairs={{0,28},{1,29},{2,30},{3,31},{64,92},{65,93},{66,94},{67,95},{128,1... | collective-permute-start | bytes 589832 | tf_op jit(solution)/shard_map/ppermute | solution.py:180
  85.4 11.5 %collective-permute-start.24 = (f32[384,128]{1,0:T(8,128)S(1)}, f32[384,128]{1,0:T(8,128)S(1)}, u32[]{:S(2)}, u32[]{:S(2)}) collective-permute-start(f32[384,128]{1,0:T(8,128)S(1)} %select_select_fusion.5), channel_id=1, source_target_pairs={{0,4},{1,5},{2,6},{3,7},{64,68},{65,69},{66,70},{67,71},{128,132},... | collective-permute-start | bytes 589832 | tf_op jit(solution)/shard_map/ppermute | solution.py:180
  86.1 13.5 %collective-permute-start.25 = (f32[512,128]{1,0:T(8,128)S(1)}, f32[512,128]{1,0:T(8,128)S(1)}, u32[]{:S(2)}, u32[]{:S(2)}) collective-permute-start(f32[512,128]{1,0:T(8,128)S(1)} %slice.47), channel_id=1, source_target_pairs={{0,1},{1,2},{2,3},{3,0},{4,5},{5,6},{6,7},{7,4},{8,9},{9,10},{10,1... | collective-permute-start | bytes 786440 | tf_op jit(solution)/shard_map/ppermute | solution.py:180
  93.1 10.2 %collective-permute-start.26 = (f32[512,128]{1,0:T(8,128)S(1)}, f32[512,128]{1,0:T(8,128)S(1)}, u32[]{:S(2)}, u32[]{:S(2)}) collective-permute-start(f32[512,128]{1,0:T(8,128)S(1)} %slice.48), channel_id=1, source_target_pairs={{0,3},{1,0},{2,1},{3,2},{4,7},{5,4},{6,5},{7,6},{8,11},{9,8},{10,9... | collective-permute-start | bytes 786440 | tf_op jit(solution)/shard_map/ppermute | solution.py:180
  96.9 44.0 %copy-start.3 = (f32[2048,128]{1,0:T(8,128)S(1)}, f32[2048,128]{1,0:T(8,128)}, u32[]{:S(2)}) copy-start(f32[2048,128]{1,0:T(8,128)} %copy-done.2) | copy-start | bytes 3145732
  103.3 2.1 %collective-permute-start.27 = (f32[384,128]{1,0:T(8,128)S(1)}, f32[384,128]{1,0:T(8,128)S(1)}, u32[]{:S(2)}, u32[]{:S(2)}) collective-permute-start(f32[384,128]{1,0:T(8,128)S(1)} %select_select_fusion.4), channel_id=1, source_target_pairs={{0,3},{1,0},{2,1},{3,2},{4,7},{5,4},{6,5},{7,6},{8,11},{9,8},{10,9... | collective-permute-start | bytes 589832 | tf_op jit(solution)/shard_map/ppermute | solution.py:180
  104.0 1.4 collective-permute-start.28
  104.7 0.8 collective-permute-start.29
  105.5 35.4 %collective-permute-start.30 = (f32[1536,128]{1,0:T(8,128)S(1)}, f32[1536,128]{1,0:T(8,128)S(1)}, u32[]{:S(2)}, u32[]{:S(2)}) collective-permute-start(f32[1536,128]{1,0:T(8,128)S(1)} %constant_dynamic-update-slice_fusion), channel_id=1, source_target_pairs={{0,32},{1,33},{2,34},{3,35},{4,36},{5,37},{6,38},{7,39},{8,40},{9,... | collective-permute-start | bytes 2359304 | tf_op jit(solution)/shard_map/ppermute | solution.py:180

commit v3 on v2

--- a/solution.py
+++ b/solution.py
@@ -8,6 +8,7 @@
 AXES = ("row", "col")
 ROWS, COLS = 16, 32
 NZ, NX = 8, 4
+HOME_ROW, HOME_Z = 1, 7
 TB = 512
 SB = 128
 HB = 256
@@ -30,14 +31,14 @@
     sub = lax.broadcasted_iota(jnp.int32, (8, SB), 0)
     s = [block[8 * t : 8 * t + 8, :] for t in range(tiles)]
     e = [jnp.where(lane == sub + 8 * t, 1.0, 0.0).astype(jnp.float32) for t in range(tiles)]
-    upper, inverse = [], []
+    inverse = []
     for b in range(tiles):
         cols = [
             [jnp.broadcast_to(s[t][:, 8 * b + m : 8 * b + m + 1], (8, SB)) for t in range(b, tiles)]
             for m in range(8)
         ]
         top, top_e = s[b], e[b]
-        out_u, out_e = jnp.zeros_like(top), jnp.zeros_like(top)
+        out_e = jnp.zeros_like(top)
         done = []
         for m in range(8):
             d = jnp.broadcast_to(cols[m][0][m : m + 1, :], (8, SB))
@@ -46,7 +47,6 @@
             lc = [c * r for c in cols[m]]
             ur = jnp.broadcast_to(top[m : m + 1, :], (8, SB)) * r
             er = jnp.broadcast_to(top_e[m : m + 1, :], (8, SB)) * r
-            out_u = jnp.where(sub == m, ur, out_u)
             out_e = jnp.where(sub == m, er, out_e)
             for k in range(m + 1, 8):
                 f = jnp.broadcast_to(lc[0][k : k + 1, :], (8, SB))
@@ -59,9 +59,8 @@
             for lc, ur, er in done:
                 s[t] = s[t] - lc[t - b] * ur
                 e[t] = e[t] - lc[t - b] * er
-        upper.append(jnp.where(lane >= sub + 8 * b, out_u, 0.0))
         inverse.append(out_e)
-    return jnp.concatenate(upper, axis=0), jnp.concatenate(inverse, axis=0)
+    return jnp.concatenate(inverse, axis=0)
 
 
 def wide(ref, first, rows, lo=0, hi=4):
@@ -73,7 +72,7 @@
         ref[pl.ds(4 * first + i, value.shape[0], stride=4), :] = value[:, i * SB : (i + 1) * SB]
 
 
-def factor_kernel(flag_ref, a_ref, low_ref, f_ref, w_ref):
+def factor_kernel(flag_ref, a_ref, f_ref, w_ref):
     @pl.when(flag_ref[0] == 1)
     def _():
         def slot(i):
@@ -82,33 +81,27 @@
         w_ref[...] = wide(a_ref, 0, TB)
         for k in range(4):
             lo, hi = k * SB, (k + 1) * SB
-            u, inv = factor_block(w_ref[lo:hi, lo:hi])
+            inv = factor_block(w_ref[lo:hi, lo:hi])
             f_ref[slot((M0, M1, M2, M3)[k]), :] = inv
-            w_ref[lo:hi, lo:hi] = u.T
             if hi < TB:
                 below = nt(w_ref[hi:, lo:hi], inv)
                 w_ref[hi:, hi:] = w_ref[hi:, hi:] - nt(below, below)
                 w_ref[hi:, lo:hi] = below
-                w_ref[lo:hi, hi:] = jnp.zeros((SB, TB - hi), jnp.float32)
                 if k < 2:
                     f_ref[slot((L20, L21)[k]), :] = below[2 * SB - hi : 3 * SB - hi]
                     f_ref[slot((L30, L31)[k]), :] = below[3 * SB - hi : 4 * SB - hi]
             if k % 2 == 1:
                 prev = f_ref[slot((M0, M2)[k // 2]), :]
                 f_ref[slot((X10, X32)[k // 2]), :] = -nn(inv, nn(w_ref[lo:hi, lo - SB : lo], prev))
-        put_wide(low_ref, 0, w_ref[...])
 
 
 def factor_tile(flag, a):
     vmem = pl.BlockSpec(memory_space=pltpu.VMEM)
     return pl.pallas_call(
         factor_kernel,
-        out_shape=(
-            jax.ShapeDtypeStruct((4 * TB, SB), jnp.float32),
-            jax.ShapeDtypeStruct((SLOTS * SB, SB), jnp.float32),
-        ),
+        out_shape=jax.ShapeDtypeStruct((SLOTS * SB, SB), jnp.float32),
         in_specs=[pl.BlockSpec(memory_space=pltpu.SMEM), vmem],
-        out_specs=(vmem, vmem),
+        out_specs=vmem,
         scratch_shapes=[pltpu.VMEM((TB, TB), jnp.float32)],
         cost_estimate=pl.CostEstimate(flops=20_000_000_000, bytes_accessed=3_000_000, transcendentals=0),
         compiler_params=pltpu.CompilerParams(vmem_limit_bytes=24 * 1024 * 1024),
@@ -116,7 +109,7 @@
     )(flag, a)
 
 
-def update_kernel(pos_ref, own_ref, left_ref, right_ref, opp_a_ref, opp_b_ref, b_ref, f_ref, low_ref, cov_ref, out_ref, y_ref):
+def update_kernel(pos_ref, own_ref, left_ref, right_ref, opp_a_ref, opp_b_ref, b_ref, f_ref, cov_ref, out_ref, y_ref):
     row, col, x = pos_ref[0], pos_ref[1], pos_ref[2]
 
     def block(i):
@@ -151,8 +144,9 @@
 
         @pl.when(col == 0)
         def _():
-            low = wide(low_ref, lax.rem(q, 2) * HB, HB)
-            put_wide(out_ref, q * HB, jnp.where(tile_row == 0, low, xs))
+            at_row = lax.rem(q, 2) * HB + lax.broadcasted_iota(jnp.int32, (HB, TB), 0)
+            above = lax.broadcasted_iota(jnp.int32, (HB, TB), 1) > at_row
+            put_wide(out_ref, q * HB, jnp.where(jnp.logical_and(tile_row == 0, above), 0.0, xs))
 
     for shift, ref in ((0, own_ref), (3, left_ref), (1, right_ref)):
         piece(lax.rem(x + shift, 4), wide(ref, 0, HB, 0, 2), wide(ref, 0, HB, 2, 4))
@@ -162,18 +156,18 @@
     piece(lax.rem(x + 2, 4), opp0, opp1)
 
 
-def update(pos, own, left, right, opp_a, opp_b, b, f, low, cov):
+def update(pos, own, left, right, opp_a, opp_b, b, f, cov):
     vmem = pl.BlockSpec(memory_space=pltpu.VMEM)
     return pl.pallas_call(
         update_kernel,
         out_shape=jax.ShapeDtypeStruct((8 * TB, SB), jnp.float32),
-        in_specs=[pl.BlockSpec(memory_space=pltpu.SMEM)] + [vmem] * 9,
+        in_specs=[pl.BlockSpec(memory_space=pltpu.SMEM)] + [vmem] * 8,
         out_specs=vmem,
         scratch_shapes=[pltpu.VMEM((TB, TB), jnp.float32)],
         cost_estimate=pl.CostEstimate(flops=8_000_000_000, bytes_accessed=9_000_000, transcendentals=0),
         compiler_params=pltpu.CompilerParams(vmem_limit_bytes=40 * 1024 * 1024),
         name="update",
-    )(pos, own, left, right, opp_a, opp_b, b, f, low, cov)
+    )(pos, own, left, right, opp_a, opp_b, b, f, cov)
 
 
 def send(value, pairs):
@@ -224,8 +218,7 @@
     y, core = row // 2, row % 2
     z, x = col // NX, col % NX
     cov = covariance.reshape(8 * TB, SB)
-    is_root = jnp.logical_and(row == 0, col == 0)
-    flag = is_root.astype(jnp.int32).reshape(1)
+    flag = jnp.logical_and(row == HOME_ROW, col == HOME_Z * NX).astype(jnp.int32).reshape(1)
     rows = range(ROWS)
     quarter_rows = HB * 4
 
@@ -236,7 +229,7 @@
         return lax.optimization_barrier(values)
 
     def scatter(q):
-        return [(at(i, 0, 0), at(i, 0, q)) for i in rows if last_col(i, q) > 0]
+        return [(at(i, 0, 0), at(i, 0, q)) for i in rows]
 
     def along_z(a, b):
         return [(at(i, a, j), at(i, b, j)) for i in rows for j in range(NX) if last_col(i, j) > 0 and reaches(b, last_col(i, j))]
@@ -257,56 +250,58 @@
     across = [(at(i, k, j), at(i + 1, k, j)) for i in rows[::2] for k in range(NZ) for j in range(NX)]
 
     def factor_y(a, b):
-        return [(at(2 * a, 0, j), at(2 * b, 0, j)) for j in range(NX)]
+        return [(at(2 * a + 1, HOME_Z, j), at(2 * b + 1, HOME_Z, j)) for j in range(NX)]
 
     def factor_z(a, b):
-        return [(at(i, a, j), at(i, b, j)) for i in rows[::2] for j in range(NX)]
+        return [(at(i, (a + HOME_Z) % NZ, j), at(i, (b + HOME_Z) % NZ, j)) for i in rows[1::2] for j in range(NX)]
+
+    home = at(HOME_ROW, HOME_Z, 0)
+    home_z = (z - HOME_Z + NZ) % NZ
 
     def by_x(values):
         return jnp.where(x == 0, values[0], jnp.where(x == 1, values[1], jnp.where(x == 2, values[2], values[3])))
 
+    b_tile = cov[0 : 4 * TB]
+    corner = send(b_tile, [(0, home)])
     quarter = [cov[quarter_rows * q : quarter_rows * (q + 1)] for q in range(4)]
     got = [send(quarter[q], scatter(q)) for q in (3, 2, 1)]
-    low, f = factor_tile(flag, cov[0 : 4 * TB])
-
-    got, f, b_tile = tied(got, f, cov[0 : 4 * TB])
+    moved = ring_sends(b_tile, ROUNDS[0], along_y)
+    corner, got = tied(corner, got)
     own = by_x([quarter[0], got[2], got[1], got[0]])
-    moved = ring_sends(b_tile, ROUNDS[0], along_y)
     got = ring_sends(own, ROUNDS[0], along_z)
 
-    f, got, moved = tied(f, got, moved)
+    corner, got, moved = tied(corner, got, moved)
     own = ring_pick(own, ROUNDS[0], z, got)
+    got = ring_sends(own, ROUNDS[1], along_z)
     b_tile = ring_pick(b_tile, ROUNDS[0], y, moved)
-    got = ring_sends(own, ROUNDS[1], along_z)
     moved = ring_sends(b_tile, ROUNDS[1], along_y)
+    f = factor_tile(flag, corner)
 
     part = [f[3 * SB * q : 3 * SB * (q + 1)] for q in range(4)]
-    given = [send(part[q], [(0, q)]) for q in (1, 2, 3)]
-    mine = by_x([part[0]] + given)
-
-    mine, got, moved = tied(mine, got, moved)
+    mine = by_x([part[0]] + [send(part[q], [(home, home + q)]) for q in (1, 2, 3)])
+    mine = ring_round(mine, ROUNDS[0], y, factor_y)
+    mine = ring_round(mine, ROUNDS[1], y, factor_y)
+
+    mine, got = tied(mine, got)
     own = ring_pick(own, ROUNDS[1], z, got)
-    b_tile = ring_pick(b_tile, ROUNDS[1], y, moved)
     left = send(own, shift_x(1, (0, 1)))
     right = send(own, shift_x(-1, (0, 1)))
-    mine = ring_round(mine, ROUNDS[0], y, factor_y)
-    mine, b_tile = tied(mine, b_tile)
-    b_other = send(b_tile, across)
-    mine = ring_round(mine, ROUNDS[1], y, factor_y)
-    mine = ring_round(mine, ROUNDS[0], z, factor_z)
-
-    mine, left, right, b_other = tied(mine, left, right, b_other)
-    b_tile = jnp.where(core == 1, b_other, b_tile)
+    mine = ring_round(mine, ROUNDS[0], home_z, factor_z)
+
+    mine, left, right, moved = tied(mine, left, right, moved)
+    b_tile = ring_pick(b_tile, ROUNDS[1], y, moved)
     opp_a = send(left[: quarter_rows // 2], shift_x(1, (0, 1)))
     opp_b = send(right[quarter_rows // 2 :], shift_x(-1, (0, 1)))
-    mine = ring_round(mine, ROUNDS[1], z, factor_z)
-
-    mine, opp_a, opp_b, b_tile = tied(mine, opp_a, opp_b, b_tile)
-    turned = jnp.concatenate([mine] + [send(mine, shift_x(-by, (0,))) for by in (1, 2, 3)], axis=0)
-    turned = jnp.where(core == 1, send(turned, across), turned)
+    b_other = send(b_tile, across)
+    mine = ring_round(mine, ROUNDS[1], home_z, factor_z)
+
+    mine, opp_a, opp_b, b_other = tied(mine, opp_a, opp_b, b_other)
+    b_tile = jnp.where(core == 1, b_other, b_tile)
+    turned = jnp.concatenate([mine] + [send(mine, shift_x(-by, (1,))) for by in (1, 2, 3)], axis=0)
+    turned = jnp.where(core == 0, send(turned, [(b, a) for a, b in across]), turned)
 
     pos = jnp.stack([row, col, x, 0]).astype(jnp.int32)
-    out = update(pos, own, left, right, opp_a, opp_b, b_tile, turned, low, cov)
+    out = update(pos, own, left, right, opp_a, opp_b, b_tile, turned, cov)
     return out.reshape(covariance.shape)
 
 

time: 155 us -> 152 us (0.981)
  the two profiles are of different devices: /device:TPU:29 before, /device:TPU:185 now
where the time goes in v3:
time: 152 us; the launch traced here: 151 us
  starting transfers between devices  56.1 us (37%)
  waiting for transfers between devices  54.7 us (36%)
  other arithmetic  15.9 us (10%)
  Pallas kernels  13.3 us (9%)
  local copies, waits for them, and re-layouts  10.6 us (7%)
    ppermute x32, starting transfers between devices, send(): return lax.ppermute(value, AXES, pairs)  56.1 us
    ppermute x32, waiting for transfers between devices, send(): return lax.ppermute(value, AXES, pairs)  54.7 us
    pallas_call x1, Pallas kernels, update(): pl.pallas_call(update_kernel, out_shape=jax.ShapeDtypeStruct((8 * TB, SB)...  13.3 us
    select_n x8, other arithmetic, ring_pick(): value = jnp.where(one_of(pos, [b for _, b in pairs]), received, value)  9.95 us
    unnamed x9, local copies, waits for them, and re-layouts  3.31 us
    select_n x2, other arithmetic, by_x(): jnp.where(x == 0, values[0], jnp.where(x == 1, values[1], jnp.where(x ==...  3.3 us
    slice x1, local copies, waits for them, and re-layouts, on_device(): b_tile = cov[0:4 * TB]  3.06 us
  transfers between devices with their start and end apart: 32, of which 6 were waited for; matrix products, arithmetic and copies ran while one was open for 11% of the time, Pallas kernels for 0%

profile of v3, /device:TPU:185, one launch (start us, length us, event | category | flops | bytes accessed | tf_op | source)
XLA Modules:
  0.0 150.9 jit_solution(11671006071109909294)
XLA Ops:
  0.0 3.1 %slice.36 = f32[1,512,1,512]{3,2,1,0:T(1,128)} slice(f32[2,512,1,512]{3,2,1,0:T(1,128)} %param.1), slice={[0:1], [0:512], [0:1], [0:512]} | slice | bytes 2097152 | tf_op jit(solution)/shard_map/slice | solution.py:264
  3.1 0.7 collective-permute-start
  3.8 1.1 fusion
  4.9 1.5 collective-permute-start.1
  6.4 1.5 collective-permute-start.2
  7.8 1.5 collective-permute-start.3
  9.3 1.6 %collective-permute-start.6 = (f32[2048,128]{1,0:T(8,128)}, f32[2048,128]{1,0:T(8,128)}, u32[]{:S(2)}, u32[]{:S(2)}) collective-permute-start(f32[2048,128]{1,0:T(8,128)} %bitcast.4), channel_id=1, source_target_pairs={{1,193},{2,194},{3,195},{4,196},{5,197},{6,198},{7,199},{8,200},{9... | collective-permute-start | bytes 3145736 | tf_op jit(solution)/shard_map/ppermute | solution.py:174
  10.9 1.6 %collective-permute-start.7 = (f32[2048,128]{1,0:T(8,128)}, f32[2048,128]{1,0:T(8,128)}, u32[]{:S(2)}, u32[]{:S(2)}) collective-permute-start(f32[2048,128]{1,0:T(8,128)} %bitcast.4), channel_id=1, source_target_pairs={{1,321},{2,322},{3,323},{4,324},{5,325},{6,326},{7,327},{8,328},{9... | collective-permute-start | bytes 3145736 | tf_op jit(solution)/shard_map/ppermute | solution.py:174
  12.6 0.0 collective-permute-done.3
  12.6 0.0 collective-permute-done.a_ref
  12.6 2.3 %slice_select_fusion = f32[1024,128]{1,0:T(8,128)} fusion(f32[4096,128]{1,0:T(8,128)S(1)} %bitcast.8, f32[1024,128]{1,0:T(8,128)} %collective-permute-done.3, f32[1024,128]{1,0:T(8,128)} %collective-permute-done.2, f32[1024,128]{1,0:T(8,128)} %collective-permute-done.1, pred[]{:T(512)S(6)} %eq.107, pred[]{:T(512)S(6)} %eq.106, pred[]{:T(512)S(6)} %eq.103), kind=kLoop, calls=%fused_computation.2 | loop fusion | flops 393216 | bytes 2621443 | tf_op jit(solution)/shard_map/jit(_where)/select_n | solution.py:262
  14.9 1.5 collective-permute-start.4
  16.4 1.5 collective-permute-start.5
  17.8 0.0 collective-permute-done.6
  17.8 0.0 collective-permute-done.7
  17.9 0.0 collective-permute-done.5
  17.9 1.2 copy-done.2
  19.1 1.4 collective-permute-start.8
  20.5 1.3 collective-permute-start.9
  21.8 1.3 collective-permute-start.10
  23.2 1.0 slice_select_fusion.1
  24.2 0.7 collective-permute-start.11
  24.9 0.7 collective-permute-start.12
  25.5 1.1 select_select_fusion.3
  26.7 1.5 collective-permute-start.15
  28.1 1.3 collective-permute-start.16
  29.5 0.7 collective-permute-start.13
  30.2 0.7 collective-permute-start.14
  30.8 2.4 %select_select_fusion.1 = f32[2048,128]{1,0:T(8,128)} fusion(f32[2048,128]{1,0:T(8,128)} %collective-permute-done.7, f32[2048,128]{1,0:T(8,128)} %collective-permute-done.6, f32[2048,128]{1,0:T(8,128)} %bitcast.4, pred[]{:T(512)S(6)} %eq.108, pred[]{:T(512)S(6)} %eq.102), kind=kLoop, calls=%fused_computation.1 | loop fusion | flops 524288 | bytes 4194306 | tf_op jit(solution)/shard_map/jit(_where)/select_n | solution.py:196
  33.2 1.6 %collective-permute-start.21 = (f32[2048,128]{1,0:T(8,128)}, f32[2048,128]{1,0:T(8,128)}, u32[]{:S(2)}, u32[]{:S(2)}) collective-permute-start(f32[2048,128]{1,0:T(8,128)} %select_select_fusion.1), channel_id=1, source_target_pairs={{1,65},{2,66},{3,67},{4,68},{5,69},{6,70},{7,71},{8,72},{9,73},{10... | collective-permute-start | bytes 3145736 | tf_op jit(solution)/shard_map/ppermute | solution.py:174
  34.8 1.6 %collective-permute-start.22 = (f32[2048,128]{1,0:T(8,128)}, f32[2048,128]{1,0:T(8,128)}, u32[]{:S(2)}, u32[]{:S(2)}) collective-permute-start(f32[2048,128]{1,0:T(8,128)} %select_select_fusion.1), channel_id=1, source_target_pairs={{1,449},{2,450},{3,451},{4,452},{5,453},{6,454},{7,455},{8,456},{9... | collective-permute-start | bytes 3145736 | tf_op jit(solution)/shard_map/ppermute | solution.py:174
  36.5 32.9 %collective-permute-done.16 = f32[1024,128]{1,0:T(8,128)} collective-permute-done((f32[1024,128]{1,0:T(8,128)S(1)}, f32[1024,128]{1,0:T(8,128)}, u32[]{:S(2)}, u32[]{:S(2)}) %collective-permute-start.16) | collective-permute-done | bytes 524320 | tf_op jit(solution)/shard_map/ppermute | solution.py:174
  69.4 0.7 collective-permute-start.17
  70.1 1.1 select_select_fusion.2.own_ref
  71.2 4.3 %collective-permute-start.19 = (f32[1024,128]{1,0:T(8,128)S(1)}, f32[1024,128]{1,0:T(8,128)S(1)}, u32[]{:S(2)}, u32[]{:S(2)}) collective-permute-start(f32[1024,128]{1,0:T(8,128)S(1)} %select_select_fusion.2.own_ref), channel_id=1, source_target_pairs={{0,1},{1,2},{2,3},{3,0},{4,5},{5,6},{6,7},{7,4},{8,9},{9,10},{10,1... | collective-permute-start | bytes 1572872 | tf_op jit(solution)/shard_map/ppermute | solution.py:174
  75.5 2.1 %collective-permute-start.20 = (f32[1024,128]{1,0:T(8,128)S(1)}, f32[1024,128]{1,0:T(8,128)}, u32[]{:S(2)}, u32[]{:S(2)}) collective-permute-start(f32[1024,128]{1,0:T(8,128)S(1)} %select_select_fusion.2.own_ref), channel_id=1, source_target_pairs={{0,3},{1,0},{2,1},{3,2},{4,7},{5,4},{6,5},{7,6},{8,11},{9,8},{10,9... | collective-permute-start | bytes 1572872 | tf_op jit(solution)/shard_map/ppermute | solution.py:174
  77.7 1.3 collective-permute-start.18
  79.0 14.5 %collective-permute-done.18 = f32[384,128]{1,0:T(8,128)} collective-permute-done((f32[384,128]{1,0:T(8,128)S(1)}, f32[384,128]{1,0:T(8,128)}, u32[]{:S(2)}, u32[]{:S(2)}) %collective-permute-start.18) | collective-permute-done | bytes 196640 | tf_op jit(solution)/shard_map/ppermute | solution.py:174
  93.5 1.6 %select_select_fusion.5 = f32[384,128]{1,0:T(8,128)} fusion(f32[384,128]{1,0:T(8,128)S(1)} %collective-permute-done.17, f32[384,128]{1,0:T(8,128)} %collective-permute-done.18, f32[384,128]{1,0:T(8,128)S(1)} %select_select_fusion.6, pred[]{:T(512)S(6)} %eq.118, pred[]{:T(512)S(6)} %eq.117), kind=kLoop, calls=%fused_computation.9 | loop fusion | flops 98304 | bytes 786434 | tf_op jit(solution)/shard_map/jit(_where)/select_n | solution.py:196
  95.2 2.7 %select_select_fusion = f32[2048,128]{1,0:T(8,128)} fusion(f32[2048,128]{1,0:T(8,128)} %collective-permute-done.22, f32[2048,128]{1,0:T(8,128)} %collective-permute-done.21, f32[2048,128]{1,0:T(8,128)} %select_select_fusion.1, pred[]{:T(512)S(6)} %or.33, pred[]{:T(512)S(6)} %or.31), kind=kLoop, calls=%fused_computation | loop fusion | flops 524288 | bytes 4194306 | tf_op jit(solution)/shard_map/jit(_where)/select_n | solution.py:196
  97.8 1.3 collective-permute-start.27
  99.1 2.0 %collective-permute-start.23 = (f32[384,128]{1,0:T(8,128)}, f32[384,128]{1,0:T(8,128)}, u32[]{:S(2)}, u32[]{:S(2)}) collective-permute-start(f32[384,128]{1,0:T(8,128)} %select_select_fusion.5), channel_id=1, source_target_pairs={{60,56},{61,57},{62,58},{63,59},{124,120},{125,121},{126,122},{127... | collective-permute-start | bytes 589832 | tf_op jit(solution)/shard_map/ppermute | solution.py:174
  101.1 2.0 %collective-permute-start.24 = (f32[384,128]{1,0:T(8,128)}, f32[384,128]{1,0:T(8,128)}, u32[]{:S(2)}, u32[]{:S(2)}) collective-permute-start(f32[384,128]{1,0:T(8,128)} %select_select_fusion.5), channel_id=1, source_target_pairs={{60,32},{61,33},{62,34},{63,35},{124,96},{125,97},{126,98},{127,99... | collective-permute-start | bytes 589832 | tf_op jit(solution)/shard_map/ppermute | solution.py:174
  103.1 0.7 slice.46
  103.8 1.9 %collective-permute-start.25 = (f32[512,128]{1,0:T(8,128)}, f32[512,128]{1,0:T(8,128)S(1)}, u32[]{:S(2)}, u32[]{:S(2)}) collective-permute-start(f32[512,128]{1,0:T(8,128)} %slice.46), channel_id=1, source_target_pairs={{0,1},{1,2},{2,3},{3,0},{4,5},{5,6},{6,7},{7,4},{8,9},{9,10},{10,1... | collective-permute-start | bytes 786440 | tf_op jit(solution)/shard_map/ppermute | solution.py:174
  105.7 1.7 %slice.47 = f32[512,128]{1,0:T(8,128)} slice(f32[1024,128]{1,0:T(8,128)} %collective-permute-done.20.right_ref), slice={[512:1024], [0:128]} | slice | bytes 524288 | tf_op jit(solution)/shard_map/slice | solution.py:294
  107.4 4.6 %collective-permute-start.26 = (f32[512,128]{1,0:T(8,128)}, f32[512,128]{1,0:T(8,128)}, u32[]{:S(2)}, u32[]{:S(2)}) collective-permute-start(f32[512,128]{1,0:T(8,128)} %slice.47), channel_id=1, source_target_pairs={{0,3},{1,0},{2,1},{3,2},{4,7},{5,4},{6,5},{7,6},{8,11},{9,8},{10,9... | collective-permute-start | bytes 786440 | tf_op jit(solution)/shard_map/ppermute | solution.py:174
  112.0 1.0 select_select_fusion.4
  113.0 1.1 collective-permute-done.25.opp_a_ref
  114.1 2.6 %collective-permute-done.26.opp_b_ref = f32[512,128]{1,0:T(8,128)} collective-permute-done((f32[512,128]{1,0:T(8,128)}, f32[512,128]{1,0:T(8,128)}, u32[]{:S(2)}, u32[]{:S(2)}) %collective-permute-start.26) | collective-permute-done | bytes 262176 | tf_op jit(solution)/shard_map/ppermute | solution.py:174
  116.7 5.3 %collective-permute-start.28 = (f32[384,128]{1,0:T(8,128)S(1)}, f32[384,128]{1,0:T(8,128)S(1)}, u32[]{:S(2)}, u32[]{:S(2)}) collective-permute-start(f32[384,128]{1,0:T(8,128)S(1)} %select_select_fusion.4), channel_id=1, source_target_pairs={{32,35},{33,32},{34,33},{35,34},{36,39},{37,36},{38,37},{39,38},{4... | collective-permute-start | bytes 589832 | tf_op jit(solution)/shard_map/ppermute | solution.py:174
  122.1 1.9 %collective-permute-start.29 = (f32[384,128]{1,0:T(8,128)S(1)}, f32[384,128]{1,0:T(8,128)S(1)}, u32[]{:S(2)}, u32[]{:S(2)}) collective-permute-start(f32[384,128]{1,0:T(8,128)S(1)} %select_select_fusion.4), channel_id=1, source_target_pairs={{32,34},{33,35},{34,32},{35,33},{36,38},{37,39},{38,36},{39,37},{4... | collective-permute-start | bytes 589832 | tf_op jit(solution)/shard_map/ppermute | solution.py:174
  124.0 2.5 %collective-permute-start.30 = (f32[384,128]{1,0:T(8,128)S(1)}, f32[384,128]{1,0:T(8,128)S(1)}, u32[]{:S(2)}, u32[]{:S(2)}) collective-permute-start(f32[384,128]{1,0:T(8,128)S(1)} %select_select_fusion.4), channel_id=1, source_target_pairs={{32,33},{33,34},{34,35},{35,32},{36,37},{37,38},{38,39},{39,36},{4... | collective-permute-start | bytes 589832 | tf_op jit(solution)/shard_map/ppermute | solution.py:174
  126.5 0.7 constant_dynamic-update-slice_fusion.3
  127.2 0.7 constant_dynamic-update-slice_fusion.2
  127.9 2.2 %collective-permute-done.29 = f32[384,128]{1,0:T(8,128)S(1)} collective-permute-done((f32[384,128]{1,0:T(8,128)S(1)}, f32[384,128]{1,0:T(8,128)S(1)}, u32[]{:S(2)}, u32[]{:S(2)}) %collective-permute-start.29) | collective-permute-done | bytes 196640 | tf_op jit(solution)/shard_map/ppermute | solution.py:174
  130.0 0.7 constant_dynamic-update-slice_fusion.1
  130.7 1.4 collective-permute-done.30
  132.1 0.7 constant_dynamic-update-slice_fusion
  132.8 2.2 %collective-permute-start.31 = (f32[1536,128]{1,0:T(8,128)}, f32[1536,128]{1,0:T(8,128)}, u32[]{:S(2)}, u32[]{:S(2)}) collective-permute-start(f32[1536,128]{1,0:T(8,128)} %constant_dynamic-update-slice_fusion), channel_id=1, source_target_pairs={{32,0},{33,1},{34,2},{35,3},{36,4},{37,5},{38,6},{39,7},{40,8},{41... | collective-permute-start | bytes 2359304 | tf_op jit(solution)/shard_map/ppermute | solution.py:174
  135.0 0.1 pad_add_fusion.pos_ref
  135.1 1.3 broadcast_select_fusion.b_ref
  136.4 1.2 broadcast_select_fusion.1.f_ref
  137.6 13.3 %update.1 = f32[4096,128]{1,0:T(8,128)} custom-call(s32[4]{0:T(128)S(1)} %pad_add_fusion.pos_ref, f32[1024,128]{1,0:T(8,128)S(1)} %select_select_fusion.2.own_ref, f32[1024,128]{1,0:T(8,128)S(1)} %collective-permute-done.19.left_ref, f32[1024,128]{1,0:T(8,128)} %collective-permute-done.20.right_ref, f32[512,128]{1,0:T(8,128)S(1)} %collective-permute-done.25.opp_a_ref, ...), custom_call_target="tpu_custom_call" | custom-call | flops 8000000000 | bytes 9000000 | tf_op jit(solution)/shard_map/update/pallas_call | solution.py:161
  (30 shorter events, 0.2 us)
Async XLA Ops:
  0.0 3.8 %copy-start = (f32[2,512,1,512]{3,2,1,0:T(1,128)S(1)}, f32[2,512,1,512]{3,2,1,0:T(1,128)}, u32[]{:S(2)}) copy-start(f32[2,512,1,512]{3,2,1,0:T(1,128)} %param.1) | copy-start | bytes 6291460
  3.1 9.5 %collective-permute-start = (f32[2048,128]{1,0:T(8,128)}, f32[2048,128]{1,0:T(8,128)S(1)}, u32[]{:S(2)}, u32[]{:S(2)}) collective-permute-start(f32[2048,128]{1,0:T(8,128)} %bitcast.4), channel_id=1, source_target_pairs={{0,60}} | collective-permute-start | bytes 3145736 | tf_op jit(solution)/shard_map/ppermute | solution.py:174
  4.9 6.0 %collective-permute-start.1 = (f32[1024,128]{1,0:T(8,128)S(1)}, f32[1024,128]{1,0:T(8,128)}, u32[]{:S(2)}, u32[]{:S(2)}) collective-permute-start(f32[1024,128]{1,0:T(8,128)S(1)} %get-tuple-element.49), channel_id=1, source_target_pairs={{0,3},{32,35},{64,67},{96,99},{128,131},{160,163},{192,195},{224,2... | collective-permute-start | bytes 1572872 | tf_op jit(solution)/shard_map/ppermute | solution.py:174
  6.4 6.2 %collective-permute-start.2 = (f32[1024,128]{1,0:T(8,128)}, f32[1024,128]{1,0:T(8,128)}, u32[]{:S(2)}, u32[]{:S(2)}) collective-permute-start(f32[1024,128]{1,0:T(8,128)} %get-tuple-element.48), channel_id=1, source_target_pairs={{0,2},{32,34},{64,66},{96,98},{128,130},{160,162},{192,194},{224,2... | collective-permute-start | bytes 1572872 | tf_op jit(solution)/shard_map/ppermute | solution.py:174
  7.8 4.7 %collective-permute-start.3 = (f32[1024,128]{1,0:T(8,128)}, f32[1024,128]{1,0:T(8,128)}, u32[]{:S(2)}, u32[]{:S(2)}) collective-permute-start(f32[1024,128]{1,0:T(8,128)} %get-tuple-element.47), channel_id=1, source_target_pairs={{0,1},{32,33},{64,65},{96,97},{128,129},{160,161},{192,193},{224,2... | collective-permute-start | bytes 1572872 | tf_op jit(solution)/shard_map/ppermute | solution.py:174
  9.3 8.5 %collective-permute-start.6 = (f32[2048,128]{1,0:T(8,128)}, f32[2048,128]{1,0:T(8,128)}, u32[]{:S(2)}, u32[]{:S(2)}) collective-permute-start(f32[2048,128]{1,0:T(8,128)} %bitcast.4), channel_id=1, source_target_pairs={{1,193},{2,194},{3,195},{4,196},{5,197},{6,198},{7,199},{8,200},{9... | collective-permute-start | bytes 3145736 | tf_op jit(solution)/shard_map/ppermute | solution.py:174
  10.9 6.9 %collective-permute-start.7 = (f32[2048,128]{1,0:T(8,128)}, f32[2048,128]{1,0:T(8,128)}, u32[]{:S(2)}, u32[]{:S(2)}) collective-permute-start(f32[2048,128]{1,0:T(8,128)} %bitcast.4), channel_id=1, source_target_pairs={{1,321},{2,322},{3,323},{4,324},{5,325},{6,326},{7,327},{8,328},{9... | collective-permute-start | bytes 3145736 | tf_op jit(solution)/shard_map/ppermute | solution.py:174
  12.6 5.3 %copy-start.1 = (f32[2048,128]{1,0:T(8,128)}, f32[2048,128]{1,0:T(8,128)S(1)}, u32[]{:S(2)}) copy-start(f32[2048,128]{1,0:T(8,128)S(1)} %collective-permute-done.a_ref) | copy-start | bytes 3145732
  14.9 3.0 %collective-permute-start.4 = (f32[1024,128]{1,0:T(8,128)}, f32[1024,128]{1,0:T(8,128)}, u32[]{:S(2)}, u32[]{:S(2)}) collective-permute-start(f32[1024,128]{1,0:T(8,128)} %slice_select_fusion), channel_id=1, source_target_pairs={{2,14},{3,15},{34,46},{35,47},{66,78},{67,79},{98,110},{99,111},{1... | collective-permute-start | bytes 1572872 | tf_op jit(solution)/shard_map/ppermute | solution.py:174
  16.4 1.5 collective-permute-start.5
  17.9 1.2 copy-start.2
  19.1 4.0 %collective-permute-start.8 = (f32[384,128]{1,0:T(8,128)S(1)}, f32[384,128]{1,0:T(8,128)}, u32[]{:S(2)}, u32[]{:S(2)}) collective-permute-start(f32[384,128]{1,0:T(8,128)S(1)} %get-tuple-element.52), channel_id=1, source_target_pairs={{60,61}} | collective-permute-start | bytes 589832 | tf_op jit(solution)/shard_map/ppermute | solution.py:174
  20.5 2.7 %collective-permute-start.9 = (f32[384,128]{1,0:T(8,128)S(1)}, f32[384,128]{1,0:T(8,128)}, u32[]{:S(2)}, u32[]{:S(2)}) collective-permute-start(f32[384,128]{1,0:T(8,128)S(1)} %get-tuple-element.51), channel_id=1, source_target_pairs={{60,62}} | collective-permute-start | bytes 589832 | tf_op jit(solution)/shard_map/ppermute | solution.py:174
  21.8 1.3 collective-permute-start.10
  24.2 5.2 %collective-permute-start.11 = (f32[384,128]{1,0:T(8,128)S(1)}, f32[384,128]{1,0:T(8,128)S(1)}, u32[]{:S(2)}, u32[]{:S(2)}) collective-permute-start(f32[384,128]{1,0:T(8,128)S(1)} %slice_select_fusion.1), channel_id=1, source_target_pairs={{60,380},{61,381},{62,382},{63,383}} | collective-permute-start | bytes 589832 | tf_op jit(solution)/shard_map/ppermute | solution.py:174
  24.9 4.6 %collective-permute-start.12 = (f32[384,128]{1,0:T(8,128)S(1)}, f32[384,128]{1,0:T(8,128)S(1)}, u32[]{:S(2)}, u32[]{:S(2)}) collective-permute-start(f32[384,128]{1,0:T(8,128)S(1)} %slice_select_fusion.1), channel_id=1, source_target_pairs={{60,252},{61,253},{62,254},{63,255}} | collective-permute-start | bytes 589832 | tf_op jit(solution)/shard_map/ppermute | solution.py:174
  26.7 9.8 %collective-permute-start.15 = (f32[1024,128]{1,0:T(8,128)S(1)}, f32[1024,128]{1,0:T(8,128)}, u32[]{:S(2)}, u32[]{:S(2)}) collective-permute-start(f32[1024,128]{1,0:T(8,128)S(1)} %select_select_fusion.3), channel_id=1, source_target_pairs={{2,6},{3,7},{34,38},{35,39},{66,70},{67,71},{98,102},{99,103},{128... | collective-permute-start | bytes 1572872 | tf_op jit(solution)/shard_map/ppermute | solution.py:174
  28.1 41.3 %collective-permute-start.16 = (f32[1024,128]{1,0:T(8,128)S(1)}, f32[1024,128]{1,0:T(8,128)}, u32[]{:S(2)}, u32[]{:S(2)}) collective-permute-start(f32[1024,128]{1,0:T(8,128)S(1)} %select_select_fusion.3), channel_id=1, source_target_pairs={{386,414},{387,415},{418,446},{419,447},{450,478},{451,479},{482,5... | collective-permute-start | bytes 1572872 | tf_op jit(solution)/shard_map/ppermute | solution.py:174
  29.5 5.3 %collective-permute-start.13 = (f32[384,128]{1,0:T(8,128)S(1)}, f32[384,128]{1,0:T(8,128)S(1)}, u32[]{:S(2)}, u32[]{:S(2)}) collective-permute-start(f32[384,128]{1,0:T(8,128)S(1)} %select_select_fusion.7), channel_id=1, source_target_pairs={{60,508},{61,509},{62,510},{63,511},{252,188},{253,189},{254,190},... | collective-permute-start | bytes 589832 | tf_op jit(solution)/shard_map/ppermute | solution.py:174
  30.2 6.3 %collective-permute-start.14 = (f32[384,128]{1,0:T(8,128)S(1)}, f32[384,128]{1,0:T(8,128)S(1)}, u32[]{:S(2)}, u32[]{:S(2)}) collective-permute-start(f32[384,128]{1,0:T(8,128)S(1)} %select_select_fusion.7), channel_id=1, source_target_pairs={{60,124},{61,125},{62,126},{63,127},{252,316},{253,317},{254,318},... | collective-permute-start | bytes 589832 | tf_op jit(solution)/shard_map/ppermute | solution.py:174
  33.2 62.0 %collective-permute-start.21 = (f32[2048,128]{1,0:T(8,128)}, f32[2048,128]{1,0:T(8,128)}, u32[]{:S(2)}, u32[]{:S(2)}) collective-permute-start(f32[2048,128]{1,0:T(8,128)} %select_select_fusion.1), channel_id=1, source_target_pairs={{1,65},{2,66},{3,67},{4,68},{5,69},{6,70},{7,71},{8,72},{9,73},{10... | collective-permute-start | bytes 3145736 | tf_op jit(solution)/shard_map/ppermute | solution.py:174
  34.8 60.4 %collective-permute-start.22 = (f32[2048,128]{1,0:T(8,128)}, f32[2048,128]{1,0:T(8,128)}, u32[]{:S(2)}, u32[]{:S(2)}) collective-permute-start(f32[2048,128]{1,0:T(8,128)} %select_select_fusion.1), channel_id=1, source_target_pairs={{1,449},{2,450},{3,451},{4,452},{5,453},{6,454},{7,455},{8,456},{9... | collective-permute-start | bytes 3145736 | tf_op jit(solution)/shard_map/ppermute | solution.py:174
  69.4 8.3 %collective-permute-start.17 = (f32[384,128]{1,0:T(8,128)S(1)}, f32[384,128]{1,0:T(8,128)S(1)}, u32[]{:S(2)}, u32[]{:S(2)}) collective-permute-start(f32[384,128]{1,0:T(8,128)S(1)} %select_select_fusion.6), channel_id=1, source_target_pairs={{60,48},{61,49},{62,50},{63,51},{124,112},{125,113},{126,114},{127... | collective-permute-start | bytes 589832 | tf_op jit(solution)/shard_map/ppermute | solution.py:174
  71.2 24.0 %collective-permute-start.19 = (f32[1024,128]{1,0:T(8,128)S(1)}, f32[1024,128]{1,0:T(8,128)S(1)}, u32[]{:S(2)}, u32[]{:S(2)}) collective-permute-start(f32[1024,128]{1,0:T(8,128)S(1)} %select_select_fusion.2.own_ref), channel_id=1, source_target_pairs={{0,1},{1,2},{2,3},{3,0},{4,5},{5,6},{6,7},{7,4},{8,9},{9,10},{10,1... | collective-permute-start | bytes 1572872 | tf_op jit(solution)/shard_map/ppermute | solution.py:174
  75.5 19.6 %collective-permute-start.20 = (f32[1024,128]{1,0:T(8,128)S(1)}, f32[1024,128]{1,0:T(8,128)}, u32[]{:S(2)}, u32[]{:S(2)}) collective-permute-start(f32[1024,128]{1,0:T(8,128)S(1)} %select_select_fusion.2.own_ref), channel_id=1, source_target_pairs={{0,3},{1,0},{2,1},{3,2},{4,7},{5,4},{6,5},{7,6},{8,11},{9,8},{10,9... | collective-permute-start | bytes 1572872 | tf_op jit(solution)/shard_map/ppermute | solution.py:174
  77.7 15.8 %collective-permute-start.18 = (f32[384,128]{1,0:T(8,128)S(1)}, f32[384,128]{1,0:T(8,128)}, u32[]{:S(2)}, u32[]{:S(2)}) collective-permute-start(f32[384,128]{1,0:T(8,128)S(1)} %select_select_fusion.6), channel_id=1, source_target_pairs={{60,40},{61,41},{62,42},{63,43},{124,104},{125,105},{126,106},{127... | collective-permute-start | bytes 589832 | tf_op jit(solution)/shard_map/ppermute | solution.py:174
  97.8 18.9 %collective-permute-start.27 = (f32[2048,128]{1,0:T(8,128)}, f32[2048,128]{1,0:T(8,128)}, u32[]{:S(2)}, u32[]{:S(2)}) collective-permute-start(f32[2048,128]{1,0:T(8,128)} %select_select_fusion), channel_id=1, source_target_pairs={{0,32},{1,33},{2,34},{3,35},{4,36},{5,37},{6,38},{7,39},{8,40},{9,... | collective-permute-start | bytes 3145736 | tf_op jit(solution)/shard_map/ppermute | solution.py:174
  99.1 12.8 %collective-permute-start.23 = (f32[384,128]{1,0:T(8,128)}, f32[384,128]{1,0:T(8,128)}, u32[]{:S(2)}, u32[]{:S(2)}) collective-permute-start(f32[384,128]{1,0:T(8,128)} %select_select_fusion.5), channel_id=1, source_target_pairs={{60,56},{61,57},{62,58},{63,59},{124,120},{125,121},{126,122},{127... | collective-permute-start | bytes 589832 | tf_op jit(solution)/shard_map/ppermute | solution.py:174
  101.1 10.9 %collective-permute-start.24 = (f32[384,128]{1,0:T(8,128)}, f32[384,128]{1,0:T(8,128)}, u32[]{:S(2)}, u32[]{:S(2)}) collective-permute-start(f32[384,128]{1,0:T(8,128)} %select_select_fusion.5), channel_id=1, source_target_pairs={{60,32},{61,33},{62,34},{63,35},{124,96},{125,97},{126,98},{127,99... | collective-permute-start | bytes 589832 | tf_op jit(solution)/shard_map/ppermute | solution.py:174
  103.8 10.3 %collective-permute-start.25 = (f32[512,128]{1,0:T(8,128)}, f32[512,128]{1,0:T(8,128)S(1)}, u32[]{:S(2)}, u32[]{:S(2)}) collective-permute-start(f32[512,128]{1,0:T(8,128)} %slice.46), channel_id=1, source_target_pairs={{0,1},{1,2},{2,3},{3,0},{4,5},{5,6},{6,7},{7,4},{8,9},{9,10},{10,1... | collective-permute-start | bytes 786440 | tf_op jit(solution)/shard_map/ppermute | solution.py:174
  107.4 9.3 %collective-permute-start.26 = (f32[512,128]{1,0:T(8,128)}, f32[512,128]{1,0:T(8,128)}, u32[]{:S(2)}, u32[]{:S(2)}) collective-permute-start(f32[512,128]{1,0:T(8,128)} %slice.47), channel_id=1, source_target_pairs={{0,3},{1,0},{2,1},{3,2},{4,7},{5,4},{6,5},{7,6},{8,11},{9,8},{10,9... | collective-permute-start | bytes 786440 | tf_op jit(solution)/shard_map/ppermute | solution.py:174
  116.7 10.4 %collective-permute-start.28 = (f32[384,128]{1,0:T(8,128)S(1)}, f32[384,128]{1,0:T(8,128)S(1)}, u32[]{:S(2)}, u32[]{:S(2)}) collective-permute-start(f32[384,128]{1,0:T(8,128)S(1)} %select_select_fusion.4), channel_id=1, source_target_pairs={{32,35},{33,32},{34,33},{35,34},{36,39},{37,36},{38,37},{39,38},{4... | collective-permute-start | bytes 589832 | tf_op jit(solution)/shard_map/ppermute | solution.py:174
  122.1 8.0 %collective-permute-start.29 = (f32[384,128]{1,0:T(8,128)S(1)}, f32[384,128]{1,0:T(8,128)S(1)}, u32[]{:S(2)}, u32[]{:S(2)}) collective-permute-start(f32[384,128]{1,0:T(8,128)S(1)} %select_select_fusion.4), channel_id=1, source_target_pairs={{32,34},{33,35},{34,32},{35,33},{36,38},{37,39},{38,36},{39,37},{4... | collective-permute-start | bytes 589832 | tf_op jit(solution)/shard_map/ppermute | solution.py:174
  124.0 8.1 %collective-permute-start.30 = (f32[384,128]{1,0:T(8,128)S(1)}, f32[384,128]{1,0:T(8,128)S(1)}, u32[]{:S(2)}, u32[]{:S(2)}) collective-permute-start(f32[384,128]{1,0:T(8,128)S(1)} %select_select_fusion.4), channel_id=1, source_target_pairs={{32,33},{33,34},{34,35},{35,32},{36,37},{37,38},{38,39},{39,36},{4... | collective-permute-start | bytes 589832 | tf_op jit(solution)/shard_map/ppermute | solution.py:174
  132.8 3.6 %collective-permute-start.31 = (f32[1536,128]{1,0:T(8,128)}, f32[1536,128]{1,0:T(8,128)}, u32[]{:S(2)}, u32[]{:S(2)}) collective-permute-start(f32[1536,128]{1,0:T(8,128)} %constant_dynamic-update-slice_fusion), channel_id=1, source_target_pairs={{32,0},{33,1},{34,2},{35,3},{36,4},{37,5},{38,6},{39,7},{40,8},{41... | collective-permute-start | bytes 2359304 | tf_op jit(solution)/shard_map/ppermute | solution.py:174

commit v4 on v3

--- a/solution.py
+++ b/solution.py
@@ -109,12 +109,17 @@
     )(flag, a)
 
 
-def update_kernel(pos_ref, own_ref, left_ref, right_ref, opp_a_ref, opp_b_ref, b_ref, f_ref, cov_ref, out_ref, y_ref):
-    row, col, x = pos_ref[0], pos_ref[1], pos_ref[2]
+def update_kernel(pos_ref, own_ref, left_ref, right_ref, opp_ref, b_ref, b_other_ref, f0_ref, f3_ref, f1_ref, f2_ref, cov_ref, out_ref, y_ref, f_ref):
+    row, col, x, core = pos_ref[0], pos_ref[1], pos_ref[2], pos_ref[3]
+    part = 3 * SB
+    for shift, ref in enumerate((f0_ref, f1_ref, f2_ref, f3_ref)):
+        f_ref[pl.ds(pl.multiple_of(lax.rem(x + shift, 4) * part, SB), part), :] = ref[...]
 
     def block(i):
-        place = lax.rem(i // 3 - x + 4, 4)
-        return f_ref[pl.ds(pl.multiple_of(place * (3 * SB) + (i % 3) * SB, SB), SB), :]
+        return f_ref[i * SB : (i + 1) * SB, :]
+
+    def b_rows(first):
+        return jnp.where(core == 1, wide(b_other_ref, first, HB), wide(b_ref, first, HB))
 
     zero = jnp.zeros((SB, SB), jnp.float32)
 
@@ -126,9 +131,9 @@
     d0 = square(block(M0), zero, block(X10), block(M1))
     d1 = square(block(M2), zero, block(X32), block(M3))
     g = square(block(L20), block(L21), block(L30), block(L31))
-    y0 = nn(d0, wide(b_ref, 0, HB))
+    y0 = nn(d0, b_rows(0))
     y_ref[0:HB, :] = y0
-    y_ref[HB:TB, :] = nn(d1, wide(b_ref, HB, HB) - nn(g, y0))
+    y_ref[HB:TB, :] = nn(d1, b_rows(HB) - nn(g, y0))
 
     def piece(q, raw0, raw1):
         x0 = nt(raw0, d0)
@@ -148,26 +153,22 @@
             above = lax.broadcasted_iota(jnp.int32, (HB, TB), 1) > at_row
             put_wide(out_ref, q * HB, jnp.where(jnp.logical_and(tile_row == 0, above), 0.0, xs))
 
-    for shift, ref in ((0, own_ref), (3, left_ref), (1, right_ref)):
+    for shift, ref in ((0, own_ref), (3, left_ref), (1, right_ref), (2, opp_ref)):
         piece(lax.rem(x + shift, 4), wide(ref, 0, HB, 0, 2), wide(ref, 0, HB, 2, 4))
-    half = HB // 2
-    opp0 = jnp.concatenate([wide(opp_a_ref, 0, half, 0, 2), wide(opp_b_ref, 0, half, 0, 2)], axis=0)
-    opp1 = jnp.concatenate([wide(opp_a_ref, 0, half, 2, 4), wide(opp_b_ref, 0, half, 2, 4)], axis=0)
-    piece(lax.rem(x + 2, 4), opp0, opp1)
-
-
-def update(pos, own, left, right, opp_a, opp_b, b, f, cov):
+
+
+def update(*operands):
     vmem = pl.BlockSpec(memory_space=pltpu.VMEM)
     return pl.pallas_call(
         update_kernel,
         out_shape=jax.ShapeDtypeStruct((8 * TB, SB), jnp.float32),
-        in_specs=[pl.BlockSpec(memory_space=pltpu.SMEM)] + [vmem] * 8,
+        in_specs=[pl.BlockSpec(memory_space=pltpu.SMEM)] + [vmem] * (len(operands) - 1),
         out_specs=vmem,
-        scratch_shapes=[pltpu.VMEM((TB, TB), jnp.float32)],
+        scratch_shapes=[pltpu.VMEM((TB, TB), jnp.float32), pltpu.VMEM((SLOTS * SB, SB), jnp.float32)],
         cost_estimate=pl.CostEstimate(flops=8_000_000_000, bytes_accessed=9_000_000, transcendentals=0),
         compiler_params=pltpu.CompilerParams(vmem_limit_bytes=40 * 1024 * 1024),
         name="update",
-    )(pos, own, left, right, opp_a, opp_b, b, f, cov)
+    )(*operands)
 
 
 def send(value, pairs):
@@ -234,15 +235,8 @@
     def along_z(a, b):
         return [(at(i, a, j), at(i, b, j)) for i in rows for j in range(NX) if last_col(i, j) > 0 and reaches(b, last_col(i, j))]
 
-    def shift_x(by, cores):
-        return [
-            (at(i, k, j), at(i, k, (j + by) % NX))
-            for i in rows
-            if i % 2 in cores
-            for k in range(NZ)
-            for j in range(NX)
-            if len(cores) == 1 or NX * k <= last_col(i, 2)
-        ]
+    def shift_x(by):
+        return [(at(i, k, j), at(i, k, (j + by) % NX)) for i in rows for k in range(NZ) for j in range(NX)]
 
     def along_y(a, b):
         return [(at(2 * a, k, j), at(2 * b, k, j)) for k in range(NZ) for j in range(NX) if k + j > 0]
@@ -266,16 +260,20 @@
     quarter = [cov[quarter_rows * q : quarter_rows * (q + 1)] for q in range(4)]
     got = [send(quarter[q], scatter(q)) for q in (3, 2, 1)]
     moved = ring_sends(b_tile, ROUNDS[0], along_y)
-    corner, got = tied(corner, got)
+
+    got, moved = tied(got, moved)
     own = by_x([quarter[0], got[2], got[1], got[0]])
     got = ring_sends(own, ROUNDS[0], along_z)
-
-    corner, got, moved = tied(corner, got, moved)
+    b_tile = ring_pick(b_tile, ROUNDS[0], y, moved)
+    moved = ring_sends(b_tile, ROUNDS[1], along_y)
+
+    corner, got = tied(corner, got)
+    f = factor_tile(flag, corner)
+    f, got, moved = tied(f, got, moved)
     own = ring_pick(own, ROUNDS[0], z, got)
     got = ring_sends(own, ROUNDS[1], along_z)
-    b_tile = ring_pick(b_tile, ROUNDS[0], y, moved)
-    moved = ring_sends(b_tile, ROUNDS[1], along_y)
-    f = factor_tile(flag, corner)
+    b_tile = ring_pick(b_tile, ROUNDS[1], y, moved)
+    b_other = send(b_tile, across)
 
     part = [f[3 * SB * q : 3 * SB * (q + 1)] for q in range(4)]
     mine = by_x([part[0]] + [send(part[q], [(home, home + q)]) for q in (1, 2, 3)])
@@ -284,24 +282,22 @@
 
     mine, got = tied(mine, got)
     own = ring_pick(own, ROUNDS[1], z, got)
-    left = send(own, shift_x(1, (0, 1)))
-    right = send(own, shift_x(-1, (0, 1)))
+    left = send(own, shift_x(1))
+    right = send(own, shift_x(-1))
     mine = ring_round(mine, ROUNDS[0], home_z, factor_z)
 
-    mine, left, right, moved = tied(mine, left, right, moved)
-    b_tile = ring_pick(b_tile, ROUNDS[1], y, moved)
-    opp_a = send(left[: quarter_rows // 2], shift_x(1, (0, 1)))
-    opp_b = send(right[quarter_rows // 2 :], shift_x(-1, (0, 1)))
-    b_other = send(b_tile, across)
+    mine, left, right = tied(mine, left, right)
+    opposite = send(left, shift_x(1))
     mine = ring_round(mine, ROUNDS[1], home_z, factor_z)
-
-    mine, opp_a, opp_b, b_other = tied(mine, opp_a, opp_b, b_other)
-    b_tile = jnp.where(core == 1, b_other, b_tile)
-    turned = jnp.concatenate([mine] + [send(mine, shift_x(-by, (1,))) for by in (1, 2, 3)], axis=0)
-    turned = jnp.where(core == 0, send(turned, [(b, a) for a, b in across]), turned)
-
-    pos = jnp.stack([row, col, x, 0]).astype(jnp.int32)
-    out = update(pos, own, left, right, opp_a, opp_b, b_tile, turned, cov)
+    mine = jnp.where(core == 0, send(mine, [(b, a) for a, b in across]), mine)
+
+    mine, opposite, b_other = tied(mine, opposite, b_other)
+    f_left = send(mine, shift_x(1))
+    f_right = send(mine, shift_x(-1))
+    f_opposite = send(f_left, shift_x(1))
+
+    pos = jnp.stack([row, col, x, core]).astype(jnp.int32)
+    out = update(pos, own, left, right, opposite, b_tile, b_other, mine, f_left, f_right, f_opposite, cov)
     return out.reshape(covariance.shape)
 
 

time: 152 us -> 160 us (1.053)
  the two profiles are of different devices: /device:TPU:185 before, /device:TPU:505 now
where the time goes in v4:
time: 160 us; the launch traced here: 159 us
  waiting for transfers between devices  76.5 us (48%)
  starting transfers between devices  46.9 us (29%)
  local copies, waits for them, and re-layouts  14.7 us (9%)
  Pallas kernels  13.7 us (9%)
  other arithmetic  6.35 us (4%)
    ppermute x31, waiting for transfers between devices, send(): return lax.ppermute(value, AXES, pairs)  76.5 us
    ppermute x31, starting transfers between devices, send(): return lax.ppermute(value, AXES, pairs)  46.9 us
    pallas_call x1, Pallas kernels, update(): pl.pallas_call(update_kernel, out_shape=jax.ShapeDtypeStruct((8 * TB, SB)...  13.7 us
    unnamed x36, local copies, waits for them, and re-layouts  9.66 us
    select_n x8, other arithmetic, ring_pick(): value = jnp.where(one_of(pos, [b for _, b in pairs]), received, value)  4.11 us
  transfers between devices with their start and end apart: 31, of which 7 were waited for; matrix products, arithmetic and copies ran while one was open for 4% of the time, Pallas kernels for 0%

profile of v4, /device:TPU:505, one launch (start us, length us, event | category | flops | bytes accessed | tf_op | source)
XLA Modules:
  0.0 158.6 jit_solution(949102973328960468)
XLA Ops:
  0.0 3.1 %slice.30 = f32[1,512,1,512]{3,2,1,0:T(1,128)} slice(f32[2,512,1,512]{3,2,1,0:T(1,128)} %param.1), slice={[0:1], [0:512], [0:1], [0:512]} | slice | bytes 2097152 | tf_op jit(solution)/shard_map/slice | solution.py:258
  3.1 1.7 %collective-permute-start.5 = (f32[2048,128]{1,0:T(8,128)}, f32[2048,128]{1,0:T(8,128)}, u32[]{:S(2)}, u32[]{:S(2)}) collective-permute-start(f32[2048,128]{1,0:T(8,128)} %bitcast.5), channel_id=1, source_target_pairs={{1,321},{2,322},{3,323},{4,324},{5,325},{6,326},{7,327},{8,328},{9... | collective-permute-start | bytes 3145736 | tf_op jit(solution)/shard_map/ppermute | solution.py:175
  4.7 1.7 %collective-permute-start.4 = (f32[2048,128]{1,0:T(8,128)}, f32[2048,128]{1,0:T(8,128)}, u32[]{:S(2)}, u32[]{:S(2)}) collective-permute-start(f32[2048,128]{1,0:T(8,128)} %bitcast.5), channel_id=1, source_target_pairs={{1,193},{2,194},{3,195},{4,196},{5,197},{6,198},{7,199},{8,200},{9... | collective-permute-start | bytes 3145736 | tf_op jit(solution)/shard_map/ppermute | solution.py:175
  6.4 1.1 fusion
  7.4 1.5 collective-permute-start.3
  8.9 1.5 collective-permute-start.2
  10.4 1.5 collective-permute-start.1
  11.8 0.7 collective-permute-start
  12.6 1.2 slice_select_fusion
  13.8 1.5 collective-permute-start.7
  15.3 0.7 collective-permute-start.6
  16.0 1.4 select_select_fusion.1
  17.4 0.7 collective-permute-start.9
  18.1 0.7 collective-permute-start.8
  18.8 0.0 copy-start.3
  18.9 1.0 copy-done.3
  19.8 0.8 copy-done.16
  20.6 1.2 copy-done.4
  21.9 0.9 copy-done.12
  22.8 0.9 fusion.1
  23.7 0.3 copy-done.14
  24.0 1.3 collective-permute-start.12
  25.4 1.3 collective-permute-start.11
  26.7 1.3 collective-permute-start.10
  28.0 1.0 select_select_fusion.8
  29.0 0.7 collective-permute-start.14
  29.7 0.7 collective-permute-start.13
  30.4 0.1 select_select_fusion.3
  30.5 0.7 collective-permute-start.18
  31.2 1.5 collective-permute-start.17
  32.7 0.7 collective-permute-start.16
  33.4 1.3 collective-permute-start.15
  34.7 0.0 copy-start.13
  34.8 52.7 %collective-permute-done.15 = f32[384,128]{1,0:T(8,128)} collective-permute-done((f32[384,128]{1,0:T(8,128)S(1)}, f32[384,128]{1,0:T(8,128)}, u32[]{:S(2)}, u32[]{:S(2)}) %collective-permute-start.15) | collective-permute-done | bytes 196640 | tf_op jit(solution)/shard_map/ppermute | solution.py:175
  87.5 1.0 select_select_fusion.6
  88.5 1.3 collective-permute-start.20
  89.8 1.3 collective-permute-start.19
  91.1 0.1 select_select_fusion.2.own_ref
  91.2 1.9 %collective-permute-start.22 = (f32[1024,128]{1,0:T(8,128)S(1)}, f32[1024,128]{1,0:T(8,128)S(1)}, u32[]{:S(2)}, u32[]{:S(2)}) collective-permute-start(f32[1024,128]{1,0:T(8,128)S(1)} %select_select_fusion.2.own_ref), channel_id=1, source_target_pairs={{0,3},{1,0},{2,1},{3,2},{4,7},{5,4},{6,5},{7,6},{8,11},{9,8},{10,9... | collective-permute-start | bytes 1572872 | tf_op jit(solution)/shard_map/ppermute | solution.py:175
  93.1 3.9 %collective-permute-start.21 = (f32[1024,128]{1,0:T(8,128)S(1)}, f32[1024,128]{1,0:T(8,128)S(1)}, u32[]{:S(2)}, u32[]{:S(2)}) collective-permute-start(f32[1024,128]{1,0:T(8,128)S(1)} %select_select_fusion.2.own_ref), channel_id=1, source_target_pairs={{0,1},{1,2},{2,3},{3,0},{4,5},{5,6},{6,7},{7,4},{8,9},{9,10},{10,1... | collective-permute-start | bytes 1572872 | tf_op jit(solution)/shard_map/ppermute | solution.py:175
  97.1 1.5 select_select_fusion.b_ref
  98.6 1.3 collective-permute-start.27
  99.9 1.7 %collective-permute-done.22.right_ref = f32[1024,128]{1,0:T(8,128)S(1)} collective-permute-done((f32[1024,128]{1,0:T(8,128)S(1)}, f32[1024,128]{1,0:T(8,128)S(1)}, u32[]{:S(2)}, u32[]{:S(2)}) %collective-permute-start.22) | collective-permute-done | bytes 524320 | tf_op jit(solution)/shard_map/ppermute | solution.py:175
  101.7 0.8 copy-done.5
  102.5 1.8 %collective-permute-done.21.left_ref = f32[1024,128]{1,0:T(8,128)S(1)} collective-permute-done((f32[1024,128]{1,0:T(8,128)S(1)}, f32[1024,128]{1,0:T(8,128)S(1)}, u32[]{:S(2)}, u32[]{:S(2)}) %collective-permute-start.21) | collective-permute-done | bytes 524320 | tf_op jit(solution)/shard_map/ppermute | solution.py:175
  104.3 0.8 copy-done.7
  105.1 1.3 collective-permute-start.24
  106.4 2.0 %collective-permute-start.23 = (f32[384,128]{1,0:T(8,128)S(1)}, f32[384,128]{1,0:T(8,128)}, u32[]{:S(2)}, u32[]{:S(2)}) collective-permute-start(f32[384,128]{1,0:T(8,128)S(1)} %select_select_fusion.5), channel_id=1, source_target_pairs={{60,56},{61,57},{62,58},{63,59},{124,120},{125,121},{126,122},{127... | collective-permute-start | bytes 589832 | tf_op jit(solution)/shard_map/ppermute | solution.py:175
  108.3 2.7 %collective-permute-start.26 = (f32[1024,128]{1,0:T(8,128)}, f32[1024,128]{1,0:T(8,128)}, u32[]{:S(2)}, u32[]{:S(2)}) collective-permute-start(f32[1024,128]{1,0:T(8,128)} %copy-done.7), channel_id=1, source_target_pairs={{0,1},{1,2},{2,3},{3,0},{4,5},{5,6},{6,7},{7,4},{8,9},{9,10},{10,1... | collective-permute-start | bytes 1572872 | tf_op jit(solution)/shard_map/ppermute | solution.py:175
  111.0 0.7 copy-done.17
  111.8 1.3 collective-permute-start.25
  113.1 1.0 collective-permute-done.25
  114.1 9.0 %collective-permute-done.26.opp_ref = f32[1024,128]{1,0:T(8,128)} collective-permute-done((f32[1024,128]{1,0:T(8,128)}, f32[1024,128]{1,0:T(8,128)}, u32[]{:S(2)}, u32[]{:S(2)}) %collective-permute-start.26) | collective-permute-done | bytes 524320 | tf_op jit(solution)/shard_map/ppermute | solution.py:175
  123.2 2.1 %collective-permute-start.28 = (f32[384,128]{1,0:T(8,128)S(1)}, f32[384,128]{1,0:T(8,128)S(1)}, u32[]{:S(2)}, u32[]{:S(2)}) collective-permute-start(f32[384,128]{1,0:T(8,128)S(1)} %broadcast_select_fusion.f0_ref), channel_id=1, source_target_pairs={{0,1},{1,2},{2,3},{3,0},{4,5},{5,6},{6,7},{7,4},{8,9},{9,10},{10,1... | collective-permute-start | bytes 589832 | tf_op jit(solution)/shard_map/ppermute | solution.py:175
  125.3 4.3 %collective-permute-start.29 = (f32[384,128]{1,0:T(8,128)S(1)}, f32[384,128]{1,0:T(8,128)S(1)}, u32[]{:S(2)}, u32[]{:S(2)}) collective-permute-start(f32[384,128]{1,0:T(8,128)S(1)} %broadcast_select_fusion.f0_ref), channel_id=1, source_target_pairs={{0,3},{1,0},{2,1},{3,2},{4,7},{5,4},{6,5},{7,6},{8,11},{9,8},{10,9... | collective-permute-start | bytes 589832 | tf_op jit(solution)/shard_map/ppermute | solution.py:175
  129.7 2.1 %collective-permute-done.28.f3_ref = f32[384,128]{1,0:T(8,128)S(1)} collective-permute-done((f32[384,128]{1,0:T(8,128)S(1)}, f32[384,128]{1,0:T(8,128)S(1)}, u32[]{:S(2)}, u32[]{:S(2)}) %collective-permute-start.28) | collective-permute-done | bytes 196640 | tf_op jit(solution)/shard_map/ppermute | solution.py:175
  131.8 1.9 %collective-permute-start.30 = (f32[384,128]{1,0:T(8,128)S(1)}, f32[384,128]{1,0:T(8,128)S(1)}, u32[]{:S(2)}, u32[]{:S(2)}) collective-permute-start(f32[384,128]{1,0:T(8,128)S(1)} %collective-permute-done.28.f3_ref), channel_id=1, source_target_pairs={{0,1},{1,2},{2,3},{3,0},{4,5},{5,6},{6,7},{7,4},{8,9},{9,10},{10,1... | collective-permute-start | bytes 589832 | tf_op jit(solution)/shard_map/ppermute | solution.py:175
  133.7 0.1 pad_add_fusion.pos_ref
  133.8 0.0 collective-permute-done.29.f1_ref
  133.8 8.0 %collective-permute-done.30.f2_ref = f32[384,128]{1,0:T(8,128)S(1)} collective-permute-done((f32[384,128]{1,0:T(8,128)S(1)}, f32[384,128]{1,0:T(8,128)S(1)}, u32[]{:S(2)}, u32[]{:S(2)}) %collective-permute-start.30) | collective-permute-done | bytes 196640 | tf_op jit(solution)/shard_map/ppermute | solution.py:175
  141.8 1.0 copy-done.2
  142.8 1.0 copy-done.6
  143.9 1.0 copy-done.8
  144.9 13.7 %update.1 = f32[4096,128]{1,0:T(8,128)} custom-call(s32[4]{0:T(128)S(1)} %pad_add_fusion.pos_ref, f32[1024,128]{1,0:T(8,128)S(1)} %copy-done.2, f32[1024,128]{1,0:T(8,128)S(1)} %copy-done.8, f32[1024,128]{1,0:T(8,128)S(1)} %copy-done.6, f32[1024,128]{1,0:T(8,128)} %collective-permute-done.26.opp_ref, f32[2048,128]{1,0:T(8,128)S(1)} %select_select_fusion.b_ref, ...), custom_call_target="tpu_custom_call" | custom-call | flops 8000000000 | bytes 9000000 | tf_op jit(solution)/shard_map/update/pallas_call | solution.py:162
  (51 shorter events, 0.2 us)
Async XLA Ops:
  0.0 6.4 %copy-start = (f32[2,512,1,512]{3,2,1,0:T(1,128)S(1)}, f32[2,512,1,512]{3,2,1,0:T(1,128)}, u32[]{:S(2)}) copy-start(f32[2,512,1,512]{3,2,1,0:T(1,128)} %param.1) | copy-start | bytes 6291460
  3.1 9.5 %collective-permute-start.5 = (f32[2048,128]{1,0:T(8,128)}, f32[2048,128]{1,0:T(8,128)}, u32[]{:S(2)}, u32[]{:S(2)}) collective-permute-start(f32[2048,128]{1,0:T(8,128)} %bitcast.5), channel_id=1, source_target_pairs={{1,321},{2,322},{3,323},{4,324},{5,325},{6,326},{7,327},{8,328},{9... | collective-permute-start | bytes 3145736 | tf_op jit(solution)/shard_map/ppermute | solution.py:175
  4.7 7.9 %collective-permute-start.4 = (f32[2048,128]{1,0:T(8,128)}, f32[2048,128]{1,0:T(8,128)}, u32[]{:S(2)}, u32[]{:S(2)}) collective-permute-start(f32[2048,128]{1,0:T(8,128)} %bitcast.5), channel_id=1, source_target_pairs={{1,193},{2,194},{3,195},{4,196},{5,197},{6,198},{7,199},{8,200},{9... | collective-permute-start | bytes 3145736 | tf_op jit(solution)/shard_map/ppermute | solution.py:175
  7.4 4.4 %collective-permute-start.3 = (f32[1024,128]{1,0:T(8,128)S(1)}, f32[1024,128]{1,0:T(8,128)}, u32[]{:S(2)}, u32[]{:S(2)}) collective-permute-start(f32[1024,128]{1,0:T(8,128)S(1)} %get-tuple-element.49), channel_id=1, source_target_pairs={{0,1},{32,33},{64,65},{96,97},{128,129},{160,161},{192,193},{224,2... | collective-permute-start | bytes 1572872 | tf_op jit(solution)/shard_map/ppermute | solution.py:175
  8.9 3.7 %collective-permute-start.2 = (f32[1024,128]{1,0:T(8,128)}, f32[1024,128]{1,0:T(8,128)}, u32[]{:S(2)}, u32[]{:S(2)}) collective-permute-start(f32[1024,128]{1,0:T(8,128)} %get-tuple-element.50), channel_id=1, source_target_pairs={{0,2},{32,34},{64,66},{96,98},{128,130},{160,162},{192,194},{224,2... | collective-permute-start | bytes 1572872 | tf_op jit(solution)/shard_map/ppermute | solution.py:175
  10.4 2.2 %collective-permute-start.1 = (f32[1024,128]{1,0:T(8,128)}, f32[1024,128]{1,0:T(8,128)}, u32[]{:S(2)}, u32[]{:S(2)}) collective-permute-start(f32[1024,128]{1,0:T(8,128)} %get-tuple-element.51), channel_id=1, source_target_pairs={{0,3},{32,35},{64,67},{96,99},{128,131},{160,163},{192,195},{224,2... | collective-permute-start | bytes 1572872 | tf_op jit(solution)/shard_map/ppermute | solution.py:175
  11.8 7.0 %collective-permute-start = (f32[2048,128]{1,0:T(8,128)}, f32[2048,128]{1,0:T(8,128)S(1)}, u32[]{:S(2)}, u32[]{:S(2)}) collective-permute-start(f32[2048,128]{1,0:T(8,128)} %bitcast.5), channel_id=1, source_target_pairs={{0,60}} | collective-permute-start | bytes 3145736 | tf_op jit(solution)/shard_map/ppermute | solution.py:175
  13.8 3.6 %copy-start.10 = (f32[1024,128]{1,0:T(8,128)}, f32[1024,128]{1,0:T(8,128)S(1)}, u32[]{:S(2)}) copy-start(f32[1024,128]{1,0:T(8,128)S(1)} %slice_select_fusion) | copy-start | bytes 1572868
  13.8 6.0 %collective-permute-start.7 = (f32[1024,128]{1,0:T(8,128)S(1)}, f32[1024,128]{1,0:T(8,128)}, u32[]{:S(2)}, u32[]{:S(2)}) collective-permute-start(f32[1024,128]{1,0:T(8,128)S(1)} %slice_select_fusion), channel_id=1, source_target_pairs={{130,150},{131,151},{162,182},{163,183},{194,214},{195,215},{226,2... | collective-permute-start | bytes 1572872 | tf_op jit(solution)/shard_map/ppermute | solution.py:175
  15.3 4.6 %collective-permute-start.6 = (f32[1024,128]{1,0:T(8,128)S(1)}, f32[1024,128]{1,0:T(8,128)S(1)}, u32[]{:S(2)}, u32[]{:S(2)}) collective-permute-start(f32[1024,128]{1,0:T(8,128)S(1)} %slice_select_fusion), channel_id=1, source_target_pairs={{2,14},{3,15},{34,46},{35,47},{66,78},{67,79},{98,110},{99,111},{1... | collective-permute-start | bytes 1572872 | tf_op jit(solution)/shard_map/ppermute | solution.py:175
  17.4 4.5 %copy-start.9 = (f32[2048,128]{1,0:T(8,128)}, f32[2048,128]{1,0:T(8,128)S(1)}, u32[]{:S(2)}) copy-start(f32[2048,128]{1,0:T(8,128)S(1)} %select_select_fusion.1) | copy-start | bytes 3145732
  17.4 4.5 %collective-permute-start.9 = (f32[2048,128]{1,0:T(8,128)S(1)}, f32[2048,128]{1,0:T(8,128)S(1)}, u32[]{:S(2)}, u32[]{:S(2)}) collective-permute-start(f32[2048,128]{1,0:T(8,128)S(1)} %select_select_fusion.1), channel_id=1, source_target_pairs={{1,449},{2,450},{3,451},{4,452},{5,453},{6,454},{7,455},{8,456},{9... | collective-permute-start | bytes 3145736 | tf_op jit(solution)/shard_map/ppermute | solution.py:175
  18.1 3.8 %collective-permute-start.8 = (f32[2048,128]{1,0:T(8,128)S(1)}, f32[2048,128]{1,0:T(8,128)S(1)}, u32[]{:S(2)}, u32[]{:S(2)}) collective-permute-start(f32[2048,128]{1,0:T(8,128)S(1)} %select_select_fusion.1), channel_id=1, source_target_pairs={{1,65},{2,66},{3,67},{4,68},{5,69},{6,70},{7,71},{8,72},{9,73},{10... | collective-permute-start | bytes 3145736 | tf_op jit(solution)/shard_map/ppermute | solution.py:175
  18.8 1.0 copy-start.3
  19.8 0.8 copy-start.16
  20.6 1.2 copy-start.4
  21.9 8.5 %copy-start.11 = (f32[1024,128]{1,0:T(8,128)S(1)}, f32[1024,128]{1,0:T(8,128)}, u32[]{:S(2)}) copy-start(f32[1024,128]{1,0:T(8,128)} %copy-done.10) | copy-start | bytes 1572868
  21.9 1.0 copy-start.12
  22.8 1.2 copy-start.14
  24.0 4.0 %collective-permute-start.12 = (f32[384,128]{1,0:T(8,128)}, f32[384,128]{1,0:T(8,128)}, u32[]{:S(2)}, u32[]{:S(2)}) collective-permute-start(f32[384,128]{1,0:T(8,128)} %get-tuple-element.52), channel_id=1, source_target_pairs={{60,63}} | collective-permute-start | bytes 589832 | tf_op jit(solution)/shard_map/ppermute | solution.py:175
  25.4 2.7 %collective-permute-start.11 = (f32[384,128]{1,0:T(8,128)}, f32[384,128]{1,0:T(8,128)}, u32[]{:S(2)}, u32[]{:S(2)}) collective-permute-start(f32[384,128]{1,0:T(8,128)} %get-tuple-element.53), channel_id=1, source_target_pairs={{60,62}} | collective-permute-start | bytes 589832 | tf_op jit(solution)/shard_map/ppermute | solution.py:175
  26.7 1.3 collective-permute-start.10
  29.0 3.6 %collective-permute-start.14 = (f32[384,128]{1,0:T(8,128)S(1)}, f32[384,128]{1,0:T(8,128)S(1)}, u32[]{:S(2)}, u32[]{:S(2)}) collective-permute-start(f32[384,128]{1,0:T(8,128)S(1)} %select_select_fusion.8), channel_id=1, source_target_pairs={{60,252},{61,253},{62,254},{63,255}} | collective-permute-start | bytes 589832 | tf_op jit(solution)/shard_map/ppermute | solution.py:175
  29.7 3.0 %collective-permute-start.13 = (f32[384,128]{1,0:T(8,128)S(1)}, f32[384,128]{1,0:T(8,128)S(1)}, u32[]{:S(2)}, u32[]{:S(2)}) collective-permute-start(f32[384,128]{1,0:T(8,128)S(1)} %select_select_fusion.8), channel_id=1, source_target_pairs={{60,380},{61,381},{62,382},{63,383}} | collective-permute-start | bytes 589832 | tf_op jit(solution)/shard_map/ppermute | solution.py:175
  30.5 58.0 %collective-permute-start.18 = (f32[1024,128]{1,0:T(8,128)S(1)}, f32[1024,128]{1,0:T(8,128)S(1)}, u32[]{:S(2)}, u32[]{:S(2)}) collective-permute-start(f32[1024,128]{1,0:T(8,128)S(1)} %select_select_fusion.3), channel_id=1, source_target_pairs={{386,414},{387,415},{418,446},{419,447},{450,478},{451,479},{482,5... | collective-permute-start | bytes 1572872 | tf_op jit(solution)/shard_map/ppermute | solution.py:175
  31.2 57.3 %collective-permute-start.17 = (f32[1024,128]{1,0:T(8,128)S(1)}, f32[1024,128]{1,0:T(8,128)}, u32[]{:S(2)}, u32[]{:S(2)}) collective-permute-start(f32[1024,128]{1,0:T(8,128)S(1)} %select_select_fusion.3), channel_id=1, source_target_pairs={{2,6},{3,7},{34,38},{35,39},{66,70},{67,71},{98,102},{99,103},{128... | collective-permute-start | bytes 1572872 | tf_op jit(solution)/shard_map/ppermute | solution.py:175
  32.7 2.1 %collective-permute-start.16 = (f32[384,128]{1,0:T(8,128)S(1)}, f32[384,128]{1,0:T(8,128)S(1)}, u32[]{:S(2)}, u32[]{:S(2)}) collective-permute-start(f32[384,128]{1,0:T(8,128)S(1)} %select_select_fusion.7), channel_id=1, source_target_pairs={{60,124},{61,125},{62,126},{63,127},{252,316},{253,317},{254,318},... | collective-permute-start | bytes 589832 | tf_op jit(solution)/shard_map/ppermute | solution.py:175
  33.4 54.1 %collective-permute-start.15 = (f32[384,128]{1,0:T(8,128)S(1)}, f32[384,128]{1,0:T(8,128)}, u32[]{:S(2)}, u32[]{:S(2)}) collective-permute-start(f32[384,128]{1,0:T(8,128)S(1)} %select_select_fusion.7), channel_id=1, source_target_pairs={{60,508},{61,509},{62,510},{63,511},{252,188},{253,189},{254,190},... | collective-permute-start | bytes 589832 | tf_op jit(solution)/shard_map/ppermute | solution.py:175
  34.7 62.3 %copy-start.13 = (f32[2048,128]{1,0:T(8,128)S(1)}, f32[2048,128]{1,0:T(8,128)}, u32[]{:S(2)}) copy-start(f32[2048,128]{1,0:T(8,128)} %copy-done.12) | copy-start | bytes 3145732
  34.8 62.3 %copy-start.15 = (f32[2048,128]{1,0:T(8,128)S(1)}, f32[2048,128]{1,0:T(8,128)}, u32[]{:S(2)}) copy-start(f32[2048,128]{1,0:T(8,128)} %copy-done.14) | copy-start | bytes 3145732
  88.5 11.4 %collective-permute-start.20 = (f32[384,128]{1,0:T(8,128)S(1)}, f32[384,128]{1,0:T(8,128)S(1)}, u32[]{:S(2)}, u32[]{:S(2)}) collective-permute-start(f32[384,128]{1,0:T(8,128)S(1)} %select_select_fusion.6), channel_id=1, source_target_pairs={{60,40},{61,41},{62,42},{63,43},{124,104},{125,105},{126,106},{127... | collective-permute-start | bytes 589832 | tf_op jit(solution)/shard_map/ppermute | solution.py:175
  89.8 10.1 %collective-permute-start.19 = (f32[384,128]{1,0:T(8,128)S(1)}, f32[384,128]{1,0:T(8,128)S(1)}, u32[]{:S(2)}, u32[]{:S(2)}) collective-permute-start(f32[384,128]{1,0:T(8,128)S(1)} %select_select_fusion.6), channel_id=1, source_target_pairs={{60,48},{61,49},{62,50},{63,51},{124,112},{125,113},{126,114},{127... | collective-permute-start | bytes 589832 | tf_op jit(solution)/shard_map/ppermute | solution.py:175
  91.2 7.4 %copy-start.1 = (f32[1024,128]{1,0:T(8,128)}, f32[1024,128]{1,0:T(8,128)S(1)}, u32[]{:S(2)}) copy-start(f32[1024,128]{1,0:T(8,128)S(1)} %select_select_fusion.2.own_ref) | copy-start | bytes 1572868
  91.2 10.5 %collective-permute-start.22 = (f32[1024,128]{1,0:T(8,128)S(1)}, f32[1024,128]{1,0:T(8,128)S(1)}, u32[]{:S(2)}, u32[]{:S(2)}) collective-permute-start(f32[1024,128]{1,0:T(8,128)S(1)} %select_select_fusion.2.own_ref), channel_id=1, source_target_pairs={{0,3},{1,0},{2,1},{3,2},{4,7},{5,4},{6,5},{7,6},{8,11},{9,8},{10,9... | collective-permute-start | bytes 1572872 | tf_op jit(solution)/shard_map/ppermute | solution.py:175
  93.1 11.1 %collective-permute-start.21 = (f32[1024,128]{1,0:T(8,128)S(1)}, f32[1024,128]{1,0:T(8,128)S(1)}, u32[]{:S(2)}, u32[]{:S(2)}) collective-permute-start(f32[1024,128]{1,0:T(8,128)S(1)} %select_select_fusion.2.own_ref), channel_id=1, source_target_pairs={{0,1},{1,2},{2,3},{3,0},{4,5},{5,6},{6,7},{7,4},{8,9},{9,10},{10,1... | collective-permute-start | bytes 1572872 | tf_op jit(solution)/shard_map/ppermute | solution.py:175
  98.6 15.6 %collective-permute-start.27 = (f32[2048,128]{1,0:T(8,128)S(1)}, f32[2048,128]{1,0:T(8,128)}, u32[]{:S(2)}, u32[]{:S(2)}) collective-permute-start(f32[2048,128]{1,0:T(8,128)S(1)} %select_select_fusion.b_ref), channel_id=1, source_target_pairs={{0,32},{1,33},{2,34},{3,35},{4,36},{5,37},{6,38},{7,39},{8,40},{9,... | collective-permute-start | bytes 3145736 | tf_op jit(solution)/shard_map/ppermute | solution.py:175
  101.7 0.8 copy-start.5
  104.3 0.8 copy-start.7
  105.1 6.0 %collective-permute-start.24 = (f32[384,128]{1,0:T(8,128)S(1)}, f32[384,128]{1,0:T(8,128)S(1)}, u32[]{:S(2)}, u32[]{:S(2)}) collective-permute-start(f32[384,128]{1,0:T(8,128)S(1)} %select_select_fusion.5), channel_id=1, source_target_pairs={{60,32},{61,33},{62,34},{63,35},{124,96},{125,97},{126,98},{127,99... | collective-permute-start | bytes 589832 | tf_op jit(solution)/shard_map/ppermute | solution.py:175
  106.4 5.4 %collective-permute-start.23 = (f32[384,128]{1,0:T(8,128)S(1)}, f32[384,128]{1,0:T(8,128)}, u32[]{:S(2)}, u32[]{:S(2)}) collective-permute-start(f32[384,128]{1,0:T(8,128)S(1)} %select_select_fusion.5), channel_id=1, source_target_pairs={{60,56},{61,57},{62,58},{63,59},{124,120},{125,121},{126,122},{127... | collective-permute-start | bytes 589832 | tf_op jit(solution)/shard_map/ppermute | solution.py:175
  108.3 14.9 %collective-permute-start.26 = (f32[1024,128]{1,0:T(8,128)}, f32[1024,128]{1,0:T(8,128)}, u32[]{:S(2)}, u32[]{:S(2)}) collective-permute-start(f32[1024,128]{1,0:T(8,128)} %copy-done.7), channel_id=1, source_target_pairs={{0,1},{1,2},{2,3},{3,0},{4,5},{5,6},{6,7},{7,4},{8,9},{9,10},{10,1... | collective-permute-start | bytes 1572872 | tf_op jit(solution)/shard_map/ppermute | solution.py:175
  111.0 0.7 copy-start.17
  111.8 2.4 %collective-permute-start.25 = (f32[384,128]{1,0:T(8,128)S(1)}, f32[384,128]{1,0:T(8,128)S(1)}, u32[]{:S(2)}, u32[]{:S(2)}) collective-permute-start(f32[384,128]{1,0:T(8,128)S(1)} %select_select_fusion.4), channel_id=1, source_target_pairs={{32,0},{33,1},{34,2},{35,3},{36,4},{37,5},{38,6},{39,7},{40,8},{41... | collective-permute-start | bytes 589832 | tf_op jit(solution)/shard_map/ppermute | solution.py:175
  123.2 8.6 %collective-permute-start.28 = (f32[384,128]{1,0:T(8,128)S(1)}, f32[384,128]{1,0:T(8,128)S(1)}, u32[]{:S(2)}, u32[]{:S(2)}) collective-permute-start(f32[384,128]{1,0:T(8,128)S(1)} %broadcast_select_fusion.f0_ref), channel_id=1, source_target_pairs={{0,1},{1,2},{2,3},{3,0},{4,5},{5,6},{6,7},{7,4},{8,9},{9,10},{10,1... | collective-permute-start | bytes 589832 | tf_op jit(solution)/shard_map/ppermute | solution.py:175
  125.3 8.5 %collective-permute-start.29 = (f32[384,128]{1,0:T(8,128)S(1)}, f32[384,128]{1,0:T(8,128)S(1)}, u32[]{:S(2)}, u32[]{:S(2)}) collective-permute-start(f32[384,128]{1,0:T(8,128)S(1)} %broadcast_select_fusion.f0_ref), channel_id=1, source_target_pairs={{0,3},{1,0},{2,1},{3,2},{4,7},{5,4},{6,5},{7,6},{8,11},{9,8},{10,9... | collective-permute-start | bytes 589832 | tf_op jit(solution)/shard_map/ppermute | solution.py:175
  131.8 10.0 %collective-permute-start.30 = (f32[384,128]{1,0:T(8,128)S(1)}, f32[384,128]{1,0:T(8,128)S(1)}, u32[]{:S(2)}, u32[]{:S(2)}) collective-permute-start(f32[384,128]{1,0:T(8,128)S(1)} %collective-permute-done.28.f3_ref), channel_id=1, source_target_pairs={{0,1},{1,2},{2,3},{3,0},{4,5},{5,6},{6,7},{7,4},{8,9},{9,10},{10,1... | collective-permute-start | bytes 589832 | tf_op jit(solution)/shard_map/ppermute | solution.py:175
  141.8 1.0 copy-start.2
  142.8 1.0 copy-start.6
  143.9 1.0 copy-start.8

commit v5 on v3

--- a/solution.py
+++ b/solution.py
@@ -43,7 +43,6 @@
         for m in range(8):
             d = jnp.broadcast_to(cols[m][0][m : m + 1, :], (8, SB))
             r = lax.rsqrt(d)
-            r = r * (1.5 - (0.5 * d) * (r * r))
             lc = [c * r for c in cols[m]]
             ur = jnp.broadcast_to(top[m : m + 1, :], (8, SB)) * r
             er = jnp.broadcast_to(top_e[m : m + 1, :], (8, SB)) * r
@@ -109,12 +108,23 @@
     )(flag, a)
 
 
-def update_kernel(pos_ref, own_ref, left_ref, right_ref, opp_a_ref, opp_b_ref, b_ref, f_ref, cov_ref, out_ref, y_ref):
-    row, col, x = pos_ref[0], pos_ref[1], pos_ref[2]
+def update_kernel(
+    pos_ref, own_ref, left_ref, right_ref, opp_a_ref, opp_b_ref, b_ref, b_other_ref, f_ref, f_other_ref, cov_ref,
+    out_ref, y_ref, raw_ref, x_ref,
+):
+    row, col, x, core = pos_ref[0], pos_ref[1], pos_ref[2], pos_ref[3]
+    for shift, part, ref in ((0, 0, own_ref), (3, 0, left_ref), (1, 0, right_ref), (2, 0, opp_a_ref), (2, 1, opp_b_ref)):
+        count = ref.shape[0] // 4
+        first = lax.rem(x + shift, 4) * HB + part * count
+        raw_ref[pl.ds(pl.multiple_of(first, SB), count), :] = wide(ref, 0, count)
 
     def block(i):
         place = lax.rem(i // 3 - x + 4, 4)
-        return f_ref[pl.ds(pl.multiple_of(place * (3 * SB) + (i % 3) * SB, SB), SB), :]
+        rows = pl.ds(pl.multiple_of(place * (3 * SB) + (i % 3) * SB, SB), SB)
+        return jnp.where(core == 0, f_other_ref[rows, :], f_ref[rows, :])
+
+    def b_rows(first):
+        return jnp.where(core == 1, wide(b_other_ref, first, HB), wide(b_ref, first, HB))
 
     zero = jnp.zeros((SB, SB), jnp.float32)
 
@@ -126,48 +136,40 @@
     d0 = square(block(M0), zero, block(X10), block(M1))
     d1 = square(block(M2), zero, block(X32), block(M3))
     g = square(block(L20), block(L21), block(L30), block(L31))
-    y0 = nn(d0, wide(b_ref, 0, HB))
-    y_ref[0:HB, :] = y0
-    y_ref[HB:TB, :] = nn(d1, wide(b_ref, HB, HB) - nn(g, y0))
-
-    def piece(q, raw0, raw1):
-        x0 = nt(raw0, d0)
-        x1 = nt(raw1 - nt(x0, g), d1)
-        xs = jnp.concatenate([x0, x1], axis=1)
-        tile_row = row + ROWS * (q // 2)
-
-        @pl.when(col > 0)
-        def _():
-            cov = wide(cov_ref, q * HB, HB)
-            new = cov - nn(xs, y_ref[...])
-            put_wide(out_ref, q * HB, jnp.where(tile_row >= col, new, cov))
-
-        @pl.when(col == 0)
-        def _():
-            at_row = lax.rem(q, 2) * HB + lax.broadcasted_iota(jnp.int32, (HB, TB), 0)
-            above = lax.broadcasted_iota(jnp.int32, (HB, TB), 1) > at_row
-            put_wide(out_ref, q * HB, jnp.where(jnp.logical_and(tile_row == 0, above), 0.0, xs))
-
-    for shift, ref in ((0, own_ref), (3, left_ref), (1, right_ref)):
-        piece(lax.rem(x + shift, 4), wide(ref, 0, HB, 0, 2), wide(ref, 0, HB, 2, 4))
-    half = HB // 2
-    opp0 = jnp.concatenate([wide(opp_a_ref, 0, half, 0, 2), wide(opp_b_ref, 0, half, 0, 2)], axis=0)
-    opp1 = jnp.concatenate([wide(opp_a_ref, 0, half, 2, 4), wide(opp_b_ref, 0, half, 2, 4)], axis=0)
-    piece(lax.rem(x + 2, 4), opp0, opp1)
-
-
-def update(pos, own, left, right, opp_a, opp_b, b, f, cov):
+    x0 = nt(raw_ref[:, 0:HB], d0)
+    x_ref[:, 0:HB] = x0
+    x_ref[:, HB:TB] = nt(raw_ref[:, HB:TB] - nt(x0, g), d1)
+
+    @pl.when(col > 0)
+    def _():
+        y0 = nn(d0, b_rows(0))
+        y_ref[0:HB, :] = y0
+        y_ref[HB:TB, :] = nn(d1, b_rows(HB) - nn(g, y0))
+        prod = nn(x_ref[...], y_ref[...])
+        for half in range(2):
+            cov = wide(cov_ref, half * TB, TB)
+            new = cov - prod[half * TB : (half + 1) * TB]
+            put_wide(out_ref, half * TB, jnp.where(row + ROWS * half >= col, new, cov))
+
+    @pl.when(col == 0)
+    def _():
+        above = lax.broadcasted_iota(jnp.int32, (TB, TB), 1) > lax.broadcasted_iota(jnp.int32, (TB, TB), 0)
+        put_wide(out_ref, 0, jnp.where(jnp.logical_and(row == 0, above), 0.0, x_ref[0:TB, :]))
+        put_wide(out_ref, TB, x_ref[TB:, :])
+
+
+def update(*operands):
     vmem = pl.BlockSpec(memory_space=pltpu.VMEM)
     return pl.pallas_call(
         update_kernel,
         out_shape=jax.ShapeDtypeStruct((8 * TB, SB), jnp.float32),
-        in_specs=[pl.BlockSpec(memory_space=pltpu.SMEM)] + [vmem] * 8,
+        in_specs=[pl.BlockSpec(memory_space=pltpu.SMEM)] + [vmem] * (len(operands) - 1),
         out_specs=vmem,
-        scratch_shapes=[pltpu.VMEM((TB, TB), jnp.float32)],
+        scratch_shapes=[pltpu.VMEM((rows, TB), jnp.float32) for rows in (TB, 2 * TB, 2 * TB)],
         cost_estimate=pl.CostEstimate(flops=8_000_000_000, bytes_accessed=9_000_000, transcendentals=0),
         compiler_params=pltpu.CompilerParams(vmem_limit_bytes=40 * 1024 * 1024),
         name="update",
-    )(pos, own, left, right, opp_a, opp_b, b, f, cov)
+    )(*operands)
 
 
 def send(value, pairs):
@@ -184,6 +186,13 @@
 ROUNDS = (
     (((0, 3),), ((0, 5),)),
     (((0, 1), (3, 4), (5, 6)), ((0, 7), (3, 2))),
+)
+
+
+FEWER = (
+    (((0, 4),),),
+    (((0, 1), (4, 5)), ((0, 7), (4, 3))),
+    (((1, 2), (5, 6)),),
 )
 
 
@@ -265,43 +274,45 @@
     corner = send(b_tile, [(0, home)])
     quarter = [cov[quarter_rows * q : quarter_rows * (q + 1)] for q in range(4)]
     got = [send(quarter[q], scatter(q)) for q in (3, 2, 1)]
-    moved = ring_sends(b_tile, ROUNDS[0], along_y)
-    corner, got = tied(corner, got)
+    moved = ring_sends(b_tile, FEWER[0], along_y)
+    corner, got, moved = tied(corner, got, moved)
     own = by_x([quarter[0], got[2], got[1], got[0]])
     got = ring_sends(own, ROUNDS[0], along_z)
-
-    corner, got, moved = tied(corner, got, moved)
+    b_tile = ring_pick(b_tile, FEWER[0], y, moved)
+    moved = ring_sends(b_tile, FEWER[1], along_y)
+
+    corner, got = tied(corner, got)
+    f = factor_tile(flag, corner)
+    f, got, moved = tied(f, got, moved)
     own = ring_pick(own, ROUNDS[0], z, got)
     got = ring_sends(own, ROUNDS[1], along_z)
-    b_tile = ring_pick(b_tile, ROUNDS[0], y, moved)
-    moved = ring_sends(b_tile, ROUNDS[1], along_y)
-    f = factor_tile(flag, corner)
+    b_tile = ring_pick(b_tile, FEWER[1], y, moved)
+    moved = ring_sends(b_tile, FEWER[2], along_y)
 
     part = [f[3 * SB * q : 3 * SB * (q + 1)] for q in range(4)]
     mine = by_x([part[0]] + [send(part[q], [(home, home + q)]) for q in (1, 2, 3)])
     mine = ring_round(mine, ROUNDS[0], y, factor_y)
     mine = ring_round(mine, ROUNDS[1], y, factor_y)
 
-    mine, got = tied(mine, got)
+    mine, got, moved = tied(mine, got, moved)
+    b_tile = ring_pick(b_tile, FEWER[2], y, moved)
+    b_other = send(b_tile, across)
     own = ring_pick(own, ROUNDS[1], z, got)
     left = send(own, shift_x(1, (0, 1)))
     right = send(own, shift_x(-1, (0, 1)))
     mine = ring_round(mine, ROUNDS[0], home_z, factor_z)
 
-    mine, left, right, moved = tied(mine, left, right, moved)
-    b_tile = ring_pick(b_tile, ROUNDS[1], y, moved)
+    mine, left, right = tied(mine, left, right)
     opp_a = send(left[: quarter_rows // 2], shift_x(1, (0, 1)))
     opp_b = send(right[quarter_rows // 2 :], shift_x(-1, (0, 1)))
-    b_other = send(b_tile, across)
     mine = ring_round(mine, ROUNDS[1], home_z, factor_z)
 
     mine, opp_a, opp_b, b_other = tied(mine, opp_a, opp_b, b_other)
-    b_tile = jnp.where(core == 1, b_other, b_tile)
     turned = jnp.concatenate([mine] + [send(mine, shift_x(-by, (1,))) for by in (1, 2, 3)], axis=0)
-    turned = jnp.where(core == 0, send(turned, [(b, a) for a, b in across]), turned)
-
-    pos = jnp.stack([row, col, x, 0]).astype(jnp.int32)
-    out = update(pos, own, left, right, opp_a, opp_b, b_tile, turned, cov)
+    turned_other = send(turned, [(b, a) for a, b in across])
+
+    pos = jnp.stack([row, col, x, core]).astype(jnp.int32)
+    out = update(pos, own, left, right, opp_a, opp_b, b_tile, b_other, turned, turned_other, cov)
     return out.reshape(covariance.shape)
 
 

time: 152 us -> 143 us (0.941)
  the two profiles are of different devices: /device:TPU:185 before, /device:TPU:177 now
where the time goes in v5:
time: 143 us
  waiting for transfers between devices  59.8 us (42%)
  starting transfers between devices  48.4 us (34%)
  Pallas kernels  13.1 us (9%)
  local copies, waits for them, and re-layouts  11.1 us (8%)
  other arithmetic  9.77 us (7%)
    ppermute x32, waiting for transfers between devices, send(): return lax.ppermute(value, AXES, pairs)  59.8 us
    ppermute x32, starting transfers between devices, send(): return lax.ppermute(value, AXES, pairs)  48.4 us
    pallas_call x1, Pallas kernels, update(): pl.pallas_call(update_kernel, out_shape=jax.ShapeDtypeStruct((8 * TB, SB)...  12.9 us
    select_n x9, other arithmetic, ring_pick(): value = jnp.where(one_of(pos, [b for _, b in pairs]), received, value)  8.49 us
    slice x1, local copies, waits for them, and re-layouts, on_device(): b_tile = cov[0:4 * TB]  3.06 us
  transfers between devices with their start and end apart: 32, of which 6 were waited for; matrix products, arithmetic and copies ran while one was open for 10% of the time, Pallas kernels for 0%

profile of v5, /device:TPU:177, one launch (start us, length us, event | category | flops | bytes accessed | tf_op | source)
XLA Modules:
  0.0 142.5 jit_solution(2620808333915904304)
XLA Ops:
  0.0 3.1 %slice.36 = f32[1,512,1,512]{3,2,1,0:T(1,128)} slice(f32[2,512,1,512]{3,2,1,0:T(1,128)} %param.1), slice={[0:1], [0:512], [0:1], [0:512]} | slice | bytes 2097152 | tf_op jit(solution)/shard_map/slice | solution.py:273
  3.1 1.6 %collective-permute-start.4 = (f32[2048,128]{1,0:T(8,128)}, f32[2048,128]{1,0:T(8,128)}, u32[]{:S(2)}, u32[]{:S(2)}) collective-permute-start(f32[2048,128]{1,0:T(8,128)} %bitcast.5), channel_id=1, source_target_pairs={{1,257},{2,258},{3,259},{4,260},{5,261},{6,262},{7,263},{8,264},{9... | collective-permute-start | bytes 3145736 | tf_op jit(solution)/shard_map/ppermute | solution.py:176
  4.7 0.7 collective-permute-start
  5.4 1.2 fusion
  6.6 1.4 %collective-permute-start.3 = (f32[1024,128]{1,0:T(8,128)}, f32[1024,128]{1,0:T(8,128)}, u32[]{:S(2)}, u32[]{:S(2)}) collective-permute-start(f32[1024,128]{1,0:T(8,128)} %get-tuple-element.53), channel_id=1, source_target_pairs={{0,1},{32,33},{64,65},{96,97},{128,129},{160,161},{192,193},{224,2... | collective-permute-start | bytes 1572872 | tf_op jit(solution)/shard_map/ppermute | solution.py:176
  8.1 1.4 %collective-permute-start.2 = (f32[1024,128]{1,0:T(8,128)}, f32[1024,128]{1,0:T(8,128)}, u32[]{:S(2)}, u32[]{:S(2)}) collective-permute-start(f32[1024,128]{1,0:T(8,128)} %get-tuple-element.54), channel_id=1, source_target_pairs={{0,2},{32,34},{64,66},{96,98},{128,130},{160,162},{192,194},{224,2... | collective-permute-start | bytes 1572872 | tf_op jit(solution)/shard_map/ppermute | solution.py:176
  9.5 1.5 %collective-permute-start.1 = (f32[1024,128]{1,0:T(8,128)}, f32[1024,128]{1,0:T(8,128)}, u32[]{:S(2)}, u32[]{:S(2)}) collective-permute-start(f32[1024,128]{1,0:T(8,128)} %get-tuple-element.55), channel_id=1, source_target_pairs={{0,3},{32,35},{64,67},{96,99},{128,131},{160,163},{192,195},{224,2... | collective-permute-start | bytes 1572872 | tf_op jit(solution)/shard_map/ppermute | solution.py:176
  11.0 0.0 collective-permute-done.4
  11.0 0.0 collective-permute-done.a_ref
  11.0 1.2 slice_select_fusion
  12.2 0.7 collective-permute-start.6
  12.9 0.7 collective-permute-start.5
  13.6 1.4 broadcast_select_fusion.1
  14.9 0.7 collective-permute-start.8
  15.7 0.7 collective-permute-start.7
  16.4 0.0 collective-permute-done.6
  16.4 0.2 factor.1
  16.7 0.0 collective-permute-done.7
  16.7 0.7 collective-permute-start.11
  17.4 0.7 collective-permute-start.10
  18.1 0.7 collective-permute-start.9
  18.8 0.1 select_select_fusion
  18.9 0.0 copy-start.1
  18.9 1.6 %collective-permute-start.18 = (f32[2048,128]{1,0:T(8,128)S(1)}, f32[2048,128]{1,0:T(8,128)}, u32[]{:S(2)}, u32[]{:S(2)}) collective-permute-start(f32[2048,128]{1,0:T(8,128)S(1)} %select_select_fusion), channel_id=1, source_target_pairs={{65,129},{66,130},{67,131},{68,132},{69,133},{70,134},{71,135},{72... | collective-permute-start | bytes 3145736 | tf_op jit(solution)/shard_map/ppermute | solution.py:176
  20.6 0.7 collective-permute-start.13
  21.3 0.7 collective-permute-start.12
  22.0 0.9 select_select_fusion.2
  22.9 1.3 collective-permute-start.17
  24.2 1.5 %collective-permute-start.16 = (f32[1024,128]{1,0:T(8,128)}, f32[1024,128]{1,0:T(8,128)}, u32[]{:S(2)}, u32[]{:S(2)}) collective-permute-start(f32[1024,128]{1,0:T(8,128)} %select_select_fusion.2), channel_id=1, source_target_pairs={{2,6},{3,7},{34,38},{35,39},{66,70},{67,71},{98,102},{99,103},{128... | collective-permute-start | bytes 1572872 | tf_op jit(solution)/shard_map/ppermute | solution.py:176
  25.7 0.7 collective-permute-start.15
  26.4 1.4 collective-permute-start.14
  27.7 0.7 copy-done.2
  28.4 1.0 select_select_fusion.5
  29.4 34.1 %collective-permute-done.17 = f32[1024,128]{1,0:T(8,128)} collective-permute-done((f32[1024,128]{1,0:T(8,128)}, f32[1024,128]{1,0:T(8,128)}, u32[]{:S(2)}, u32[]{:S(2)}) %collective-permute-start.17) | collective-permute-done | bytes 524320 | tf_op jit(solution)/shard_map/ppermute | solution.py:176
  63.5 1.3 broadcast_select_fusion.b_ref
  64.9 1.3 collective-permute-start.27
  66.2 2.1 %select_select_fusion.1.own_ref = f32[1024,128]{1,0:T(8,128)} fusion(f32[1024,128]{1,0:T(8,128)} %collective-permute-done.17, f32[1024,128]{1,0:T(8,128)} %collective-permute-done.16, f32[1024,128]{1,0:T(8,128)} %select_select_fusion.2, pred[]{:T(512)S(6)} %or.43, pred[]{:T(512)S(6)} %or.36), kind=kLoop, calls=%fused_computation.2 | loop fusion | flops 262144 | bytes 2097154 | tf_op jit(solution)/shard_map/jit(_where)/select_n | solution.py:205
  68.3 1.9 %collective-permute-start.22 = (f32[1024,128]{1,0:T(8,128)}, f32[1024,128]{1,0:T(8,128)}, u32[]{:S(2)}, u32[]{:S(2)}) collective-permute-start(f32[1024,128]{1,0:T(8,128)} %select_select_fusion.1.own_ref), channel_id=1, source_target_pairs={{0,3},{1,0},{2,1},{3,2},{4,7},{5,4},{6,5},{7,6},{8,11},{9,8},{10,9... | collective-permute-start | bytes 1572872 | tf_op jit(solution)/shard_map/ppermute | solution.py:176
  70.2 3.4 %collective-permute-start.21 = (f32[1024,128]{1,0:T(8,128)}, f32[1024,128]{1,0:T(8,128)}, u32[]{:S(2)}, u32[]{:S(2)}) collective-permute-start(f32[1024,128]{1,0:T(8,128)} %select_select_fusion.1.own_ref), channel_id=1, source_target_pairs={{0,1},{1,2},{2,3},{3,0},{4,5},{5,6},{6,7},{7,4},{8,9},{9,10},{10,1... | collective-permute-start | bytes 1572872 | tf_op jit(solution)/shard_map/ppermute | solution.py:176
  73.6 1.3 collective-permute-start.20
  74.9 1.4 collective-permute-start.19
  76.2 12.5 %collective-permute-done.20 = f32[384,128]{1,0:T(8,128)S(1)} collective-permute-done((f32[384,128]{1,0:T(8,128)S(1)}, f32[384,128]{1,0:T(8,128)S(1)}, u32[]{:S(2)}, u32[]{:S(2)}) %collective-permute-start.20) | collective-permute-done | bytes 196640 | tf_op jit(solution)/shard_map/ppermute | solution.py:176
  88.7 0.7 select_select_fusion.4
  89.4 2.0 %collective-permute-start.24 = (f32[384,128]{1,0:T(8,128)}, f32[384,128]{1,0:T(8,128)}, u32[]{:S(2)}, u32[]{:S(2)}) collective-permute-start(f32[384,128]{1,0:T(8,128)} %select_select_fusion.4), channel_id=1, source_target_pairs={{60,32},{61,33},{62,34},{63,35},{124,96},{125,97},{126,98},{127,99... | collective-permute-start | bytes 589832 | tf_op jit(solution)/shard_map/ppermute | solution.py:176
  91.4 2.0 %collective-permute-start.23 = (f32[384,128]{1,0:T(8,128)}, f32[384,128]{1,0:T(8,128)}, u32[]{:S(2)}, u32[]{:S(2)}) collective-permute-start(f32[384,128]{1,0:T(8,128)} %select_select_fusion.4), channel_id=1, source_target_pairs={{60,56},{61,57},{62,58},{63,59},{124,120},{125,121},{126,122},{127... | collective-permute-start | bytes 589832 | tf_op jit(solution)/shard_map/ppermute | solution.py:176
  93.4 1.7 %slice.46 = f32[512,128]{1,0:T(8,128)} slice(f32[1024,128]{1,0:T(8,128)} %collective-permute-done.21.left_ref), slice={[0:512], [0:128]} | slice | bytes 524288 | tf_op jit(solution)/shard_map/slice | solution.py:306
  95.1 1.7 %slice.47 = f32[512,128]{1,0:T(8,128)} slice(f32[1024,128]{1,0:T(8,128)} %collective-permute-done.22.right_ref), slice={[512:1024], [0:128]} | slice | bytes 524288 | tf_op jit(solution)/shard_map/slice | solution.py:307
  96.7 4.6 %collective-permute-start.26 = (f32[512,128]{1,0:T(8,128)}, f32[512,128]{1,0:T(8,128)S(1)}, u32[]{:S(2)}, u32[]{:S(2)}) collective-permute-start(f32[512,128]{1,0:T(8,128)} %slice.47), channel_id=1, source_target_pairs={{0,3},{1,0},{2,1},{3,2},{4,7},{5,4},{6,5},{7,6},{8,11},{9,8},{10,9... | collective-permute-start | bytes 786440 | tf_op jit(solution)/shard_map/ppermute | solution.py:176
  101.3 1.9 %collective-permute-start.25 = (f32[512,128]{1,0:T(8,128)}, f32[512,128]{1,0:T(8,128)}, u32[]{:S(2)}, u32[]{:S(2)}) collective-permute-start(f32[512,128]{1,0:T(8,128)} %slice.46), channel_id=1, source_target_pairs={{0,1},{1,2},{2,3},{3,0},{4,5},{5,6},{6,7},{7,4},{8,9},{9,10},{10,1... | collective-permute-start | bytes 786440 | tf_op jit(solution)/shard_map/ppermute | solution.py:176
  103.3 1.0 select_select_fusion.3
  104.2 2.7 %collective-permute-done.26.opp_b_ref = f32[512,128]{1,0:T(8,128)S(1)} collective-permute-done((f32[512,128]{1,0:T(8,128)}, f32[512,128]{1,0:T(8,128)S(1)}, u32[]{:S(2)}, u32[]{:S(2)}) %collective-permute-start.26) | collective-permute-done | bytes 262176 | tf_op jit(solution)/shard_map/ppermute | solution.py:176
  106.9 4.6 %collective-permute-done.25.opp_a_ref = f32[512,128]{1,0:T(8,128)} collective-permute-done((f32[512,128]{1,0:T(8,128)}, f32[512,128]{1,0:T(8,128)}, u32[]{:S(2)}, u32[]{:S(2)}) %collective-permute-start.25) | collective-permute-done | bytes 262176 | tf_op jit(solution)/shard_map/ppermute | solution.py:176
  111.5 1.9 %collective-permute-start.28 = (f32[384,128]{1,0:T(8,128)S(1)}, f32[384,128]{1,0:T(8,128)S(1)}, u32[]{:S(2)}, u32[]{:S(2)}) collective-permute-start(f32[384,128]{1,0:T(8,128)S(1)} %select_select_fusion.3), channel_id=1, source_target_pairs={{32,35},{33,32},{34,33},{35,34},{36,39},{37,36},{38,37},{39,38},{4... | collective-permute-start | bytes 589832 | tf_op jit(solution)/shard_map/ppermute | solution.py:176
  113.4 3.4 %collective-permute-start.30 = (f32[384,128]{1,0:T(8,128)S(1)}, f32[384,128]{1,0:T(8,128)S(1)}, u32[]{:S(2)}, u32[]{:S(2)}) collective-permute-start(f32[384,128]{1,0:T(8,128)S(1)} %select_select_fusion.3), channel_id=1, source_target_pairs={{32,33},{33,34},{34,35},{35,32},{36,37},{37,38},{38,39},{39,36},{4... | collective-permute-start | bytes 589832 | tf_op jit(solution)/shard_map/ppermute | solution.py:176
  116.8 1.9 %collective-permute-start.29 = (f32[384,128]{1,0:T(8,128)S(1)}, f32[384,128]{1,0:T(8,128)S(1)}, u32[]{:S(2)}, u32[]{:S(2)}) collective-permute-start(f32[384,128]{1,0:T(8,128)S(1)} %select_select_fusion.3), channel_id=1, source_target_pairs={{32,34},{33,35},{34,32},{35,33},{36,38},{37,39},{38,36},{39,37},{4... | collective-permute-start | bytes 589832 | tf_op jit(solution)/shard_map/ppermute | solution.py:176
  118.7 0.7 constant_dynamic-update-slice_fusion.3
  119.4 0.7 constant_dynamic-update-slice_fusion.2
  120.1 4.6 %collective-permute-done.29 = f32[384,128]{1,0:T(8,128)S(1)} collective-permute-done((f32[384,128]{1,0:T(8,128)S(1)}, f32[384,128]{1,0:T(8,128)S(1)}, u32[]{:S(2)}, u32[]{:S(2)}) %collective-permute-start.29) | collective-permute-done | bytes 196640 | tf_op jit(solution)/shard_map/ppermute | solution.py:176
  124.7 0.7 constant_dynamic-update-slice_fusion.1
  125.4 0.7 constant_dynamic-update-slice_fusion.f_ref
  126.1 2.2 %collective-permute-start.31 = (f32[1536,128]{1,0:T(8,128)}, f32[1536,128]{1,0:T(8,128)}, u32[]{:S(2)}, u32[]{:S(2)}) collective-permute-start(f32[1536,128]{1,0:T(8,128)} %constant_dynamic-update-slice_fusion.f_ref), channel_id=1, source_target_pairs={{32,0},{33,1},{34,2},{35,3},{36,4},{37,5},{38,6},{39,7},{40,8},{41... | collective-permute-start | bytes 2359304 | tf_op jit(solution)/shard_map/ppermute | solution.py:176
  128.3 0.1 pad_add_fusion.pos_ref
  128.3 1.3 collective-permute-done.31.f_other_ref
  129.6 12.9 %update.1 = f32[4096,128]{1,0:T(8,128)} custom-call(s32[4]{0:T(128)S(1)} %pad_add_fusion.pos_ref, f32[1024,128]{1,0:T(8,128)} %select_select_fusion.1.own_ref, f32[1024,128]{1,0:T(8,128)} %collective-permute-done.21.left_ref, f32[1024,128]{1,0:T(8,128)} %collective-permute-done.22.right_ref, f32[512,128]{1,0:T(8,128)} %collective-permute-done.25.opp_a_ref, ...), custom_call_target="tpu_custom_call" | custom-call | flops 8000000000 | bytes 9000000 | tf_op jit(solution)/shard_map/update/pallas_call | solution.py:163
  (29 shorter events, 0.2 us)
Async XLA Ops:
  0.0 5.4 %copy-start = (f32[2,512,1,512]{3,2,1,0:T(1,128)S(1)}, f32[2,512,1,512]{3,2,1,0:T(1,128)}, u32[]{:S(2)}) copy-start(f32[2,512,1,512]{3,2,1,0:T(1,128)} %param.1) | copy-start | bytes 6291460
  3.1 7.9 %collective-permute-start.4 = (f32[2048,128]{1,0:T(8,128)}, f32[2048,128]{1,0:T(8,128)}, u32[]{:S(2)}, u32[]{:S(2)}) collective-permute-start(f32[2048,128]{1,0:T(8,128)} %bitcast.5), channel_id=1, source_target_pairs={{1,257},{2,258},{3,259},{4,260},{5,261},{6,262},{7,263},{8,264},{9... | collective-permute-start | bytes 3145736 | tf_op jit(solution)/shard_map/ppermute | solution.py:176
  4.7 6.3 %collective-permute-start = (f32[2048,128]{1,0:T(8,128)}, f32[2048,128]{1,0:T(8,128)S(1)}, u32[]{:S(2)}, u32[]{:S(2)}) collective-permute-start(f32[2048,128]{1,0:T(8,128)} %bitcast.5), channel_id=1, source_target_pairs={{0,60}} | collective-permute-start | bytes 3145736 | tf_op jit(solution)/shard_map/ppermute | solution.py:176
  6.6 4.4 %collective-permute-start.3 = (f32[1024,128]{1,0:T(8,128)}, f32[1024,128]{1,0:T(8,128)}, u32[]{:S(2)}, u32[]{:S(2)}) collective-permute-start(f32[1024,128]{1,0:T(8,128)} %get-tuple-element.53), channel_id=1, source_target_pairs={{0,1},{32,33},{64,65},{96,97},{128,129},{160,161},{192,193},{224,2... | collective-permute-start | bytes 1572872 | tf_op jit(solution)/shard_map/ppermute | solution.py:176
  8.1 2.9 %collective-permute-start.2 = (f32[1024,128]{1,0:T(8,128)}, f32[1024,128]{1,0:T(8,128)}, u32[]{:S(2)}, u32[]{:S(2)}) collective-permute-start(f32[1024,128]{1,0:T(8,128)} %get-tuple-element.54), channel_id=1, source_target_pairs={{0,2},{32,34},{64,66},{96,98},{128,130},{160,162},{192,194},{224,2... | collective-permute-start | bytes 1572872 | tf_op jit(solution)/shard_map/ppermute | solution.py:176
  9.5 1.5 %collective-permute-start.1 = (f32[1024,128]{1,0:T(8,128)}, f32[1024,128]{1,0:T(8,128)}, u32[]{:S(2)}, u32[]{:S(2)}) collective-permute-start(f32[1024,128]{1,0:T(8,128)} %get-tuple-element.55), channel_id=1, source_target_pairs={{0,3},{32,35},{64,67},{96,99},{128,131},{160,163},{192,195},{224,2... | collective-permute-start | bytes 1572872 | tf_op jit(solution)/shard_map/ppermute | solution.py:176
  12.2 4.2 %collective-permute-start.6 = (f32[1024,128]{1,0:T(8,128)S(1)}, f32[1024,128]{1,0:T(8,128)S(1)}, u32[]{:S(2)}, u32[]{:S(2)}) collective-permute-start(f32[1024,128]{1,0:T(8,128)S(1)} %slice_select_fusion), channel_id=1, source_target_pairs={{130,150},{131,151},{162,182},{163,183},{194,214},{195,215},{226,2... | collective-permute-start | bytes 1572872 | tf_op jit(solution)/shard_map/ppermute | solution.py:176
  12.9 3.5 %collective-permute-start.5 = (f32[1024,128]{1,0:T(8,128)S(1)}, f32[1024,128]{1,0:T(8,128)S(1)}, u32[]{:S(2)}, u32[]{:S(2)}) collective-permute-start(f32[1024,128]{1,0:T(8,128)S(1)} %slice_select_fusion), channel_id=1, source_target_pairs={{2,14},{3,15},{34,46},{35,47},{66,78},{67,79},{98,110},{99,111},{1... | collective-permute-start | bytes 1572872 | tf_op jit(solution)/shard_map/ppermute | solution.py:176
  14.9 1.7 %collective-permute-start.8 = (f32[2048,128]{1,0:T(8,128)S(1)}, f32[2048,128]{1,0:T(8,128)S(1)}, u32[]{:S(2)}, u32[]{:S(2)}) collective-permute-start(f32[2048,128]{1,0:T(8,128)S(1)} %broadcast_select_fusion.1), channel_id=1, source_target_pairs={{1,449},{2,450},{3,451},{4,452},{5,453},{6,454},{7,455},{8,456},{9... | collective-permute-start | bytes 3145736 | tf_op jit(solution)/shard_map/ppermute | solution.py:176
  15.7 1.0 collective-permute-start.7
  16.7 3.9 %collective-permute-start.11 = (f32[384,128]{1,0:T(8,128)S(1)}, f32[384,128]{1,0:T(8,128)S(1)}, u32[]{:S(2)}, u32[]{:S(2)}) collective-permute-start(f32[384,128]{1,0:T(8,128)S(1)} %get-tuple-element.56), channel_id=1, source_target_pairs={{60,63}} | collective-permute-start | bytes 589832 | tf_op jit(solution)/shard_map/ppermute | solution.py:176
  17.4 3.2 %collective-permute-start.10 = (f32[384,128]{1,0:T(8,128)S(1)}, f32[384,128]{1,0:T(8,128)S(1)}, u32[]{:S(2)}, u32[]{:S(2)}) collective-permute-start(f32[384,128]{1,0:T(8,128)S(1)} %get-tuple-element.57), channel_id=1, source_target_pairs={{60,62}} | collective-permute-start | bytes 589832 | tf_op jit(solution)/shard_map/ppermute | solution.py:176
  18.1 2.5 %collective-permute-start.9 = (f32[384,128]{1,0:T(8,128)S(1)}, f32[384,128]{1,0:T(8,128)S(1)}, u32[]{:S(2)}, u32[]{:S(2)}) collective-permute-start(f32[384,128]{1,0:T(8,128)S(1)} %get-tuple-element.58), channel_id=1, source_target_pairs={{60,61}} | collective-permute-start | bytes 589832 | tf_op jit(solution)/shard_map/ppermute | solution.py:176
  18.9 10.4 %copy-start.1 = (f32[2048,128]{1,0:T(8,128)}, f32[2048,128]{1,0:T(8,128)S(1)}, u32[]{:S(2)}) copy-start(f32[2048,128]{1,0:T(8,128)S(1)} %select_select_fusion) | copy-start | bytes 3145732
  18.9 44.6 %collective-permute-start.18 = (f32[2048,128]{1,0:T(8,128)S(1)}, f32[2048,128]{1,0:T(8,128)}, u32[]{:S(2)}, u32[]{:S(2)}) collective-permute-start(f32[2048,128]{1,0:T(8,128)S(1)} %select_select_fusion), channel_id=1, source_target_pairs={{65,129},{66,130},{67,131},{68,132},{69,133},{70,134},{71,135},{72... | collective-permute-start | bytes 3145736 | tf_op jit(solution)/shard_map/ppermute | solution.py:176
  20.6 5.0 %collective-permute-start.13 = (f32[384,128]{1,0:T(8,128)S(1)}, f32[384,128]{1,0:T(8,128)S(1)}, u32[]{:S(2)}, u32[]{:S(2)}) collective-permute-start(f32[384,128]{1,0:T(8,128)S(1)} %select_select_fusion.7), channel_id=1, source_target_pairs={{60,252},{61,253},{62,254},{63,255}} | collective-permute-start | bytes 589832 | tf_op jit(solution)/shard_map/ppermute | solution.py:176
  21.3 4.3 %collective-permute-start.12 = (f32[384,128]{1,0:T(8,128)S(1)}, f32[384,128]{1,0:T(8,128)S(1)}, u32[]{:S(2)}, u32[]{:S(2)}) collective-permute-start(f32[384,128]{1,0:T(8,128)S(1)} %select_select_fusion.7), channel_id=1, source_target_pairs={{60,380},{61,381},{62,382},{63,383}} | collective-permute-start | bytes 589832 | tf_op jit(solution)/shard_map/ppermute | solution.py:176
  22.9 40.6 %collective-permute-start.17 = (f32[1024,128]{1,0:T(8,128)}, f32[1024,128]{1,0:T(8,128)}, u32[]{:S(2)}, u32[]{:S(2)}) collective-permute-start(f32[1024,128]{1,0:T(8,128)} %select_select_fusion.2), channel_id=1, source_target_pairs={{386,414},{387,415},{418,446},{419,447},{450,478},{451,479},{482,5... | collective-permute-start | bytes 1572872 | tf_op jit(solution)/shard_map/ppermute | solution.py:176
  24.2 39.3 %collective-permute-start.16 = (f32[1024,128]{1,0:T(8,128)}, f32[1024,128]{1,0:T(8,128)}, u32[]{:S(2)}, u32[]{:S(2)}) collective-permute-start(f32[1024,128]{1,0:T(8,128)} %select_select_fusion.2), channel_id=1, source_target_pairs={{2,6},{3,7},{34,38},{35,39},{66,70},{67,71},{98,102},{99,103},{128... | collective-permute-start | bytes 1572872 | tf_op jit(solution)/shard_map/ppermute | solution.py:176
  25.7 2.0 %collective-permute-start.15 = (f32[384,128]{1,0:T(8,128)S(1)}, f32[384,128]{1,0:T(8,128)S(1)}, u32[]{:S(2)}, u32[]{:S(2)}) collective-permute-start(f32[384,128]{1,0:T(8,128)S(1)} %select_select_fusion.6), channel_id=1, source_target_pairs={{60,124},{61,125},{62,126},{63,127},{252,316},{253,317},{254,318},... | collective-permute-start | bytes 589832 | tf_op jit(solution)/shard_map/ppermute | solution.py:176
  26.4 2.0 %collective-permute-start.14 = (f32[384,128]{1,0:T(8,128)S(1)}, f32[384,128]{1,0:T(8,128)}, u32[]{:S(2)}, u32[]{:S(2)}) collective-permute-start(f32[384,128]{1,0:T(8,128)S(1)} %select_select_fusion.6), channel_id=1, source_target_pairs={{60,508},{61,509},{62,510},{63,511},{252,188},{253,189},{254,190},... | collective-permute-start | bytes 589832 | tf_op jit(solution)/shard_map/ppermute | solution.py:176
  27.7 0.7 copy-start.2
  64.9 46.6 %collective-permute-start.27 = (f32[2048,128]{1,0:T(8,128)S(1)}, f32[2048,128]{1,0:T(8,128)}, u32[]{:S(2)}, u32[]{:S(2)}) collective-permute-start(f32[2048,128]{1,0:T(8,128)S(1)} %broadcast_select_fusion.b_ref), channel_id=1, source_target_pairs={{0,32},{1,33},{2,34},{3,35},{4,36},{5,37},{6,38},{7,39},{8,40},{9,... | collective-permute-start | bytes 3145736 | tf_op jit(solution)/shard_map/ppermute | solution.py:176
  68.3 21.2 %collective-permute-start.22 = (f32[1024,128]{1,0:T(8,128)}, f32[1024,128]{1,0:T(8,128)}, u32[]{:S(2)}, u32[]{:S(2)}) collective-permute-start(f32[1024,128]{1,0:T(8,128)} %select_select_fusion.1.own_ref), channel_id=1, source_target_pairs={{0,3},{1,0},{2,1},{3,2},{4,7},{5,4},{6,5},{7,6},{8,11},{9,8},{10,9... | collective-permute-start | bytes 1572872 | tf_op jit(solution)/shard_map/ppermute | solution.py:176
  70.2 19.3 %collective-permute-start.21 = (f32[1024,128]{1,0:T(8,128)}, f32[1024,128]{1,0:T(8,128)}, u32[]{:S(2)}, u32[]{:S(2)}) collective-permute-start(f32[1024,128]{1,0:T(8,128)} %select_select_fusion.1.own_ref), channel_id=1, source_target_pairs={{0,1},{1,2},{2,3},{3,0},{4,5},{5,6},{6,7},{7,4},{8,9},{9,10},{10,1... | collective-permute-start | bytes 1572872 | tf_op jit(solution)/shard_map/ppermute | solution.py:176
  73.6 15.2 %collective-permute-start.20 = (f32[384,128]{1,0:T(8,128)S(1)}, f32[384,128]{1,0:T(8,128)S(1)}, u32[]{:S(2)}, u32[]{:S(2)}) collective-permute-start(f32[384,128]{1,0:T(8,128)S(1)} %select_select_fusion.5), channel_id=1, source_target_pairs={{60,40},{61,41},{62,42},{63,43},{124,104},{125,105},{126,106},{127... | collective-permute-start | bytes 589832 | tf_op jit(solution)/shard_map/ppermute | solution.py:176
  74.9 13.9 %collective-permute-start.19 = (f32[384,128]{1,0:T(8,128)S(1)}, f32[384,128]{1,0:T(8,128)}, u32[]{:S(2)}, u32[]{:S(2)}) collective-permute-start(f32[384,128]{1,0:T(8,128)S(1)} %select_select_fusion.5), channel_id=1, source_target_pairs={{60,48},{61,49},{62,50},{63,51},{124,112},{125,113},{126,114},{127... | collective-permute-start | bytes 589832 | tf_op jit(solution)/shard_map/ppermute | solution.py:176
  89.4 13.8 %collective-permute-start.24 = (f32[384,128]{1,0:T(8,128)}, f32[384,128]{1,0:T(8,128)}, u32[]{:S(2)}, u32[]{:S(2)}) collective-permute-start(f32[384,128]{1,0:T(8,128)} %select_select_fusion.4), channel_id=1, source_target_pairs={{60,32},{61,33},{62,34},{63,35},{124,96},{125,97},{126,98},{127,99... | collective-permute-start | bytes 589832 | tf_op jit(solution)/shard_map/ppermute | solution.py:176
  91.4 11.9 %collective-permute-start.23 = (f32[384,128]{1,0:T(8,128)}, f32[384,128]{1,0:T(8,128)}, u32[]{:S(2)}, u32[]{:S(2)}) collective-permute-start(f32[384,128]{1,0:T(8,128)} %select_select_fusion.4), channel_id=1, source_target_pairs={{60,56},{61,57},{62,58},{63,59},{124,120},{125,121},{126,122},{127... | collective-permute-start | bytes 589832 | tf_op jit(solution)/shard_map/ppermute | solution.py:176
  96.7 10.2 %collective-permute-start.26 = (f32[512,128]{1,0:T(8,128)}, f32[512,128]{1,0:T(8,128)S(1)}, u32[]{:S(2)}, u32[]{:S(2)}) collective-permute-start(f32[512,128]{1,0:T(8,128)} %slice.47), channel_id=1, source_target_pairs={{0,3},{1,0},{2,1},{3,2},{4,7},{5,4},{6,5},{7,6},{8,11},{9,8},{10,9... | collective-permute-start | bytes 786440 | tf_op jit(solution)/shard_map/ppermute | solution.py:176
  101.3 10.2 %collective-permute-start.25 = (f32[512,128]{1,0:T(8,128)}, f32[512,128]{1,0:T(8,128)}, u32[]{:S(2)}, u32[]{:S(2)}) collective-permute-start(f32[512,128]{1,0:T(8,128)} %slice.46), channel_id=1, source_target_pairs={{0,1},{1,2},{2,3},{3,0},{4,5},{5,6},{6,7},{7,4},{8,9},{9,10},{10,1... | collective-permute-start | bytes 786440 | tf_op jit(solution)/shard_map/ppermute | solution.py:176
  111.5 7.9 %collective-permute-start.28 = (f32[384,128]{1,0:T(8,128)S(1)}, f32[384,128]{1,0:T(8,128)S(1)}, u32[]{:S(2)}, u32[]{:S(2)}) collective-permute-start(f32[384,128]{1,0:T(8,128)S(1)} %select_select_fusion.3), channel_id=1, source_target_pairs={{32,35},{33,32},{34,33},{35,34},{36,39},{37,36},{38,37},{39,38},{4... | collective-permute-start | bytes 589832 | tf_op jit(solution)/shard_map/ppermute | solution.py:176
  113.4 12.0 %collective-permute-start.30 = (f32[384,128]{1,0:T(8,128)S(1)}, f32[384,128]{1,0:T(8,128)S(1)}, u32[]{:S(2)}, u32[]{:S(2)}) collective-permute-start(f32[384,128]{1,0:T(8,128)S(1)} %select_select_fusion.3), channel_id=1, source_target_pairs={{32,33},{33,34},{34,35},{35,32},{36,37},{37,38},{38,39},{39,36},{4... | collective-permute-start | bytes 589832 | tf_op jit(solution)/shard_map/ppermute | solution.py:176
  116.8 7.9 %collective-permute-start.29 = (f32[384,128]{1,0:T(8,128)S(1)}, f32[384,128]{1,0:T(8,128)S(1)}, u32[]{:S(2)}, u32[]{:S(2)}) collective-permute-start(f32[384,128]{1,0:T(8,128)S(1)} %select_select_fusion.3), channel_id=1, source_target_pairs={{32,34},{33,35},{34,32},{35,33},{36,38},{37,39},{38,36},{39,37},{4... | collective-permute-start | bytes 589832 | tf_op jit(solution)/shard_map/ppermute | solution.py:176
  126.1 3.5 %collective-permute-start.31 = (f32[1536,128]{1,0:T(8,128)}, f32[1536,128]{1,0:T(8,128)}, u32[]{:S(2)}, u32[]{:S(2)}) collective-permute-start(f32[1536,128]{1,0:T(8,128)} %constant_dynamic-update-slice_fusion.f_ref), channel_id=1, source_target_pairs={{32,0},{33,1},{34,2},{35,3},{36,4},{37,5},{38,6},{39,7},{40,8},{41... | collective-permute-start | bytes 2359304 | tf_op jit(solution)/shard_map/ppermute | solution.py:176

commit v6 on v5

--- a/solution.py
+++ b/solution.py
@@ -109,14 +109,13 @@
 
 
 def update_kernel(
-    pos_ref, own_ref, left_ref, right_ref, opp_a_ref, opp_b_ref, b_ref, b_other_ref, f_ref, f_other_ref, cov_ref,
+    pos_ref, own_ref, left_ref, right_ref, opp_ref, b_ref, b_other_ref, f_ref, f_other_ref, cov_ref,
     out_ref, y_ref, raw_ref, x_ref,
 ):
     row, col, x, core = pos_ref[0], pos_ref[1], pos_ref[2], pos_ref[3]
-    for shift, part, ref in ((0, 0, own_ref), (3, 0, left_ref), (1, 0, right_ref), (2, 0, opp_a_ref), (2, 1, opp_b_ref)):
-        count = ref.shape[0] // 4
-        first = lax.rem(x + shift, 4) * HB + part * count
-        raw_ref[pl.ds(pl.multiple_of(first, SB), count), :] = wide(ref, 0, count)
+    for shift, ref in ((0, own_ref), (3, left_ref), (1, right_ref), (2, opp_ref)):
+        first = lax.rem(x + shift, 4) * HB
+        raw_ref[pl.ds(pl.multiple_of(first, HB), HB), :] = wide(ref, 0, HB)
 
     def block(i):
         place = lax.rem(i // 3 - x + 4, 4)
@@ -295,24 +294,21 @@
     mine = ring_round(mine, ROUNDS[1], y, factor_y)
 
     mine, got, moved = tied(mine, got, moved)
-    b_tile = ring_pick(b_tile, FEWER[2], y, moved)
-    b_other = send(b_tile, across)
     own = ring_pick(own, ROUNDS[1], z, got)
     left = send(own, shift_x(1, (0, 1)))
     right = send(own, shift_x(-1, (0, 1)))
+    opposite = send(own, shift_x(2, (0, 1)))
     mine = ring_round(mine, ROUNDS[0], home_z, factor_z)
-
-    mine, left, right = tied(mine, left, right)
-    opp_a = send(left[: quarter_rows // 2], shift_x(1, (0, 1)))
-    opp_b = send(right[quarter_rows // 2 :], shift_x(-1, (0, 1)))
     mine = ring_round(mine, ROUNDS[1], home_z, factor_z)
 
-    mine, opp_a, opp_b, b_other = tied(mine, opp_a, opp_b, b_other)
+    mine, left, right, opposite, moved = tied(mine, left, right, opposite, moved)
+    b_tile = ring_pick(b_tile, FEWER[2], y, moved)
+    b_other = send(b_tile, across)
     turned = jnp.concatenate([mine] + [send(mine, shift_x(-by, (1,))) for by in (1, 2, 3)], axis=0)
     turned_other = send(turned, [(b, a) for a, b in across])
 
     pos = jnp.stack([row, col, x, core]).astype(jnp.int32)
-    out = update(pos, own, left, right, opp_a, opp_b, b_tile, b_other, turned, turned_other, cov)
+    out = update(pos, own, left, right, opposite, b_tile, b_other, turned, turned_other, cov)
     return out.reshape(covariance.shape)
 
 

time: 143 us -> 136 us (0.951)
  the two profiles are of different devices: /device:TPU:177 before, /device:TPU:505 now
where the time goes in v6:
time: 136 us; the launch traced here: 135 us
  starting transfers between devices  52.6 us (39%)
  waiting for transfers between devices  52.1 us (38%)
  Pallas kernels  12.9 us (9%)
  local copies, waits for them, and re-layouts  9.97 us (7%)
  other arithmetic  7.32 us (5%)
    ppermute x31, starting transfers between devices, send(): return lax.ppermute(value, AXES, pairs)  52.6 us
    ppermute x31, waiting for transfers between devices, send(): return lax.ppermute(value, AXES, pairs)  52.1 us
    pallas_call x1, Pallas kernels, update(): pl.pallas_call(update_kernel, out_shape=jax.ShapeDtypeStruct((8 * TB, SB)...  12.7 us
    select_n x9, other arithmetic, ring_pick(): value = jnp.where(one_of(pos, [b for _, b in pairs]), received, value)  6.05 us
    unnamed x15, local copies, waits for them, and re-layouts  4.98 us
    slice x1, local copies, waits for them, and re-layouts, on_device(): b_tile = cov[0:4 * TB]  3.06 us
  transfers between devices with their start and end apart: 31, of which 7 were waited for; matrix products, arithmetic and copies ran while one was open for 7% of the time, Pallas kernels for 0%

profile of v6, /device:TPU:505, one launch (start us, length us, event | category | flops | bytes accessed | tf_op | source)
XLA Modules:
  0.0 135.2 jit_solution(9641953363053528815)
XLA Ops:
  0.0 3.1 %slice.30 = f32[1,512,1,512]{3,2,1,0:T(1,128)} slice(f32[2,512,1,512]{3,2,1,0:T(1,128)} %param.1), slice={[0:1], [0:512], [0:1], [0:512]} | slice | bytes 2097152 | tf_op jit(solution)/shard_map/slice | solution.py:272
  3.1 1.6 %collective-permute-start.4 = (f32[2048,128]{1,0:T(8,128)}, f32[2048,128]{1,0:T(8,128)}, u32[]{:S(2)}, u32[]{:S(2)}) collective-permute-start(f32[2048,128]{1,0:T(8,128)} %bitcast.5), channel_id=1, source_target_pairs={{1,257},{2,258},{3,259},{4,260},{5,261},{6,262},{7,263},{8,264},{9... | collective-permute-start | bytes 3145736 | tf_op jit(solution)/shard_map/ppermute | solution.py:175
  4.7 0.7 collective-permute-start
  5.4 1.2 fusion
  6.6 1.4 %collective-permute-start.3 = (f32[1024,128]{1,0:T(8,128)}, f32[1024,128]{1,0:T(8,128)}, u32[]{:S(2)}, u32[]{:S(2)}) collective-permute-start(f32[1024,128]{1,0:T(8,128)} %get-tuple-element.49), channel_id=1, source_target_pairs={{0,1},{32,33},{64,65},{96,97},{128,129},{160,161},{192,193},{224,2... | collective-permute-start | bytes 1572872 | tf_op jit(solution)/shard_map/ppermute | solution.py:175
  8.1 1.5 %collective-permute-start.2 = (f32[1024,128]{1,0:T(8,128)}, f32[1024,128]{1,0:T(8,128)}, u32[]{:S(2)}, u32[]{:S(2)}) collective-permute-start(f32[1024,128]{1,0:T(8,128)} %get-tuple-element.50), channel_id=1, source_target_pairs={{0,2},{32,34},{64,66},{96,98},{128,130},{160,162},{192,194},{224,2... | collective-permute-start | bytes 1572872 | tf_op jit(solution)/shard_map/ppermute | solution.py:175
  9.5 1.5 %collective-permute-start.1 = (f32[1024,128]{1,0:T(8,128)}, f32[1024,128]{1,0:T(8,128)}, u32[]{:S(2)}, u32[]{:S(2)}) collective-permute-start(f32[1024,128]{1,0:T(8,128)} %get-tuple-element.51), channel_id=1, source_target_pairs={{0,3},{32,35},{64,67},{96,99},{128,131},{160,163},{192,195},{224,2... | collective-permute-start | bytes 1572872 | tf_op jit(solution)/shard_map/ppermute | solution.py:175
  11.0 0.0 collective-permute-done.4
  11.0 0.0 collective-permute-done.a_ref
  11.0 1.2 slice_select_fusion
  12.2 0.7 collective-permute-start.6
  12.9 0.7 collective-permute-start.5
  13.6 1.4 broadcast_select_fusion.1
  14.9 0.7 collective-permute-start.8
  15.7 0.7 collective-permute-start.7
  16.4 0.0 collective-permute-done.6
  16.4 0.2 factor.1
  16.7 0.0 collective-permute-done.7
  16.7 0.7 collective-permute-start.11
  17.4 0.7 collective-permute-start.10
  18.1 0.7 collective-permute-start.9
  18.8 0.1 select_select_fusion
  18.9 0.0 copy-start.5
  18.9 1.6 %collective-permute-start.18 = (f32[2048,128]{1,0:T(8,128)S(1)}, f32[2048,128]{1,0:T(8,128)}, u32[]{:S(2)}, u32[]{:S(2)}) collective-permute-start(f32[2048,128]{1,0:T(8,128)S(1)} %select_select_fusion), channel_id=1, source_target_pairs={{65,129},{66,130},{67,131},{68,132},{69,133},{70,134},{71,135},{72... | collective-permute-start | bytes 3145736 | tf_op jit(solution)/shard_map/ppermute | solution.py:175
  20.6 0.0 collective-permute-done.9
  20.6 0.7 collective-permute-start.13
  21.3 0.7 collective-permute-start.12
  22.0 0.9 select_select_fusion.2
  22.9 1.5 %collective-permute-start.17 = (f32[1024,128]{1,0:T(8,128)}, f32[1024,128]{1,0:T(8,128)}, u32[]{:S(2)}, u32[]{:S(2)}) collective-permute-start(f32[1024,128]{1,0:T(8,128)} %select_select_fusion.2), channel_id=1, source_target_pairs={{386,414},{387,415},{418,446},{419,447},{450,478},{451,479},{482,5... | collective-permute-start | bytes 1572872 | tf_op jit(solution)/shard_map/ppermute | solution.py:175
  24.3 1.5 %collective-permute-start.16 = (f32[1024,128]{1,0:T(8,128)}, f32[1024,128]{1,0:T(8,128)}, u32[]{:S(2)}, u32[]{:S(2)}) collective-permute-start(f32[1024,128]{1,0:T(8,128)} %select_select_fusion.2), channel_id=1, source_target_pairs={{2,6},{3,7},{34,38},{35,39},{66,70},{67,71},{98,102},{99,103},{128... | collective-permute-start | bytes 1572872 | tf_op jit(solution)/shard_map/ppermute | solution.py:175
  25.8 0.7 collective-permute-start.15
  26.5 1.3 collective-permute-start.14
  27.9 37.9 %collective-permute-done.14 = f32[384,128]{1,0:T(8,128)} collective-permute-done((f32[384,128]{1,0:T(8,128)S(1)}, f32[384,128]{1,0:T(8,128)}, u32[]{:S(2)}, u32[]{:S(2)}) %collective-permute-start.14) | collective-permute-done | bytes 196640 | tf_op jit(solution)/shard_map/ppermute | solution.py:175
  65.8 1.0 select_select_fusion.5
  66.8 0.0 collective-permute-done.16
  66.8 1.3 collective-permute-start.20
  68.1 1.3 collective-permute-start.19
  69.4 1.3 select_select_fusion.1.own_ref
  70.7 3.5 %collective-permute-start.25 = (f32[1024,128]{1,0:T(8,128)S(1)}, f32[1024,128]{1,0:T(8,128)S(1)}, u32[]{:S(2)}, u32[]{:S(2)}) collective-permute-start(f32[1024,128]{1,0:T(8,128)S(1)} %select_select_fusion.1.own_ref), channel_id=1, source_target_pairs={{0,2},{1,3},{2,0},{3,1},{4,6},{5,7},{6,4},{7,5},{8,10},{9,11},{10,... | collective-permute-start | bytes 1572872 | tf_op jit(solution)/shard_map/ppermute | solution.py:175
  74.2 4.6 %collective-permute-start.24 = (f32[1024,128]{1,0:T(8,128)S(1)}, f32[1024,128]{1,0:T(8,128)}, u32[]{:S(2)}, u32[]{:S(2)}) collective-permute-start(f32[1024,128]{1,0:T(8,128)S(1)} %select_select_fusion.1.own_ref), channel_id=1, source_target_pairs={{0,3},{1,0},{2,1},{3,2},{4,7},{5,4},{6,5},{7,6},{8,11},{9,8},{10,9... | collective-permute-start | bytes 1572872 | tf_op jit(solution)/shard_map/ppermute | solution.py:175
  78.8 1.9 %collective-permute-start.23 = (f32[1024,128]{1,0:T(8,128)S(1)}, f32[1024,128]{1,0:T(8,128)}, u32[]{:S(2)}, u32[]{:S(2)}) collective-permute-start(f32[1024,128]{1,0:T(8,128)S(1)} %select_select_fusion.1.own_ref), channel_id=1, source_target_pairs={{0,1},{1,2},{2,3},{3,0},{4,5},{5,6},{6,7},{7,4},{8,9},{9,10},{10,1... | collective-permute-start | bytes 1572872 | tf_op jit(solution)/shard_map/ppermute | solution.py:175
  80.8 1.3 collective-permute-start.22
  82.1 2.0 %collective-permute-start.21 = (f32[384,128]{1,0:T(8,128)S(1)}, f32[384,128]{1,0:T(8,128)}, u32[]{:S(2)}, u32[]{:S(2)}) collective-permute-start(f32[384,128]{1,0:T(8,128)S(1)} %select_select_fusion.4), channel_id=1, source_target_pairs={{60,56},{61,57},{62,58},{63,59},{124,120},{125,121},{126,122},{127... | collective-permute-start | bytes 589832 | tf_op jit(solution)/shard_map/ppermute | solution.py:175
  84.1 0.6 collective-permute-done.22
  84.7 1.3 collective-permute-done.21
  86.1 1.8 %collective-permute-done.25.opp_ref = f32[1024,128]{1,0:T(8,128)S(1)} collective-permute-done((f32[1024,128]{1,0:T(8,128)S(1)}, f32[1024,128]{1,0:T(8,128)S(1)}, u32[]{:S(2)}, u32[]{:S(2)}) %collective-permute-start.25) | collective-permute-done | bytes 524320 | tf_op jit(solution)/shard_map/ppermute | solution.py:175
  87.9 0.8 copy-done.3
  88.7 4.1 %collective-permute-done.24.right_ref = f32[1024,128]{1,0:T(8,128)} collective-permute-done((f32[1024,128]{1,0:T(8,128)S(1)}, f32[1024,128]{1,0:T(8,128)}, u32[]{:S(2)}, u32[]{:S(2)}) %collective-permute-start.24) | collective-permute-done | bytes 524320 | tf_op jit(solution)/shard_map/ppermute | solution.py:175
  92.7 5.0 %collective-permute-done.23.left_ref = f32[1024,128]{1,0:T(8,128)} collective-permute-done((f32[1024,128]{1,0:T(8,128)S(1)}, f32[1024,128]{1,0:T(8,128)}, u32[]{:S(2)}, u32[]{:S(2)}) %collective-permute-start.23) | collective-permute-done | bytes 524320 | tf_op jit(solution)/shard_map/ppermute | solution.py:175
  97.8 3.6 %collective-permute-start.29 = (f32[384,128]{1,0:T(8,128)S(1)}, f32[384,128]{1,0:T(8,128)S(1)}, u32[]{:S(2)}, u32[]{:S(2)}) collective-permute-start(f32[384,128]{1,0:T(8,128)S(1)} %select_select_fusion.3), channel_id=1, source_target_pairs={{32,33},{33,34},{34,35},{35,32},{36,37},{37,38},{38,39},{39,36},{4... | collective-permute-start | bytes 589832 | tf_op jit(solution)/shard_map/ppermute | solution.py:175
  101.3 3.5 %collective-permute-start.28 = (f32[384,128]{1,0:T(8,128)S(1)}, f32[384,128]{1,0:T(8,128)S(1)}, u32[]{:S(2)}, u32[]{:S(2)}) collective-permute-start(f32[384,128]{1,0:T(8,128)S(1)} %select_select_fusion.3), channel_id=1, source_target_pairs={{32,34},{33,35},{34,32},{35,33},{36,38},{37,39},{38,36},{39,37},{4... | collective-permute-start | bytes 589832 | tf_op jit(solution)/shard_map/ppermute | solution.py:175
  104.8 4.0 %collective-permute-start.27 = (f32[384,128]{1,0:T(8,128)S(1)}, f32[384,128]{1,0:T(8,128)S(1)}, u32[]{:S(2)}, u32[]{:S(2)}) collective-permute-start(f32[384,128]{1,0:T(8,128)S(1)} %select_select_fusion.3), channel_id=1, source_target_pairs={{32,35},{33,32},{34,33},{35,34},{36,39},{37,36},{38,37},{39,38},{4... | collective-permute-start | bytes 589832 | tf_op jit(solution)/shard_map/ppermute | solution.py:175
  108.8 1.4 broadcast_select_fusion.b_ref
  110.2 1.3 collective-permute-start.26
  111.5 0.7 constant_dynamic-update-slice_fusion.3
  112.2 0.7 constant_dynamic-update-slice_fusion.2
  112.9 0.7 constant_dynamic-update-slice_fusion.1
  113.6 0.7 constant_dynamic-update-slice_fusion.f_ref
  114.3 4.9 %collective-permute-start.30 = (f32[1536,128]{1,0:T(8,128)}, f32[1536,128]{1,0:T(8,128)}, u32[]{:S(2)}, u32[]{:S(2)}) collective-permute-start(f32[1536,128]{1,0:T(8,128)} %constant_dynamic-update-slice_fusion.f_ref), channel_id=1, source_target_pairs={{32,0},{33,1},{34,2},{35,3},{36,4},{37,5},{38,6},{39,7},{40,8},{41... | collective-permute-start | bytes 2359304 | tf_op jit(solution)/shard_map/ppermute | solution.py:175
  119.1 0.1 pad_add_fusion.pos_ref
  119.2 1.3 collective-permute-done.30.f_other_ref
  120.5 1.0 copy-done.2
  121.5 1.0 copy-done.4
  122.6 12.7 %update.1 = f32[4096,128]{1,0:T(8,128)} custom-call(s32[4]{0:T(128)S(1)} %pad_add_fusion.pos_ref, f32[1024,128]{1,0:T(8,128)S(1)} %copy-done.2, f32[1024,128]{1,0:T(8,128)} %collective-permute-done.23.left_ref, f32[1024,128]{1,0:T(8,128)} %collective-permute-done.24.right_ref, f32[1024,128]{1,0:T(8,128)S(1)} %copy-done.4, ...), custom_call_target="tpu_custom_call" | custom-call | flops 8000000000 | bytes 9000000 | tf_op jit(solution)/shard_map/update/pallas_call | solution.py:162
  (31 shorter events, 0.2 us)
Async XLA Ops:
  0.0 5.4 %copy-start = (f32[2,512,1,512]{3,2,1,0:T(1,128)S(1)}, f32[2,512,1,512]{3,2,1,0:T(1,128)}, u32[]{:S(2)}) copy-start(f32[2,512,1,512]{3,2,1,0:T(1,128)} %param.1) | copy-start | bytes 6291460
  3.1 7.9 %collective-permute-start.4 = (f32[2048,128]{1,0:T(8,128)}, f32[2048,128]{1,0:T(8,128)}, u32[]{:S(2)}, u32[]{:S(2)}) collective-permute-start(f32[2048,128]{1,0:T(8,128)} %bitcast.5), channel_id=1, source_target_pairs={{1,257},{2,258},{3,259},{4,260},{5,261},{6,262},{7,263},{8,264},{9... | collective-permute-start | bytes 3145736 | tf_op jit(solution)/shard_map/ppermute | solution.py:175
  4.7 6.3 %collective-permute-start = (f32[2048,128]{1,0:T(8,128)}, f32[2048,128]{1,0:T(8,128)S(1)}, u32[]{:S(2)}, u32[]{:S(2)}) collective-permute-start(f32[2048,128]{1,0:T(8,128)} %bitcast.5), channel_id=1, source_target_pairs={{0,60}} | collective-permute-start | bytes 3145736 | tf_op jit(solution)/shard_map/ppermute | solution.py:175
  6.6 4.4 %collective-permute-start.3 = (f32[1024,128]{1,0:T(8,128)}, f32[1024,128]{1,0:T(8,128)}, u32[]{:S(2)}, u32[]{:S(2)}) collective-permute-start(f32[1024,128]{1,0:T(8,128)} %get-tuple-element.49), channel_id=1, source_target_pairs={{0,1},{32,33},{64,65},{96,97},{128,129},{160,161},{192,193},{224,2... | collective-permute-start | bytes 1572872 | tf_op jit(solution)/shard_map/ppermute | solution.py:175
  8.1 2.9 %collective-permute-start.2 = (f32[1024,128]{1,0:T(8,128)}, f32[1024,128]{1,0:T(8,128)}, u32[]{:S(2)}, u32[]{:S(2)}) collective-permute-start(f32[1024,128]{1,0:T(8,128)} %get-tuple-element.50), channel_id=1, source_target_pairs={{0,2},{32,34},{64,66},{96,98},{128,130},{160,162},{192,194},{224,2... | collective-permute-start | bytes 1572872 | tf_op jit(solution)/shard_map/ppermute | solution.py:175
  9.5 1.5 %collective-permute-start.1 = (f32[1024,128]{1,0:T(8,128)}, f32[1024,128]{1,0:T(8,128)}, u32[]{:S(2)}, u32[]{:S(2)}) collective-permute-start(f32[1024,128]{1,0:T(8,128)} %get-tuple-element.51), channel_id=1, source_target_pairs={{0,3},{32,35},{64,67},{96,99},{128,131},{160,163},{192,195},{224,2... | collective-permute-start | bytes 1572872 | tf_op jit(solution)/shard_map/ppermute | solution.py:175
  12.2 4.2 %collective-permute-start.6 = (f32[1024,128]{1,0:T(8,128)S(1)}, f32[1024,128]{1,0:T(8,128)S(1)}, u32[]{:S(2)}, u32[]{:S(2)}) collective-permute-start(f32[1024,128]{1,0:T(8,128)S(1)} %slice_select_fusion), channel_id=1, source_target_pairs={{130,150},{131,151},{162,182},{163,183},{194,214},{195,215},{226,2... | collective-permute-start | bytes 1572872 | tf_op jit(solution)/shard_map/ppermute | solution.py:175
  12.9 3.5 %collective-permute-start.5 = (f32[1024,128]{1,0:T(8,128)S(1)}, f32[1024,128]{1,0:T(8,128)S(1)}, u32[]{:S(2)}, u32[]{:S(2)}) collective-permute-start(f32[1024,128]{1,0:T(8,128)S(1)} %slice_select_fusion), channel_id=1, source_target_pairs={{2,14},{3,15},{34,46},{35,47},{66,78},{67,79},{98,110},{99,111},{1... | collective-permute-start | bytes 1572872 | tf_op jit(solution)/shard_map/ppermute | solution.py:175
  14.9 1.7 %collective-permute-start.8 = (f32[2048,128]{1,0:T(8,128)S(1)}, f32[2048,128]{1,0:T(8,128)S(1)}, u32[]{:S(2)}, u32[]{:S(2)}) collective-permute-start(f32[2048,128]{1,0:T(8,128)S(1)} %broadcast_select_fusion.1), channel_id=1, source_target_pairs={{1,449},{2,450},{3,451},{4,452},{5,453},{6,454},{7,455},{8,456},{9... | collective-permute-start | bytes 3145736 | tf_op jit(solution)/shard_map/ppermute | solution.py:175
  15.7 1.0 collective-permute-start.7
  16.7 3.8 %collective-permute-start.11 = (f32[384,128]{1,0:T(8,128)S(1)}, f32[384,128]{1,0:T(8,128)S(1)}, u32[]{:S(2)}, u32[]{:S(2)}) collective-permute-start(f32[384,128]{1,0:T(8,128)S(1)} %get-tuple-element.52), channel_id=1, source_target_pairs={{60,63}} | collective-permute-start | bytes 589832 | tf_op jit(solution)/shard_map/ppermute | solution.py:175
  17.4 3.2 %collective-permute-start.10 = (f32[384,128]{1,0:T(8,128)S(1)}, f32[384,128]{1,0:T(8,128)S(1)}, u32[]{:S(2)}, u32[]{:S(2)}) collective-permute-start(f32[384,128]{1,0:T(8,128)S(1)} %get-tuple-element.53), channel_id=1, source_target_pairs={{60,62}} | collective-permute-start | bytes 589832 | tf_op jit(solution)/shard_map/ppermute | solution.py:175
  18.1 2.5 %collective-permute-start.9 = (f32[384,128]{1,0:T(8,128)S(1)}, f32[384,128]{1,0:T(8,128)S(1)}, u32[]{:S(2)}, u32[]{:S(2)}) collective-permute-start(f32[384,128]{1,0:T(8,128)S(1)} %get-tuple-element.54), channel_id=1, source_target_pairs={{60,61}} | collective-permute-start | bytes 589832 | tf_op jit(solution)/shard_map/ppermute | solution.py:175
  18.9 47.8 %copy-start.5 = (f32[2048,128]{1,0:T(8,128)}, f32[2048,128]{1,0:T(8,128)S(1)}, u32[]{:S(2)}) copy-start(f32[2048,128]{1,0:T(8,128)S(1)} %select_select_fusion) | copy-start | bytes 3145732
  18.9 47.9 %collective-permute-start.18 = (f32[2048,128]{1,0:T(8,128)S(1)}, f32[2048,128]{1,0:T(8,128)}, u32[]{:S(2)}, u32[]{:S(2)}) collective-permute-start(f32[2048,128]{1,0:T(8,128)S(1)} %select_select_fusion), channel_id=1, source_target_pairs={{65,129},{66,130},{67,131},{68,132},{69,133},{70,134},{71,135},{72... | collective-permute-start | bytes 3145736 | tf_op jit(solution)/shard_map/ppermute | solution.py:175
  20.6 5.2 %collective-permute-start.13 = (f32[384,128]{1,0:T(8,128)S(1)}, f32[384,128]{1,0:T(8,128)S(1)}, u32[]{:S(2)}, u32[]{:S(2)}) collective-permute-start(f32[384,128]{1,0:T(8,128)S(1)} %select_select_fusion.7), channel_id=1, source_target_pairs={{60,252},{61,253},{62,254},{63,255}} | collective-permute-start | bytes 589832 | tf_op jit(solution)/shard_map/ppermute | solution.py:175
  21.3 4.5 %collective-permute-start.12 = (f32[384,128]{1,0:T(8,128)S(1)}, f32[384,128]{1,0:T(8,128)S(1)}, u32[]{:S(2)}, u32[]{:S(2)}) collective-permute-start(f32[384,128]{1,0:T(8,128)S(1)} %select_select_fusion.7), channel_id=1, source_target_pairs={{60,380},{61,381},{62,382},{63,383}} | collective-permute-start | bytes 589832 | tf_op jit(solution)/shard_map/ppermute | solution.py:175
  22.9 43.9 %collective-permute-start.17 = (f32[1024,128]{1,0:T(8,128)}, f32[1024,128]{1,0:T(8,128)}, u32[]{:S(2)}, u32[]{:S(2)}) collective-permute-start(f32[1024,128]{1,0:T(8,128)} %select_select_fusion.2), channel_id=1, source_target_pairs={{386,414},{387,415},{418,446},{419,447},{450,478},{451,479},{482,5... | collective-permute-start | bytes 1572872 | tf_op jit(solution)/shard_map/ppermute | solution.py:175
  24.3 42.5 %collective-permute-start.16 = (f32[1024,128]{1,0:T(8,128)}, f32[1024,128]{1,0:T(8,128)}, u32[]{:S(2)}, u32[]{:S(2)}) collective-permute-start(f32[1024,128]{1,0:T(8,128)} %select_select_fusion.2), channel_id=1, source_target_pairs={{2,6},{3,7},{34,38},{35,39},{66,70},{67,71},{98,102},{99,103},{128... | collective-permute-start | bytes 1572872 | tf_op jit(solution)/shard_map/ppermute | solution.py:175
  25.8 2.0 %collective-permute-start.15 = (f32[384,128]{1,0:T(8,128)S(1)}, f32[384,128]{1,0:T(8,128)S(1)}, u32[]{:S(2)}, u32[]{:S(2)}) collective-permute-start(f32[384,128]{1,0:T(8,128)S(1)} %select_select_fusion.6), channel_id=1, source_target_pairs={{60,124},{61,125},{62,126},{63,127},{252,316},{253,317},{254,318},... | collective-permute-start | bytes 589832 | tf_op jit(solution)/shard_map/ppermute | solution.py:175
  26.5 39.3 %collective-permute-start.14 = (f32[384,128]{1,0:T(8,128)S(1)}, f32[384,128]{1,0:T(8,128)}, u32[]{:S(2)}, u32[]{:S(2)}) collective-permute-start(f32[384,128]{1,0:T(8,128)S(1)} %select_select_fusion.6), channel_id=1, source_target_pairs={{60,508},{61,509},{62,510},{63,511},{252,188},{253,189},{254,190},... | collective-permute-start | bytes 589832 | tf_op jit(solution)/shard_map/ppermute | solution.py:175
  66.8 14.0 %collective-permute-start.20 = (f32[384,128]{1,0:T(8,128)S(1)}, f32[384,128]{1,0:T(8,128)S(1)}, u32[]{:S(2)}, u32[]{:S(2)}) collective-permute-start(f32[384,128]{1,0:T(8,128)S(1)} %select_select_fusion.5), channel_id=1, source_target_pairs={{60,40},{61,41},{62,42},{63,43},{124,104},{125,105},{126,106},{127... | collective-permute-start | bytes 589832 | tf_op jit(solution)/shard_map/ppermute | solution.py:175
  68.1 12.7 %collective-permute-start.19 = (f32[384,128]{1,0:T(8,128)S(1)}, f32[384,128]{1,0:T(8,128)S(1)}, u32[]{:S(2)}, u32[]{:S(2)}) collective-permute-start(f32[384,128]{1,0:T(8,128)S(1)} %select_select_fusion.5), channel_id=1, source_target_pairs={{60,48},{61,49},{62,50},{63,51},{124,112},{125,113},{126,114},{127... | collective-permute-start | bytes 589832 | tf_op jit(solution)/shard_map/ppermute | solution.py:175
  70.7 34.1 %copy-start.1 = (f32[1024,128]{1,0:T(8,128)}, f32[1024,128]{1,0:T(8,128)S(1)}, u32[]{:S(2)}) copy-start(f32[1024,128]{1,0:T(8,128)S(1)} %select_select_fusion.1.own_ref) | copy-start | bytes 1572868
  70.7 17.2 %collective-permute-start.25 = (f32[1024,128]{1,0:T(8,128)S(1)}, f32[1024,128]{1,0:T(8,128)S(1)}, u32[]{:S(2)}, u32[]{:S(2)}) collective-permute-start(f32[1024,128]{1,0:T(8,128)S(1)} %select_select_fusion.1.own_ref), channel_id=1, source_target_pairs={{0,2},{1,3},{2,0},{3,1},{4,6},{5,7},{6,4},{7,5},{8,10},{9,11},{10,... | collective-permute-start | bytes 1572872 | tf_op jit(solution)/shard_map/ppermute | solution.py:175
  74.2 18.5 %collective-permute-start.24 = (f32[1024,128]{1,0:T(8,128)S(1)}, f32[1024,128]{1,0:T(8,128)}, u32[]{:S(2)}, u32[]{:S(2)}) collective-permute-start(f32[1024,128]{1,0:T(8,128)S(1)} %select_select_fusion.1.own_ref), channel_id=1, source_target_pairs={{0,3},{1,0},{2,1},{3,2},{4,7},{5,4},{6,5},{7,6},{8,11},{9,8},{10,9... | collective-permute-start | bytes 1572872 | tf_op jit(solution)/shard_map/ppermute | solution.py:175
  78.8 18.9 %collective-permute-start.23 = (f32[1024,128]{1,0:T(8,128)S(1)}, f32[1024,128]{1,0:T(8,128)}, u32[]{:S(2)}, u32[]{:S(2)}) collective-permute-start(f32[1024,128]{1,0:T(8,128)S(1)} %select_select_fusion.1.own_ref), channel_id=1, source_target_pairs={{0,1},{1,2},{2,3},{3,0},{4,5},{5,6},{6,7},{7,4},{8,9},{9,10},{10,1... | collective-permute-start | bytes 1572872 | tf_op jit(solution)/shard_map/ppermute | solution.py:175
  80.8 3.9 %collective-permute-start.22 = (f32[384,128]{1,0:T(8,128)S(1)}, f32[384,128]{1,0:T(8,128)S(1)}, u32[]{:S(2)}, u32[]{:S(2)}) collective-permute-start(f32[384,128]{1,0:T(8,128)S(1)} %select_select_fusion.4), channel_id=1, source_target_pairs={{60,32},{61,33},{62,34},{63,35},{124,96},{125,97},{126,98},{127,99... | collective-permute-start | bytes 589832 | tf_op jit(solution)/shard_map/ppermute | solution.py:175
  82.1 3.9 %collective-permute-start.21 = (f32[384,128]{1,0:T(8,128)S(1)}, f32[384,128]{1,0:T(8,128)}, u32[]{:S(2)}, u32[]{:S(2)}) collective-permute-start(f32[384,128]{1,0:T(8,128)S(1)} %select_select_fusion.4), channel_id=1, source_target_pairs={{60,56},{61,57},{62,58},{63,59},{124,120},{125,121},{126,122},{127... | collective-permute-start | bytes 589832 | tf_op jit(solution)/shard_map/ppermute | solution.py:175
  87.9 0.8 copy-start.3
  97.8 15.8 %collective-permute-start.29 = (f32[384,128]{1,0:T(8,128)S(1)}, f32[384,128]{1,0:T(8,128)S(1)}, u32[]{:S(2)}, u32[]{:S(2)}) collective-permute-start(f32[384,128]{1,0:T(8,128)S(1)} %select_select_fusion.3), channel_id=1, source_target_pairs={{32,33},{33,34},{34,35},{35,32},{36,37},{37,38},{38,39},{39,36},{4... | collective-permute-start | bytes 589832 | tf_op jit(solution)/shard_map/ppermute | solution.py:175
  101.3 11.5 %collective-permute-start.28 = (f32[384,128]{1,0:T(8,128)S(1)}, f32[384,128]{1,0:T(8,128)S(1)}, u32[]{:S(2)}, u32[]{:S(2)}) collective-permute-start(f32[384,128]{1,0:T(8,128)S(1)} %select_select_fusion.3), channel_id=1, source_target_pairs={{32,34},{33,35},{34,32},{35,33},{36,38},{37,39},{38,36},{39,37},{4... | collective-permute-start | bytes 589832 | tf_op jit(solution)/shard_map/ppermute | solution.py:175
  104.8 7.3 %collective-permute-start.27 = (f32[384,128]{1,0:T(8,128)S(1)}, f32[384,128]{1,0:T(8,128)S(1)}, u32[]{:S(2)}, u32[]{:S(2)}) collective-permute-start(f32[384,128]{1,0:T(8,128)S(1)} %select_select_fusion.3), channel_id=1, source_target_pairs={{32,35},{33,32},{34,33},{35,34},{36,39},{37,36},{38,37},{39,38},{4... | collective-permute-start | bytes 589832 | tf_op jit(solution)/shard_map/ppermute | solution.py:175
  110.2 10.3 %collective-permute-start.26 = (f32[2048,128]{1,0:T(8,128)S(1)}, f32[2048,128]{1,0:T(8,128)}, u32[]{:S(2)}, u32[]{:S(2)}) collective-permute-start(f32[2048,128]{1,0:T(8,128)S(1)} %broadcast_select_fusion.b_ref), channel_id=1, source_target_pairs={{0,32},{1,33},{2,34},{3,35},{4,36},{5,37},{6,38},{7,39},{8,40},{9,... | collective-permute-start | bytes 3145736 | tf_op jit(solution)/shard_map/ppermute | solution.py:175
  114.3 6.2 %collective-permute-start.30 = (f32[1536,128]{1,0:T(8,128)}, f32[1536,128]{1,0:T(8,128)}, u32[]{:S(2)}, u32[]{:S(2)}) collective-permute-start(f32[1536,128]{1,0:T(8,128)} %constant_dynamic-update-slice_fusion.f_ref), channel_id=1, source_target_pairs={{32,0},{33,1},{34,2},{35,3},{36,4},{37,5},{38,6},{39,7},{40,8},{41... | collective-permute-start | bytes 2359304 | tf_op jit(solution)/shard_map/ppermute | solution.py:175
  120.5 1.0 copy-start.2
  121.5 1.0 copy-start.4

commit v7 on v6

--- a/solution.py
+++ b/solution.py
@@ -301,9 +301,10 @@
     mine = ring_round(mine, ROUNDS[0], home_z, factor_z)
     mine = ring_round(mine, ROUNDS[1], home_z, factor_z)
 
-    mine, left, right, opposite, moved = tied(mine, left, right, opposite, moved)
+    mine, moved = tied(mine, moved)
     b_tile = ring_pick(b_tile, FEWER[2], y, moved)
     b_other = send(b_tile, across)
+    mine, left, right, opposite, b_other = tied(mine, left, right, opposite, b_other)
     turned = jnp.concatenate([mine] + [send(mine, shift_x(-by, (1,))) for by in (1, 2, 3)], axis=0)
     turned_other = send(turned, [(b, a) for a, b in across])
 

time: 136 us -> 156 us (1.15)
  the two profiles are of different devices: /device:TPU:505 before, /device:TPU:119 now
where the time goes in v7:
time: 156 us; the launch traced here: 155 us
  waiting for transfers between devices  74.2 us (48%)
  starting transfers between devices  45.7 us (29%)
  local copies, waits for them, and re-layouts  15.1 us (10%)
  Pallas kernels  12.6 us (8%)
  other arithmetic  7.15 us (5%)
    ppermute x31, waiting for transfers between devices, send(): return lax.ppermute(value, AXES, pairs)  74.2 us
    ppermute x31, starting transfers between devices, send(): return lax.ppermute(value, AXES, pairs)  45.7 us
    pallas_call x1, Pallas kernels, update(): pl.pallas_call(update_kernel, out_shape=jax.ShapeDtypeStruct((8 * TB, SB)...  12.3 us
    unnamed x25, local copies, waits for them, and re-layouts  10.1 us
    select_n x9, other arithmetic, ring_pick(): value = jnp.where(one_of(pos, [b for _, b in pairs]), received, value)  5.88 us
  transfers between devices with their start and end apart: 31, of which 6 were waited for; matrix products, arithmetic and copies ran while one was open for 5% of the time, Pallas kernels for 0%

profile of v7, /device:TPU:119, one launch (start us, length us, event | category | flops | bytes accessed | tf_op | source)
XLA Modules:
  0.0 155.2 jit_solution(10127861736898327820)
XLA Ops:
  0.0 3.1 %slice.30 = f32[1,512,1,512]{3,2,1,0:T(1,128)} slice(f32[2,512,1,512]{3,2,1,0:T(1,128)} %param.1), slice={[0:1], [0:512], [0:1], [0:512]} | slice | bytes 2097152 | tf_op jit(solution)/shard_map/slice | solution.py:272
  3.1 1.6 %collective-permute-start.4 = (f32[2048,128]{1,0:T(8,128)}, f32[2048,128]{1,0:T(8,128)}, u32[]{:S(2)}, u32[]{:S(2)}) collective-permute-start(f32[2048,128]{1,0:T(8,128)} %bitcast.5), channel_id=1, source_target_pairs={{1,257},{2,258},{3,259},{4,260},{5,261},{6,262},{7,263},{8,264},{9... | collective-permute-start | bytes 3145736 | tf_op jit(solution)/shard_map/ppermute | solution.py:175
  4.7 0.7 collective-permute-start
  5.4 1.2 fusion
  6.6 1.5 collective-permute-start.3
  8.1 1.5 collective-permute-start.2
  9.6 1.5 collective-permute-start.1
  11.0 1.2 slice_select_fusion
  12.2 0.7 collective-permute-start.6
  12.9 0.7 collective-permute-start.5
  13.6 1.4 broadcast_select_fusion.1
  15.0 0.7 collective-permute-start.8
  15.7 0.7 collective-permute-start.7
  16.5 0.2 factor.1
  16.8 0.7 collective-permute-start.11
  17.4 0.7 collective-permute-start.10
  18.1 0.7 collective-permute-start.9
  18.8 0.1 select_select_fusion
  19.0 0.0 copy-start.9
  19.0 1.7 %collective-permute-start.18 = (f32[2048,128]{1,0:T(8,128)S(1)}, f32[2048,128]{1,0:T(8,128)}, u32[]{:S(2)}, u32[]{:S(2)}) collective-permute-start(f32[2048,128]{1,0:T(8,128)S(1)} %select_select_fusion), channel_id=1, source_target_pairs={{65,129},{66,130},{67,131},{68,132},{69,133},{70,134},{71,135},{72... | collective-permute-start | bytes 3145736 | tf_op jit(solution)/shard_map/ppermute | solution.py:175
  20.7 0.7 collective-permute-start.13
  21.4 0.7 collective-permute-start.12
  22.1 0.9 select_select_fusion.2
  22.9 1.5 collective-permute-start.17
  24.4 1.3 collective-permute-start.16
  25.7 0.7 collective-permute-start.15
  26.4 1.3 collective-permute-start.14
  27.7 0.7 copy-done.10
  28.4 1.0 select_select_fusion.5
  29.4 30.6 %collective-permute-done.16 = f32[1024,128]{1,0:T(8,128)} collective-permute-done((f32[1024,128]{1,0:T(8,128)}, f32[1024,128]{1,0:T(8,128)}, u32[]{:S(2)}, u32[]{:S(2)}) %collective-permute-start.16) | collective-permute-done | bytes 524320 | tf_op jit(solution)/shard_map/ppermute | solution.py:175
  60.0 0.7 collective-permute-start.20
  60.7 0.7 collective-permute-start.19
  61.4 0.7 collective-permute-start.22
  62.1 1.3 collective-permute-start.21
  63.4 22.0 %collective-permute-done.21 = f32[384,128]{1,0:T(8,128)S(1)} collective-permute-done((f32[384,128]{1,0:T(8,128)S(1)}, f32[384,128]{1,0:T(8,128)S(1)}, u32[]{:S(2)}, u32[]{:S(2)}) %collective-permute-start.21) | collective-permute-done | bytes 196640 | tf_op jit(solution)/shard_map/ppermute | solution.py:175
  85.5 1.3 broadcast_select_fusion.b_ref
  86.8 1.3 collective-permute-start.26
  88.1 1.1 select_select_fusion.1.own_ref
  89.3 3.9 %collective-permute-start.25 = (f32[1024,128]{1,0:T(8,128)S(1)}, f32[1024,128]{1,0:T(8,128)S(1)}, u32[]{:S(2)}, u32[]{:S(2)}) collective-permute-start(f32[1024,128]{1,0:T(8,128)S(1)} %select_select_fusion.1.own_ref), channel_id=1, source_target_pairs={{0,2},{1,3},{2,0},{3,1},{4,6},{5,7},{6,4},{7,5},{8,10},{9,11},{10,... | collective-permute-start | bytes 1572872 | tf_op jit(solution)/shard_map/ppermute | solution.py:175
  93.2 1.9 %collective-permute-start.24 = (f32[1024,128]{1,0:T(8,128)S(1)}, f32[1024,128]{1,0:T(8,128)S(1)}, u32[]{:S(2)}, u32[]{:S(2)}) collective-permute-start(f32[1024,128]{1,0:T(8,128)S(1)} %select_select_fusion.1.own_ref), channel_id=1, source_target_pairs={{0,3},{1,0},{2,1},{3,2},{4,7},{5,4},{6,5},{7,6},{8,11},{9,8},{10,9... | collective-permute-start | bytes 1572872 | tf_op jit(solution)/shard_map/ppermute | solution.py:175
  95.1 4.6 %collective-permute-start.23 = (f32[1024,128]{1,0:T(8,128)S(1)}, f32[1024,128]{1,0:T(8,128)S(1)}, u32[]{:S(2)}, u32[]{:S(2)}) collective-permute-start(f32[1024,128]{1,0:T(8,128)S(1)} %select_select_fusion.1.own_ref), channel_id=1, source_target_pairs={{0,1},{1,2},{2,3},{3,0},{4,5},{5,6},{6,7},{7,4},{8,9},{9,10},{10,1... | collective-permute-start | bytes 1572872 | tf_op jit(solution)/shard_map/ppermute | solution.py:175
  99.7 0.0 copy-start.1
  99.7 0.8 copy-done.1
  100.5 3.5 %collective-permute-done.25.opp_ref = f32[1024,128]{1,0:T(8,128)S(1)} collective-permute-done((f32[1024,128]{1,0:T(8,128)S(1)}, f32[1024,128]{1,0:T(8,128)S(1)}, u32[]{:S(2)}, u32[]{:S(2)}) %collective-permute-start.25) | collective-permute-done | bytes 524320 | tf_op jit(solution)/shard_map/ppermute | solution.py:175
  104.0 0.8 copy-done.3
  104.8 12.9 %collective-permute-done.24.right_ref = f32[1024,128]{1,0:T(8,128)S(1)} collective-permute-done((f32[1024,128]{1,0:T(8,128)S(1)}, f32[1024,128]{1,0:T(8,128)S(1)}, u32[]{:S(2)}, u32[]{:S(2)}) %collective-permute-start.24) | collective-permute-done | bytes 524320 | tf_op jit(solution)/shard_map/ppermute | solution.py:175
  117.7 0.8 copy-done.5
  118.5 0.8 copy-done.7
  119.4 1.9 %collective-permute-start.27 = (f32[384,128]{1,0:T(8,128)S(1)}, f32[384,128]{1,0:T(8,128)S(1)}, u32[]{:S(2)}, u32[]{:S(2)}) collective-permute-start(f32[384,128]{1,0:T(8,128)S(1)} %select_select_fusion.3), channel_id=1, source_target_pairs={{32,35},{33,32},{34,33},{35,34},{36,39},{37,36},{38,37},{39,38},{4... | collective-permute-start | bytes 589832 | tf_op jit(solution)/shard_map/ppermute | solution.py:175
  121.3 4.6 %collective-permute-start.29 = (f32[384,128]{1,0:T(8,128)S(1)}, f32[384,128]{1,0:T(8,128)S(1)}, u32[]{:S(2)}, u32[]{:S(2)}) collective-permute-start(f32[384,128]{1,0:T(8,128)S(1)} %select_select_fusion.3), channel_id=1, source_target_pairs={{32,33},{33,34},{34,35},{35,32},{36,37},{37,38},{38,39},{39,36},{4... | collective-permute-start | bytes 589832 | tf_op jit(solution)/shard_map/ppermute | solution.py:175
  125.9 2.7 %collective-permute-start.28 = (f32[384,128]{1,0:T(8,128)S(1)}, f32[384,128]{1,0:T(8,128)S(1)}, u32[]{:S(2)}, u32[]{:S(2)}) collective-permute-start(f32[384,128]{1,0:T(8,128)S(1)} %select_select_fusion.3), channel_id=1, source_target_pairs={{32,34},{33,35},{34,32},{35,33},{36,38},{37,39},{38,36},{39,37},{4... | collective-permute-start | bytes 589832 | tf_op jit(solution)/shard_map/ppermute | solution.py:175
  128.6 0.7 constant_dynamic-update-slice_fusion.3
  129.3 0.7 constant_dynamic-update-slice_fusion.2
  130.0 3.8 %collective-permute-done.28 = f32[384,128]{1,0:T(8,128)S(1)} collective-permute-done((f32[384,128]{1,0:T(8,128)S(1)}, f32[384,128]{1,0:T(8,128)S(1)}, u32[]{:S(2)}, u32[]{:S(2)}) %collective-permute-start.28) | collective-permute-done | bytes 196640 | tf_op jit(solution)/shard_map/ppermute | solution.py:175
  133.8 0.7 constant_dynamic-update-slice_fusion.1
  134.5 0.7 constant_dynamic-update-slice_fusion.f_ref
  135.2 2.2 %collective-permute-start.30 = (f32[1536,128]{1,0:T(8,128)}, f32[1536,128]{1,0:T(8,128)}, u32[]{:S(2)}, u32[]{:S(2)}) collective-permute-start(f32[1536,128]{1,0:T(8,128)} %constant_dynamic-update-slice_fusion.f_ref), channel_id=1, source_target_pairs={{32,0},{33,1},{34,2},{35,3},{36,4},{37,5},{38,6},{39,7},{40,8},{41... | collective-permute-start | bytes 2359304 | tf_op jit(solution)/shard_map/ppermute | solution.py:175
  137.3 0.1 pad_add_fusion.pos_ref
  137.4 1.3 collective-permute-done.30.f_other_ref
  138.7 1.0 copy-done.2
  139.8 1.0 copy-done.4
  140.8 1.0 copy-done.6
  141.8 1.0 copy-done.8
  142.9 12.3 %update.1 = f32[4096,128]{1,0:T(8,128)} custom-call(s32[4]{0:T(128)S(1)} %pad_add_fusion.pos_ref, f32[1024,128]{1,0:T(8,128)S(1)} %copy-done.2, f32[1024,128]{1,0:T(8,128)S(1)} %copy-done.8, f32[1024,128]{1,0:T(8,128)S(1)} %copy-done.6, f32[1024,128]{1,0:T(8,128)S(1)} %copy-done.4, f32[2048,128]{1,0:T(8,128)S(1)} %broadcast_select_fusion.b_ref, ...), custom_call_target="tpu_custom_call" | custom-call | flops 8000000000 | bytes 9000000 | tf_op jit(solution)/shard_map/update/pallas_call | solution.py:162
  (41 shorter events, 0.3 us)
Async XLA Ops:
  0.0 5.4 %copy-start = (f32[2,512,1,512]{3,2,1,0:T(1,128)S(1)}, f32[2,512,1,512]{3,2,1,0:T(1,128)}, u32[]{:S(2)}) copy-start(f32[2,512,1,512]{3,2,1,0:T(1,128)} %param.1) | copy-start | bytes 6291460
  3.1 8.0 %collective-permute-start.4 = (f32[2048,128]{1,0:T(8,128)}, f32[2048,128]{1,0:T(8,128)}, u32[]{:S(2)}, u32[]{:S(2)}) collective-permute-start(f32[2048,128]{1,0:T(8,128)} %bitcast.5), channel_id=1, source_target_pairs={{1,257},{2,258},{3,259},{4,260},{5,261},{6,262},{7,263},{8,264},{9... | collective-permute-start | bytes 3145736 | tf_op jit(solution)/shard_map/ppermute | solution.py:175
  4.7 6.3 %collective-permute-start = (f32[2048,128]{1,0:T(8,128)}, f32[2048,128]{1,0:T(8,128)S(1)}, u32[]{:S(2)}, u32[]{:S(2)}) collective-permute-start(f32[2048,128]{1,0:T(8,128)} %bitcast.5), channel_id=1, source_target_pairs={{0,60}} | collective-permute-start | bytes 3145736 | tf_op jit(solution)/shard_map/ppermute | solution.py:175
  6.6 4.4 %collective-permute-start.3 = (f32[1024,128]{1,0:T(8,128)}, f32[1024,128]{1,0:T(8,128)}, u32[]{:S(2)}, u32[]{:S(2)}) collective-permute-start(f32[1024,128]{1,0:T(8,128)} %get-tuple-element.53), channel_id=1, source_target_pairs={{0,1},{32,33},{64,65},{96,97},{128,129},{160,161},{192,193},{224,2... | collective-permute-start | bytes 1572872 | tf_op jit(solution)/shard_map/ppermute | solution.py:175
  8.1 2.9 %collective-permute-start.2 = (f32[1024,128]{1,0:T(8,128)}, f32[1024,128]{1,0:T(8,128)}, u32[]{:S(2)}, u32[]{:S(2)}) collective-permute-start(f32[1024,128]{1,0:T(8,128)} %get-tuple-element.54), channel_id=1, source_target_pairs={{0,2},{32,34},{64,66},{96,98},{128,130},{160,162},{192,194},{224,2... | collective-permute-start | bytes 1572872 | tf_op jit(solution)/shard_map/ppermute | solution.py:175
  9.6 1.5 collective-permute-start.1
  12.2 4.2 %collective-permute-start.6 = (f32[1024,128]{1,0:T(8,128)S(1)}, f32[1024,128]{1,0:T(8,128)S(1)}, u32[]{:S(2)}, u32[]{:S(2)}) collective-permute-start(f32[1024,128]{1,0:T(8,128)S(1)} %slice_select_fusion), channel_id=1, source_target_pairs={{130,150},{131,151},{162,182},{163,183},{194,214},{195,215},{226,2... | collective-permute-start | bytes 1572872 | tf_op jit(solution)/shard_map/ppermute | solution.py:175
  12.9 3.5 %collective-permute-start.5 = (f32[1024,128]{1,0:T(8,128)S(1)}, f32[1024,128]{1,0:T(8,128)S(1)}, u32[]{:S(2)}, u32[]{:S(2)}) collective-permute-start(f32[1024,128]{1,0:T(8,128)S(1)} %slice_select_fusion), channel_id=1, source_target_pairs={{2,14},{3,15},{34,46},{35,47},{66,78},{67,79},{98,110},{99,111},{1... | collective-permute-start | bytes 1572872 | tf_op jit(solution)/shard_map/ppermute | solution.py:175
  15.0 1.7 %collective-permute-start.8 = (f32[2048,128]{1,0:T(8,128)S(1)}, f32[2048,128]{1,0:T(8,128)S(1)}, u32[]{:S(2)}, u32[]{:S(2)}) collective-permute-start(f32[2048,128]{1,0:T(8,128)S(1)} %broadcast_select_fusion.1), channel_id=1, source_target_pairs={{1,449},{2,450},{3,451},{4,452},{5,453},{6,454},{7,455},{8,456},{9... | collective-permute-start | bytes 3145736 | tf_op jit(solution)/shard_map/ppermute | solution.py:175
  15.7 1.0 collective-permute-start.7
  16.8 3.9 %collective-permute-start.11 = (f32[384,128]{1,0:T(8,128)S(1)}, f32[384,128]{1,0:T(8,128)S(1)}, u32[]{:S(2)}, u32[]{:S(2)}) collective-permute-start(f32[384,128]{1,0:T(8,128)S(1)} %get-tuple-element.56), channel_id=1, source_target_pairs={{60,63}} | collective-permute-start | bytes 589832 | tf_op jit(solution)/shard_map/ppermute | solution.py:175
  17.4 3.2 %collective-permute-start.10 = (f32[384,128]{1,0:T(8,128)S(1)}, f32[384,128]{1,0:T(8,128)S(1)}, u32[]{:S(2)}, u32[]{:S(2)}) collective-permute-start(f32[384,128]{1,0:T(8,128)S(1)} %get-tuple-element.57), channel_id=1, source_target_pairs={{60,62}} | collective-permute-start | bytes 589832 | tf_op jit(solution)/shard_map/ppermute | solution.py:175
  18.1 2.5 %collective-permute-start.9 = (f32[384,128]{1,0:T(8,128)S(1)}, f32[384,128]{1,0:T(8,128)S(1)}, u32[]{:S(2)}, u32[]{:S(2)}) collective-permute-start(f32[384,128]{1,0:T(8,128)S(1)} %get-tuple-element.58), channel_id=1, source_target_pairs={{60,61}} | collective-permute-start | bytes 589832 | tf_op jit(solution)/shard_map/ppermute | solution.py:175
  19.0 10.4 %copy-start.9 = (f32[2048,128]{1,0:T(8,128)}, f32[2048,128]{1,0:T(8,128)S(1)}, u32[]{:S(2)}) copy-start(f32[2048,128]{1,0:T(8,128)S(1)} %select_select_fusion) | copy-start | bytes 3145732
  19.0 41.0 %collective-permute-start.18 = (f32[2048,128]{1,0:T(8,128)S(1)}, f32[2048,128]{1,0:T(8,128)}, u32[]{:S(2)}, u32[]{:S(2)}) collective-permute-start(f32[2048,128]{1,0:T(8,128)S(1)} %select_select_fusion), channel_id=1, source_target_pairs={{65,129},{66,130},{67,131},{68,132},{69,133},{70,134},{71,135},{72... | collective-permute-start | bytes 3145736 | tf_op jit(solution)/shard_map/ppermute | solution.py:175
  20.7 5.0 %collective-permute-start.13 = (f32[384,128]{1,0:T(8,128)S(1)}, f32[384,128]{1,0:T(8,128)S(1)}, u32[]{:S(2)}, u32[]{:S(2)}) collective-permute-start(f32[384,128]{1,0:T(8,128)S(1)} %select_select_fusion.7), channel_id=1, source_target_pairs={{60,252},{61,253},{62,254},{63,255}} | collective-permute-start | bytes 589832 | tf_op jit(solution)/shard_map/ppermute | solution.py:175
  21.4 4.3 %collective-permute-start.12 = (f32[384,128]{1,0:T(8,128)S(1)}, f32[384,128]{1,0:T(8,128)S(1)}, u32[]{:S(2)}, u32[]{:S(2)}) collective-permute-start(f32[384,128]{1,0:T(8,128)S(1)} %select_select_fusion.7), channel_id=1, source_target_pairs={{60,380},{61,381},{62,382},{63,383}} | collective-permute-start | bytes 589832 | tf_op jit(solution)/shard_map/ppermute | solution.py:175
  22.9 6.5 %collective-permute-start.17 = (f32[1024,128]{1,0:T(8,128)}, f32[1024,128]{1,0:T(8,128)}, u32[]{:S(2)}, u32[]{:S(2)}) collective-permute-start(f32[1024,128]{1,0:T(8,128)} %select_select_fusion.2), channel_id=1, source_target_pairs={{386,414},{387,415},{418,446},{419,447},{450,478},{451,479},{482,5... | collective-permute-start | bytes 1572872 | tf_op jit(solution)/shard_map/ppermute | solution.py:175
  24.4 35.6 %collective-permute-start.16 = (f32[1024,128]{1,0:T(8,128)}, f32[1024,128]{1,0:T(8,128)}, u32[]{:S(2)}, u32[]{:S(2)}) collective-permute-start(f32[1024,128]{1,0:T(8,128)} %select_select_fusion.2), channel_id=1, source_target_pairs={{2,6},{3,7},{34,38},{35,39},{66,70},{67,71},{98,102},{99,103},{128... | collective-permute-start | bytes 1572872 | tf_op jit(solution)/shard_map/ppermute | solution.py:175
  25.7 2.0 %collective-permute-start.15 = (f32[384,128]{1,0:T(8,128)S(1)}, f32[384,128]{1,0:T(8,128)S(1)}, u32[]{:S(2)}, u32[]{:S(2)}) collective-permute-start(f32[384,128]{1,0:T(8,128)S(1)} %select_select_fusion.6), channel_id=1, source_target_pairs={{60,124},{61,125},{62,126},{63,127},{252,316},{253,317},{254,318},... | collective-permute-start | bytes 589832 | tf_op jit(solution)/shard_map/ppermute | solution.py:175
  26.4 2.0 %collective-permute-start.14 = (f32[384,128]{1,0:T(8,128)S(1)}, f32[384,128]{1,0:T(8,128)}, u32[]{:S(2)}, u32[]{:S(2)}) collective-permute-start(f32[384,128]{1,0:T(8,128)S(1)} %select_select_fusion.6), channel_id=1, source_target_pairs={{60,508},{61,509},{62,510},{63,511},{252,188},{253,189},{254,190},... | collective-permute-start | bytes 589832 | tf_op jit(solution)/shard_map/ppermute | solution.py:175
  27.7 0.7 copy-start.10
  60.0 1.4 collective-permute-start.20
  60.7 0.7 collective-permute-start.19
  61.4 2.0 %collective-permute-start.22 = (f32[384,128]{1,0:T(8,128)S(1)}, f32[384,128]{1,0:T(8,128)S(1)}, u32[]{:S(2)}, u32[]{:S(2)}) collective-permute-start(f32[384,128]{1,0:T(8,128)S(1)} %select_select_fusion.4), channel_id=1, source_target_pairs={{60,32},{61,33},{62,34},{63,35},{124,96},{125,97},{126,98},{127,99... | collective-permute-start | bytes 589832 | tf_op jit(solution)/shard_map/ppermute | solution.py:175
  62.1 23.3 %collective-permute-start.21 = (f32[384,128]{1,0:T(8,128)S(1)}, f32[384,128]{1,0:T(8,128)S(1)}, u32[]{:S(2)}, u32[]{:S(2)}) collective-permute-start(f32[384,128]{1,0:T(8,128)S(1)} %select_select_fusion.4), channel_id=1, source_target_pairs={{60,56},{61,57},{62,58},{63,59},{124,120},{125,121},{126,122},{127... | collective-permute-start | bytes 589832 | tf_op jit(solution)/shard_map/ppermute | solution.py:175
  86.8 32.5 %collective-permute-start.26 = (f32[2048,128]{1,0:T(8,128)S(1)}, f32[2048,128]{1,0:T(8,128)}, u32[]{:S(2)}, u32[]{:S(2)}) collective-permute-start(f32[2048,128]{1,0:T(8,128)S(1)} %broadcast_select_fusion.b_ref), channel_id=1, source_target_pairs={{0,32},{1,33},{2,34},{3,35},{4,36},{5,37},{6,38},{7,39},{8,40},{9,... | collective-permute-start | bytes 3145736 | tf_op jit(solution)/shard_map/ppermute | solution.py:175
  89.3 14.8 %collective-permute-start.25 = (f32[1024,128]{1,0:T(8,128)S(1)}, f32[1024,128]{1,0:T(8,128)S(1)}, u32[]{:S(2)}, u32[]{:S(2)}) collective-permute-start(f32[1024,128]{1,0:T(8,128)S(1)} %select_select_fusion.1.own_ref), channel_id=1, source_target_pairs={{0,2},{1,3},{2,0},{3,1},{4,6},{5,7},{6,4},{7,5},{8,10},{9,11},{10,... | collective-permute-start | bytes 1572872 | tf_op jit(solution)/shard_map/ppermute | solution.py:175
  93.2 24.5 %collective-permute-start.24 = (f32[1024,128]{1,0:T(8,128)S(1)}, f32[1024,128]{1,0:T(8,128)S(1)}, u32[]{:S(2)}, u32[]{:S(2)}) collective-permute-start(f32[1024,128]{1,0:T(8,128)S(1)} %select_select_fusion.1.own_ref), channel_id=1, source_target_pairs={{0,3},{1,0},{2,1},{3,2},{4,7},{5,4},{6,5},{7,6},{8,11},{9,8},{10,9... | collective-permute-start | bytes 1572872 | tf_op jit(solution)/shard_map/ppermute | solution.py:175
  95.1 23.4 %collective-permute-start.23 = (f32[1024,128]{1,0:T(8,128)S(1)}, f32[1024,128]{1,0:T(8,128)S(1)}, u32[]{:S(2)}, u32[]{:S(2)}) collective-permute-start(f32[1024,128]{1,0:T(8,128)S(1)} %select_select_fusion.1.own_ref), channel_id=1, source_target_pairs={{0,1},{1,2},{2,3},{3,0},{4,5},{5,6},{6,7},{7,4},{8,9},{9,10},{10,1... | collective-permute-start | bytes 1572872 | tf_op jit(solution)/shard_map/ppermute | solution.py:175
  99.7 0.8 copy-start.1
  104.0 0.8 copy-start.3
  117.7 0.8 copy-start.5
  118.5 0.8 copy-start.7
  119.4 9.9 %collective-permute-start.27 = (f32[384,128]{1,0:T(8,128)S(1)}, f32[384,128]{1,0:T(8,128)S(1)}, u32[]{:S(2)}, u32[]{:S(2)}) collective-permute-start(f32[384,128]{1,0:T(8,128)S(1)} %select_select_fusion.3), channel_id=1, source_target_pairs={{32,35},{33,32},{34,33},{35,34},{36,39},{37,36},{38,37},{39,38},{4... | collective-permute-start | bytes 589832 | tf_op jit(solution)/shard_map/ppermute | solution.py:175
  121.3 13.2 %collective-permute-start.29 = (f32[384,128]{1,0:T(8,128)S(1)}, f32[384,128]{1,0:T(8,128)S(1)}, u32[]{:S(2)}, u32[]{:S(2)}) collective-permute-start(f32[384,128]{1,0:T(8,128)S(1)} %select_select_fusion.3), channel_id=1, source_target_pairs={{32,33},{33,34},{34,35},{35,32},{36,37},{37,38},{38,39},{39,36},{4... | collective-permute-start | bytes 589832 | tf_op jit(solution)/shard_map/ppermute | solution.py:175
  125.9 7.9 %collective-permute-start.28 = (f32[384,128]{1,0:T(8,128)S(1)}, f32[384,128]{1,0:T(8,128)S(1)}, u32[]{:S(2)}, u32[]{:S(2)}) collective-permute-start(f32[384,128]{1,0:T(8,128)S(1)} %select_select_fusion.3), channel_id=1, source_target_pairs={{32,34},{33,35},{34,32},{35,33},{36,38},{37,39},{38,36},{39,37},{4... | collective-permute-start | bytes 589832 | tf_op jit(solution)/shard_map/ppermute | solution.py:175
  135.2 3.5 %collective-permute-start.30 = (f32[1536,128]{1,0:T(8,128)}, f32[1536,128]{1,0:T(8,128)}, u32[]{:S(2)}, u32[]{:S(2)}) collective-permute-start(f32[1536,128]{1,0:T(8,128)} %constant_dynamic-update-slice_fusion.f_ref), channel_id=1, source_target_pairs={{32,0},{33,1},{34,2},{35,3},{36,4},{37,5},{38,6},{39,7},{40,8},{41... | collective-permute-start | bytes 2359304 | tf_op jit(solution)/shard_map/ppermute | solution.py:175
  138.7 1.0 copy-start.2
  139.8 1.0 copy-start.4
  140.8 1.0 copy-start.6
  141.8 1.0 copy-start.8
